TPU v7x, 32 devices: a whole 2x2x4 slice. The times are simulated.
32 devices in a mesh: dp: 8 (over z, x), tensor: 4 (over y, core).
Axes of the slice: x: 2, y: 2, z: 4, core: 2. Of those that a mesh axis runs over, the one named last changes fastest.
Arguments:
- piece_table: bfloat16 [32768, 512], P('dp', 'tensor'), may hold values from -6 to 6
- piece_ids: int32 [2, 512, 8], P(None, 'dp'), may hold values from 0 to 32767
- piece_counts: int32 [2, 512], P(None, 'dp'), may hold values from 1 to 7, as said below
- text_ids: int32 [2, 8192], P(None, 'dp'), may hold values from 0 to 63
- cotangent: float32 [2, 8192, 2048], P(None, ('dp', 'tensor')), may hold values from -6 to 6
- rms_gain_one: bfloat16 [2048], replicated, may hold values from 0.25 to 1.75
- w_query: bfloat16 [2048, 2048], P(None, 'tensor'), may hold values from -0.125 to 0.125
- w_key: bfloat16 [2048, 256], P(None, 'tensor'), may hold values from -0.125 to 0.125
- w_value: bfloat16 [2048, 256], P(None, 'tensor'), may hold values from -0.125 to 0.125
- w_output: bfloat16 [2048, 2048], P('tensor'), may hold values from -0.5 to 0.5
- rms_gain_two: bfloat16 [2048], replicated, may hold values from 0.25 to 1.75
- w_gate: bfloat16 [2048, 5632], P(None, 'tensor'), may hold values from -0.125 to 0.125
- w_up: bfloat16 [2048, 5632], P(None, 'tensor'), may hold values from -0.125 to 0.125
- w_down: bfloat16 [5632, 2048], P('tensor'), may hold values from -0.15625 to 0.15625
- ln_gain_one: bfloat16 [2, 512], P(None, ('dp', 'tensor')), may hold values from 0.25 to 1.75
- ln_bias_one: bfloat16 [2, 512], P(None, ('dp', 'tensor')), may hold values from -2.390625 to 2.390625
- w_qkv: bfloat16 [2, 512, 1536], P(None, ('dp', 'tensor')), may hold values from -0.25 to 0.25
- bias_query: bfloat16 [2, 512], P(None, ('dp', 'tensor')), may hold values from -3 to 3
- bias_value: bfloat16 [2, 512], P(None, ('dp', 'tensor')), may hold values from -3 to 3
- w_attn_out: bfloat16 [2, 512, 512], P(None, ('dp', 'tensor')), may hold values from -0.375 to 0.375
- bias_attn_out: bfloat16 [2, 512], P(None, ('dp', 'tensor')), may hold values from -3 to 3
- ln_gain_two: bfloat16 [2, 512], P(None, ('dp', 'tensor')), may hold values from 0.25 to 1.75
- ln_bias_two: bfloat16 [2, 512], P(None, ('dp', 'tensor')), may hold values from -2.390625 to 2.390625
- w_inner: bfloat16 [2, 512, 2048], P(None, ('dp', 'tensor')), may hold values from -0.25 to 0.25
- bias_inner: bfloat16 [2, 2048], P(None, ('dp', 'tensor')), may hold values from -3 to 3
- w_outer: bfloat16 [2, 2048, 512], P(None, ('dp', 'tensor')), may hold values from -0.1875 to 0.1875
- bias_outer: bfloat16 [2, 512], P(None, ('dp', 'tensor')), may hold values from -3 to 3
- final_gain: bfloat16 [512], P(('dp', 'tensor')), may hold values from 0.25 to 1.75
- final_bias: bfloat16 [512], P(('dp', 'tensor')), may hold values from -2.390625 to 2.390625
- w_proj: bfloat16 [512, 2048], P(('dp', 'tensor')), may hold values from -0.25 to 0.25
Outputs:
- lm_out: bfloat16 [2, 8192, 2048], P(None, ('dp', 'tensor'))
- table_grad: float32 [32768, 512], P('dp', 'tensor')
- grad_ln_gain_one: float32 [2, 512], P(None, ('dp', 'tensor'))
- grad_ln_bias_one: float32 [2, 512], P(None, ('dp', 'tensor'))
- grad_w_qkv: float32 [2, 512, 1536], P(None, ('dp', 'tensor'))
- grad_bias_query: float32 [2, 512], P(None, ('dp', 'tensor'))
- grad_bias_value: float32 [2, 512], P(None, ('dp', 'tensor'))
- grad_w_attn_out: float32 [2, 512, 512], P(None, ('dp', 'tensor'))
- grad_bias_attn_out: float32 [2, 512], P(None, ('dp', 'tensor'))
- grad_ln_gain_two: float32 [2, 512], P(None, ('dp', 'tensor'))
- grad_ln_bias_two: float32 [2, 512], P(None, ('dp', 'tensor'))
- grad_w_inner: float32 [2, 512, 2048], P(None, ('dp', 'tensor'))
- grad_bias_inner: float32 [2, 2048], P(None, ('dp', 'tensor'))
- grad_w_outer: float32 [2, 2048, 512], P(None, ('dp', 'tensor'))
- grad_bias_outer: float32 [2, 512], P(None, ('dp', 'tensor'))
- grad_final_gain: float32 [512], P(('dp', 'tensor'))
- grad_final_bias: float32 [512], P(('dp', 'tensor'))
- grad_w_proj: float32 [512, 2048], P(('dp', 'tensor'))
Inputs may be any that keep to these rules, and one draw needn't show every extreme that they name: text_ids address entries of the same micro-batch and the same group of 64 entries as the step on tokens states. `piece_counts`: every micro-batch has an entry with 7 filled slots.
All inputs are finite; a program needn't handle non-finite values.
Results may differ from a plain program's by a relative error of at most 0.028.
Values may be sent and summed in bfloat16 or wider, within the bound.
No kernel may reach another device: no remote copies, remote signals or barrier semaphores. Data moves between devices by JAX's collectives and lax.ppermute only.
A program may use at most 448 MiB of HBM per device.

v0:
```python
import jax
import jax.numpy as jnp
from jax import lax
from jax.sharding import PartitionSpec as P

HEAD_DIM = 64


EPS_NORM = 1e-05
HIGH = lax.Precision.HIGHEST
SQRT_HALF = 0.7071067811865476
INV_SQRT_TAU = 0.3989422804014327


def matmul(left, right):
    return jnp.dot(left, right, preferred_element_type=jnp.float32)


def matmul_right_t(left, right):
    return lax.dot_general(
        left, right, (((1,), (1,)), ((), ())), preferred_element_type=jnp.float32
    )


def matmul_left_t(left, right, precision=None):
    return lax.dot_general(
        left,
        right,
        (((0,), (0,)), ((), ())),
        precision=precision,
        preferred_element_type=jnp.float32,
    )


def norm_parts(values):
    centered = values - jnp.mean(values, axis=-1, keepdims=True)
    inverse = lax.rsqrt(jnp.mean(centered * centered, axis=-1, keepdims=True) + EPS_NORM)
    return (centered * inverse, inverse)


def norm_back(normed, inverse, grad_scaled):
    return inverse * (
        grad_scaled
        - jnp.mean(grad_scaled, axis=-1, keepdims=True)
        - normed * jnp.mean(grad_scaled * normed, axis=-1, keepdims=True)
    )


def rms_parts(values):
    return lax.rsqrt(jnp.mean(values * values, axis=-1, keepdims=True) + EPS_NORM)


def rms_back(values, inverse, grad_scaled):
    return inverse * grad_scaled - values * inverse**3 * jnp.mean(
        grad_scaled * values, axis=-1, keepdims=True
    )


def rotary_tables(seq_length):
    half_dim = HEAD_DIM // 2
    freqs = 10000.0 ** (-jnp.arange(half_dim, dtype=jnp.float32) * 2.0 / HEAD_DIM)
    angles = jnp.arange(seq_length, dtype=jnp.float32)[:, None] * freqs[None, :]
    angles = jnp.concatenate([angles, angles], axis=-1)
    return (jnp.cos(angles), jnp.sin(angles))


def half_turn(values):
    half_dim = HEAD_DIM // 2
    return jnp.concatenate([-values[..., half_dim:], values[..., :half_dim]], axis=-1)


def rotate(values, cosine, sine):
    return values * cosine[:, None, :] + half_turn(values) * sine[:, None, :]


def unrotate(grads, cosine, sine):
    return grads * cosine[:, None, :] - half_turn(grads * sine[:, None, :])


def fetch_params(shard_params):
    (
        ln_gain_one,
        ln_bias_one,
        w_qkv,
        bias_query,
        bias_value,
        w_attn_out,
        bias_attn_out,
        ln_gain_two,
        ln_bias_two,
        w_inner,
        bias_inner,
        w_outer,
        bias_outer,
        final_gain,
        final_bias,
        w_proj,
    ) = shard_params
    return (
        lax.all_gather(ln_gain_one, ("dp", "tensor"), axis=1, tiled=True),
        lax.all_gather(ln_bias_one, ("dp", "tensor"), axis=1, tiled=True),
        lax.all_gather(w_qkv, ("dp", "tensor"), axis=1, tiled=True),
        lax.all_gather(bias_query, ("dp", "tensor"), axis=1, tiled=True),
        lax.all_gather(bias_value, ("dp", "tensor"), axis=1, tiled=True),
        lax.all_gather(w_attn_out, ("dp", "tensor"), axis=1, tiled=True),
        lax.all_gather(bias_attn_out, ("dp", "tensor"), axis=1, tiled=True),
        lax.all_gather(ln_gain_two, ("dp", "tensor"), axis=1, tiled=True),
        lax.all_gather(ln_bias_two, ("dp", "tensor"), axis=1, tiled=True),
        lax.all_gather(w_inner, ("dp", "tensor"), axis=1, tiled=True),
        lax.all_gather(bias_inner, ("dp", "tensor"), axis=1, tiled=True),
        lax.all_gather(w_outer, ("dp", "tensor"), axis=1, tiled=True),
        lax.all_gather(bias_outer, ("dp", "tensor"), axis=1, tiled=True),
        lax.all_gather(final_gain, ("dp", "tensor"), axis=0, tiled=True),
        lax.all_gather(final_bias, ("dp", "tensor"), axis=0, tiled=True),
        lax.all_gather(w_proj, ("dp", "tensor"), axis=0, tiled=True),
    )


def hyper_forward(hidden_rows, valid_keys, weights):
    (
        gain_one,
        shift_one,
        qkv_weight,
        query_bias,
        value_bias,
        out_weight,
        out_bias,
        gain_two,
        shift_two,
        inner_weight,
        inner_bias,
        outer_weight,
        outer_bias,
    ) = weights
    entry_count, slot_count = valid_keys.shape
    width = hidden_rows.shape[1]
    normed_one, inverse_one = norm_parts(hidden_rows)
    normed_in = (normed_one * gain_one.astype(jnp.float32) + shift_one.astype(jnp.float32)).astype(
        jnp.bfloat16
    )
    mixed = matmul(normed_in, qkv_weight)
    queries = (mixed[:, :width] + query_bias.astype(jnp.float32)).reshape(
        entry_count, slot_count, -1, HEAD_DIM
    )
    keys_all = mixed[:, width : 2 * width].reshape(entry_count, slot_count, -1, HEAD_DIM)
    values_all = (mixed[:, 2 * width :] + value_bias.astype(jnp.float32)).reshape(
        entry_count, slot_count, -1, HEAD_DIM
    )
    scores = jnp.einsum("bqhd,bkhd->bhqk", queries, keys_all, precision=HIGH) * HEAD_DIM ** (-0.5)
    scores = jnp.where(valid_keys[:, None, None, :], scores, -1e30)
    weights_soft = jnp.exp(scores - jnp.max(scores, axis=-1, keepdims=True))
    weights_soft = weights_soft / jnp.sum(weights_soft, axis=-1, keepdims=True)
    context = jnp.einsum("bhqk,bkhd->bqhd", weights_soft, values_all, precision=HIGH).reshape(
        entry_count * slot_count, width
    )
    context_low = context.astype(jnp.bfloat16)
    middle = hidden_rows + matmul(context_low, out_weight) + out_bias.astype(jnp.float32)
    normed_two, inverse_two = norm_parts(middle)
    normed_mid = (normed_two * gain_two.astype(jnp.float32) + shift_two.astype(jnp.float32)).astype(
        jnp.bfloat16
    )
    inner = matmul(normed_mid, inner_weight) + inner_bias.astype(jnp.float32)
    activated = jax.nn.gelu(inner, approximate=False).astype(jnp.bfloat16)
    result = middle + matmul(activated, outer_weight) + outer_bias.astype(jnp.float32)
    kept = (
        normed_one,
        inverse_one,
        normed_in,
        queries,
        keys_all,
        values_all,
        weights_soft,
        context_low,
        normed_two,
        inverse_two,
        normed_mid,
        inner,
        activated,
    )
    return (result, kept)


def hyper_backward(grad_rows, kept, weights):
    (
        gain_one,
        shift_one,
        qkv_weight,
        query_bias,
        value_bias,
        out_weight,
        out_bias,
        gain_two,
        shift_two,
        inner_weight,
        inner_bias,
        outer_weight,
        outer_bias,
    ) = weights
    (
        normed_one,
        inverse_one,
        normed_in,
        queries,
        keys_all,
        values_all,
        weights_soft,
        context_low,
        normed_two,
        inverse_two,
        normed_mid,
        inner,
        activated,
    ) = kept
    width = grad_rows.shape[1]
    grad_outer_bias = jnp.sum(grad_rows, axis=0)
    grad_rows_low = grad_rows.astype(jnp.bfloat16)
    grad_outer = matmul_left_t(activated, grad_rows_low)
    grad_active = matmul_right_t(grad_rows_low, outer_weight)
    slope = (
        0.5 * (1.0 + lax.erf(inner * SQRT_HALF))
        + inner * jnp.exp(-0.5 * inner * inner) * INV_SQRT_TAU
    )
    grad_inner = grad_active * slope
    grad_inner_bias = jnp.sum(grad_inner, axis=0)
    grad_inner_low = grad_inner.astype(jnp.bfloat16)
    grad_inner_weight = matmul_left_t(normed_mid, grad_inner_low)
    grad_normed_mid = matmul_right_t(grad_inner_low, inner_weight)
    grad_gain_two = jnp.sum(grad_normed_mid * normed_two, axis=0)
    grad_shift_two = jnp.sum(grad_normed_mid, axis=0)
    grad_middle = grad_rows + norm_back(
        normed_two, inverse_two, grad_normed_mid * gain_two.astype(jnp.float32)
    )
    grad_out_bias = jnp.sum(grad_middle, axis=0)
    grad_middle_low = grad_middle.astype(jnp.bfloat16)
    grad_out_weight = matmul_left_t(context_low, grad_middle_low)
    grad_context = matmul_right_t(grad_middle_low, out_weight).reshape(queries.shape)
    grad_soft = jnp.einsum("bqhd,bkhd->bhqk", grad_context, values_all, precision=HIGH)
    grad_scores = (
        weights_soft
        * (grad_soft - jnp.sum(weights_soft * grad_soft, axis=-1, keepdims=True))
        * HEAD_DIM ** (-0.5)
    )
    grad_values = jnp.einsum("bhqk,bqhd->bkhd", weights_soft, grad_context, precision=HIGH).reshape(
        -1, width
    )
    grad_queries = jnp.einsum("bhqk,bkhd->bqhd", grad_scores, keys_all, precision=HIGH).reshape(
        -1, width
    )
    grad_keys = jnp.einsum("bhqk,bqhd->bkhd", grad_scores, queries, precision=HIGH).reshape(
        -1, width
    )
    grad_query_bias = jnp.sum(grad_queries, axis=0)
    grad_value_bias = jnp.sum(grad_values, axis=0)
    grad_mixed_low = jnp.concatenate([grad_queries, grad_keys, grad_values], axis=1).astype(
        jnp.bfloat16
    )
    grad_qkv = matmul_left_t(normed_in, grad_mixed_low)
    grad_normed_in = matmul_right_t(grad_mixed_low, qkv_weight)
    grad_gain_one = jnp.sum(grad_normed_in * normed_one, axis=0)
    grad_shift_one = jnp.sum(grad_normed_in, axis=0)
    grad_below = grad_middle + norm_back(
        normed_one, inverse_one, grad_normed_in * gain_one.astype(jnp.float32)
    )
    return (
        grad_below,
        (
            grad_gain_one,
            grad_shift_one,
            grad_qkv,
            grad_query_bias,
            grad_value_bias,
            grad_out_weight,
            grad_out_bias,
            grad_gain_two,
            grad_shift_two,
            grad_inner_weight,
            grad_inner_bias,
            grad_outer,
            grad_outer_bias,
        ),
    )


def local(
    piece_table,
    piece_ids,
    piece_counts,
    text_ids,
    cotangent,
    rms_gain_one,
    w_query,
    w_key,
    w_value,
    w_output,
    rms_gain_two,
    w_gate,
    w_up,
    w_down,
    ln_gain_one,
    ln_bias_one,
    w_qkv,
    bias_query,
    bias_value,
    w_attn_out,
    bias_attn_out,
    ln_gain_two,
    ln_bias_two,
    w_inner,
    bias_inner,
    w_outer,
    bias_outer,
    final_gain,
    final_bias,
    w_proj,
):
    shard_params = (
        ln_gain_one,
        ln_bias_one,
        w_qkv,
        bias_query,
        bias_value,
        w_attn_out,
        bias_attn_out,
        ln_gain_two,
        ln_bias_two,
        w_inner,
        bias_inner,
        w_outer,
        bias_outer,
        final_gain,
        final_bias,
        w_proj,
    )
    tensor_size = lax.axis_size("tensor")
    tensor_index = lax.axis_index("tensor")
    micro_count, group_entries, slot_count = piece_ids.shape
    own_entries = group_entries // tensor_size
    seq_length = text_ids.shape[1]
    share_rows = cotangent.shape[1]
    share_start = tensor_index * share_rows
    layer_count = ln_gain_one.shape[0]
    width = ln_gain_one.shape[1] * lax.axis_size(("dp", "tensor"))
    gain_first = rms_gain_one.astype(jnp.float32)
    gain_second = rms_gain_two.astype(jnp.float32)
    cosine, sine = rotary_tables(seq_length)
    positions = jnp.arange(seq_length)
    causal = positions[:, None] >= positions[None, :]
    scale = HEAD_DIM ** (-0.5)
    table_full = lax.all_gather(piece_table, "dp", axis=0, tiled=True)
    table_accum = jnp.zeros(table_full.shape, jnp.float32)
    grad_accum = None
    block_outputs = []
    for batch_index in range(micro_count):
        fetched = fetch_params(shard_params)
        ids_group = piece_ids[batch_index]
        looked = jnp.take(table_full, ids_group.reshape(-1), axis=0).reshape(
            group_entries, slot_count, -1
        )
        own_rows = lax.all_to_all(looked, "tensor", split_axis=0, concat_axis=2, tiled=True)
        counts_own = lax.dynamic_slice_in_dim(
            piece_counts[batch_index], tensor_index * own_entries, own_entries, 0
        )
        valid_keys = jnp.arange(slot_count)[None, :] < counts_own[:, None]
        hidden_rows = own_rows.reshape(own_entries * slot_count, width).astype(jnp.float32)
        saved = []
        for layer_index in range(layer_count):
            hidden_rows, kept = hyper_forward(
                hidden_rows, valid_keys, [stack[layer_index] for stack in fetched[:13]]
            )
            saved.append(kept)
        pooled = hidden_rows.reshape(own_entries, slot_count, width)[:, 0]
        normed_final, inverse_final = norm_parts(pooled)
        final_gain_wide = fetched[13].astype(jnp.float32)
        pooled_norm = (normed_final * final_gain_wide + fetched[14].astype(jnp.float32)).astype(
            jnp.bfloat16
        )
        embeds = matmul(pooled_norm, fetched[15]).astype(jnp.bfloat16)
        embeds_group = lax.all_gather(embeds, "tensor", axis=0, tiled=True)
        token_ids = text_ids[batch_index]
        tokens_full = jnp.take(embeds_group, token_ids, axis=0).astype(jnp.float32)
        tokens_share = lax.dynamic_slice_in_dim(tokens_full, share_start, share_rows, 0)
        inverse_first = rms_parts(tokens_full)
        normed_first = (tokens_full * inverse_first * gain_first).astype(jnp.bfloat16)
        queries = rotate(
            matmul(normed_first, w_query).reshape(seq_length, -1, HEAD_DIM), cosine, sine
        ).astype(jnp.bfloat16)
        keys_rot = rotate(
            matmul(normed_first, w_key).reshape(seq_length, -1, HEAD_DIM), cosine, sine
        ).astype(jnp.bfloat16)
        values_lm = (
            matmul(normed_first, w_value).astype(jnp.bfloat16).reshape(seq_length, -1, HEAD_DIM)
        )
        kv_local = keys_rot.shape[1]
        queries = queries.reshape(seq_length, kv_local, -1, HEAD_DIM)
        scores = (
            jnp.einsum("sjgd,tjd->jgst", queries, keys_rot, preferred_element_type=jnp.float32)
            * scale
        )
        scores = jnp.where(causal, scores, -1e30)
        row_max = jnp.max(scores, axis=-1, keepdims=True)
        expon = jnp.exp(scores - row_max)
        row_total = jnp.sum(expon, axis=-1, keepdims=True)
        log_total = row_max + jnp.log(row_total)
        soft_low = (expon / row_total).astype(jnp.bfloat16)
        context = (
            jnp.einsum("jgst,tjd->sjgd", soft_low, values_lm, preferred_element_type=jnp.float32)
            .astype(jnp.bfloat16)
            .reshape(seq_length, -1)
        )
        attn_share = lax.psum_scatter(
            matmul(context, w_output).astype(jnp.bfloat16),
            "tensor",
            scatter_dimension=0,
            tiled=True,
        ).astype(jnp.float32)
        hidden_share = tokens_share + attn_share
        inverse_second = rms_parts(hidden_share)
        normed_second = (hidden_share * inverse_second * gain_second).astype(jnp.bfloat16)
        normed_second_all = lax.all_gather(normed_second, "tensor", axis=0, tiled=True)
        gate = matmul(normed_second_all, w_gate)
        upward = matmul(normed_second_all, w_up)
        sigmoid_gate = jax.nn.sigmoid(gate)
        silu_gate = gate * sigmoid_gate
        activated = (silu_gate * upward).astype(jnp.bfloat16)
        mlp_share = lax.psum_scatter(
            matmul(activated, w_down).astype(jnp.bfloat16),
            "tensor",
            scatter_dimension=0,
            tiled=True,
        ).astype(jnp.float32)
        block_outputs.append((hidden_share + mlp_share).astype(jnp.bfloat16))
        grad_output = cotangent[batch_index]
        grad_mlp = lax.all_gather(grad_output.astype(jnp.bfloat16), "tensor", axis=0, tiled=True)
        grad_active = matmul_right_t(grad_mlp, w_down)
        slope_silu = sigmoid_gate * (1.0 + gate * (1.0 - sigmoid_gate))
        grad_gate = (grad_active * upward * slope_silu).astype(jnp.bfloat16)
        grad_upward = (grad_active * silu_gate).astype(jnp.bfloat16)
        grad_normed_second = lax.psum_scatter(
            (matmul_right_t(grad_gate, w_gate) + matmul_right_t(grad_upward, w_up)).astype(
                jnp.bfloat16
            ),
            "tensor",
            scatter_dimension=0,
            tiled=True,
        ).astype(jnp.float32)
        grad_hidden = grad_output + rms_back(
            hidden_share, inverse_second, grad_normed_second * gain_second
        )
        grad_attn = lax.all_gather(grad_hidden.astype(jnp.bfloat16), "tensor", axis=0, tiled=True)
        grad_context = (
            matmul_right_t(grad_attn, w_output).astype(jnp.bfloat16).reshape(queries.shape)
        )
        scores_again = (
            jnp.einsum("sjgd,tjd->jgst", queries, keys_rot, preferred_element_type=jnp.float32)
            * scale
        )
        soft_again = jnp.where(causal, jnp.exp(scores_again - log_total), 0.0)
        grad_soft = jnp.einsum(
            "sjgd,tjd->jgst", grad_context, values_lm, preferred_element_type=jnp.float32
        )
        grad_scores = (
            soft_again * (grad_soft - jnp.sum(soft_again * grad_soft, axis=-1, keepdims=True))
        ).astype(jnp.bfloat16)
        grad_values = jnp.einsum(
            "jgst,sjgd->tjd",
            soft_again.astype(jnp.bfloat16),
            grad_context,
            preferred_element_type=jnp.float32,
        )
        grad_queries = (
            jnp.einsum("jgst,tjd->sjgd", grad_scores, keys_rot, preferred_element_type=jnp.float32)
            * scale
        )
        grad_keys = (
            jnp.einsum("jgst,sjgd->tjd", grad_scores, queries, preferred_element_type=jnp.float32)
            * scale
        )
        grad_queries = (
            unrotate(grad_queries.reshape(seq_length, -1, HEAD_DIM), cosine, sine)
            .astype(jnp.bfloat16)
            .reshape(seq_length, -1)
        )
        grad_keys = unrotate(grad_keys, cosine, sine).astype(jnp.bfloat16).reshape(seq_length, -1)
        grad_values = grad_values.astype(jnp.bfloat16).reshape(seq_length, -1)
        grad_normed_first = (
            matmul_right_t(grad_queries, w_query)
            + matmul_right_t(grad_keys, w_key)
            + matmul_right_t(grad_values, w_value)
        )
        grad_tokens = rms_back(tokens_full, inverse_first, grad_normed_first * gain_first)
        onehot_full = (token_ids[:, None] == jnp.arange(group_entries)[None, :]).astype(jnp.float32)
        onehot_share = lax.dynamic_slice_in_dim(onehot_full, share_start, share_rows, 0)
        grad_embeds = lax.psum_scatter(
            (
                matmul_left_t(onehot_full, grad_tokens, HIGH)
                + matmul_left_t(onehot_share, grad_hidden, HIGH)
            ).astype(jnp.bfloat16),
            "tensor",
            scatter_dimension=0,
            tiled=True,
        )
        grad_projection = matmul_left_t(pooled_norm, grad_embeds)
        grad_pooled_norm = matmul_right_t(grad_embeds, fetched[15])
        grad_gain_final = jnp.sum(grad_pooled_norm * normed_final, axis=0)
        grad_bias_final = jnp.sum(grad_pooled_norm, axis=0)
        grad_pooled = norm_back(normed_final, inverse_final, grad_pooled_norm * final_gain_wide)
        grad_rows = jnp.concatenate(
            [grad_pooled[:, None, :], jnp.zeros((own_entries, slot_count - 1, width), jnp.float32)],
            axis=1,
        ).reshape(own_entries * slot_count, width)
        layer_grads = []
        for layer_index in range(layer_count - 1, -1, -1):
            grad_rows, grads_one = hyper_backward(
                grad_rows, saved[layer_index], [stack[layer_index] for stack in fetched[:13]]
            )
            layer_grads.insert(0, grads_one)
        batch_grads = [
            jnp.stack([grads_one[position] for grads_one in layer_grads]) for position in range(13)
        ]
        batch_grads = batch_grads + [grad_gain_final, grad_bias_final, grad_projection]
        grad_accum = (
            batch_grads
            if grad_accum is None
            else [first + second for first, second in zip(grad_accum, batch_grads)]
        )
        grad_pieces = grad_rows.astype(jnp.bfloat16).reshape(own_entries, slot_count, width)
        grad_looked = lax.all_to_all(grad_pieces, "tensor", split_axis=2, concat_axis=0, tiled=True)
        grad_slots = grad_looked.reshape(-1, grad_looked.shape[-1])
        table_accum = table_accum.at[ids_group.reshape(-1)].add(grad_slots.astype(jnp.float32))
    table_grad = lax.psum_scatter(table_accum, "dp", scatter_dimension=0, tiled=True)
    (
        grad_gain_one,
        grad_bias_one,
        grad_qkv,
        grad_query_bias,
        grad_value_bias,
        grad_attn_out,
        grad_attn_bias,
        grad_gain_two,
        grad_bias_two,
        grad_inner,
        grad_inner_bias,
        grad_outer,
        grad_outer_bias,
        grad_final_gain,
        grad_final_bias,
        grad_proj,
    ) = grad_accum
    reduced = (
        lax.psum_scatter(grad_gain_one, ("dp", "tensor"), scatter_dimension=1, tiled=True),
        lax.psum_scatter(grad_bias_one, ("dp", "tensor"), scatter_dimension=1, tiled=True),
        lax.psum_scatter(grad_qkv, ("dp", "tensor"), scatter_dimension=1, tiled=True),
        lax.psum_scatter(grad_query_bias, ("dp", "tensor"), scatter_dimension=1, tiled=True),
        lax.psum_scatter(grad_value_bias, ("dp", "tensor"), scatter_dimension=1, tiled=True),
        lax.psum_scatter(grad_attn_out, ("dp", "tensor"), scatter_dimension=1, tiled=True),
        lax.psum_scatter(grad_attn_bias, ("dp", "tensor"), scatter_dimension=1, tiled=True),
        lax.psum_scatter(grad_gain_two, ("dp", "tensor"), scatter_dimension=1, tiled=True),
        lax.psum_scatter(grad_bias_two, ("dp", "tensor"), scatter_dimension=1, tiled=True),
        lax.psum_scatter(grad_inner, ("dp", "tensor"), scatter_dimension=1, tiled=True),
        lax.psum_scatter(grad_inner_bias, ("dp", "tensor"), scatter_dimension=1, tiled=True),
        lax.psum_scatter(grad_outer, ("dp", "tensor"), scatter_dimension=1, tiled=True),
        lax.psum_scatter(grad_outer_bias, ("dp", "tensor"), scatter_dimension=1, tiled=True),
        lax.psum_scatter(grad_final_gain, ("dp", "tensor"), scatter_dimension=0, tiled=True),
        lax.psum_scatter(grad_final_bias, ("dp", "tensor"), scatter_dimension=0, tiled=True),
        lax.psum_scatter(grad_proj, ("dp", "tensor"), scatter_dimension=0, tiled=True),
    )
    return (jnp.stack(block_outputs), table_grad) + tuple(reduced)


def solution(mesh):
    return jax.shard_map(
        local,
        mesh=mesh,
        in_specs=(
            P("dp", "tensor"),
            P(None, "dp", None),
            P(None, "dp"),
            P(None, "dp"),
            P(None, ("dp", "tensor"), None),
            P(),
            P(None, "tensor"),
            P(None, "tensor"),
            P(None, "tensor"),
            P("tensor", None),
            P(),
            P(None, "tensor"),
            P(None, "tensor"),
            P("tensor", None),
            P(None, ("dp", "tensor")),
            P(None, ("dp", "tensor")),
            P(None, ("dp", "tensor"), None),
            P(None, ("dp", "tensor")),
            P(None, ("dp", "tensor")),
            P(None, ("dp", "tensor"), None),
            P(None, ("dp", "tensor")),
            P(None, ("dp", "tensor")),
            P(None, ("dp", "tensor")),
            P(None, ("dp", "tensor"), None),
            P(None, ("dp", "tensor")),
            P(None, ("dp", "tensor"), None),
            P(None, ("dp", "tensor")),
            P(("dp", "tensor")),
            P(("dp", "tensor")),
            P(("dp", "tensor"), None),
        ),
        out_specs=(
            P(None, ("dp", "tensor"), None),
            P("dp", "tensor"),
            P(None, ("dp", "tensor")),
            P(None, ("dp", "tensor")),
            P(None, ("dp", "tensor"), None),
            P(None, ("dp", "tensor")),
            P(None, ("dp", "tensor")),
            P(None, ("dp", "tensor"), None),
            P(None, ("dp", "tensor")),
            P(None, ("dp", "tensor")),
            P(None, ("dp", "tensor")),
            P(None, ("dp", "tensor"), None),
            P(None, ("dp", "tensor")),
            P(None, ("dp", "tensor"), None),
            P(None, ("dp", "tensor")),
            P(("dp", "tensor")),
            P(("dp", "tensor")),
            P(("dp", "tensor"), None),
        ),
        check_vma=False,
    )
```

profile of v0, /device:TPU:0, one launch (start us, length us, event | category | flops | bytes accessed | tf_op | source)
XLA Modules:
  0.0 3729.8 jit_solution(8293748039886830675)
XLA Ops:
  17.5 45.0 %all-reduce.7 = (bf16[512]{0:T(512)(128)(2,1)S(1)}, bf16[512]{0:T(512)(128)(2,1)S(1)}) all-reduce(bf16[512]{0:T(512)(128)(2,1)S(1)} %dynamic-update-slice.1, bf16[512]{0:T(512)(128)(2,1)S(1)} %dynamic-update-slice), channel_id=1, replica_groups=mesh['dp'=8,'tensor'=4] {'dp','tensor'}, use_global_device_ids=true, to_apply=%add.3 | all-reduce | flops 1024 | bytes 4096
  63.2 39.3 %all-gather.4 = bf16[32,16,2]{1,2,0:T(2,128)(2,1)S(1)} all-gather(bf16[1,16,2]{1,2,0:T(2,128)(2,1)} %bitcast.1106), channel_id=1, replica_groups=mesh['dp'=8,'tensor'=4] {'dp','tensor'}, dimensions={0}, use_global_device_ids=true | all-gather | bytes 2112 | tf_op jit(solution)/shard_map/all_gather | solution.py:106
  140.8 37.7 %all-gather.1 = bf16[32,16,2]{1,2,0:T(2,128)(2,1)S(1)} all-gather(bf16[1,16,2]{1,2,0:T(2,128)(2,1)} %bitcast.1108), channel_id=1, replica_groups=mesh['dp'=8,'tensor'=4] {'dp','tensor'}, dimensions={0}, use_global_device_ids=true | all-gather | bytes 2112 | tf_op jit(solution)/shard_map/all_gather | solution.py:101
  216.7 37.8 %all-gather.3 = bf16[32,16,2]{1,2,0:T(2,128)(2,1)S(1)} all-gather(bf16[1,16,2]{1,2,0:T(2,128)(2,1)} %bitcast.1110), channel_id=1, replica_groups=mesh['dp'=8,'tensor'=4] {'dp','tensor'}, dimensions={0}, use_global_device_ids=true | all-gather | bytes 2112 | tf_op jit(solution)/shard_map/all_gather | solution.py:103
  294.2 37.8 %all-gather.7 = bf16[32,64,2]{1,2,0:T(2,128)(2,1)S(1)} all-gather(bf16[1,64,2]{1,2,0:T(2,128)(2,1)} %bitcast.1112), channel_id=1, replica_groups=mesh['dp'=8,'tensor'=4] {'dp','tensor'}, dimensions={0}, use_global_device_ids=true | all-gather | bytes 8448 | tf_op jit(solution)/shard_map/all_gather | solution.py:110
  992.1 43.5 %reduce-scatter.44.cloned.1.call-done = bf16[256,2048]{1,0:T(8,128)(2,1)} async-done(((bf16[1024,2048]{1,0:T(8,128)(2,1)}), bf16[256,2048]{1,0:T(8,128)(2,1)}) %reduce-scatter.44.cloned.1.call-update) | async-done | bytes 1048592 | tf_op jit(solution)/shard_map/reduce_scatter | solution.py:425
  1035.5 47.1 %reduce-scatter.48.cloned.1.call-done = bf16[256,2048]{1,0:T(8,128)(2,1)} async-done(((bf16[1024,2048]{1,0:T(8,128)(2,1)}), bf16[256,2048]{1,0:T(8,128)(2,1)}) %reduce-scatter.48.cloned.1.call-update) | async-done | bytes 1048592 | tf_op jit(solution)/shard_map/reduce_scatter | solution.py:425
  1166.0 44.5 %fusion = (f32[8,1024]{1,0:T(8,128)S(1)}, f32[8,1024]{1,0:T(8,128)S(1)}, f32[1024,1024,8]{1,0,2:T(8,128)}) fusion(f32[1024,1024,8]{1,0,2:T(8,128)} %get-tuple-element.254, f32[8,1024]{1,0:T(8,128)S(1)} %log_add_fusion, pred[1024,1024]{0,1:T(8,128)(4,1)S(1)} %copy-done.2, f32[1024,1024,8]{1,0,2:T(8,128)} %fusion.433, f32[8,1024]{1,0:T(8,128)S(1)} %log_add_fusion.1, ...), kind=kOutput, calls=%fused_computation.8 | convolution fusion | flops 1157611520 | bytes 136577024 | tf_op jit(solution)/shard_map/sjgd,tjd->jgst/dot_general | solution.py:458
  1210.5 55.3 %fusion.19 = (bf16[8,1024,1024]{1,2,0:T(8,128)(2,1)}, bf16[8,1024,1024]{1,2,0:T(8,128)(2,1)}) fusion(f32[1024,1024,8]{1,0,2:T(8,128)} %get-tuple-element.255, f32[1024,1024,8]{1,0,2:T(8,128)} %get-tuple-element.254, f32[8,1024]{1,0:T(8,128)S(1)} %get-tuple-element.20, f32[8,1024]{1,0:T(8,128)S(1)} %log_add_fusion, pred[1024,1024]{0,1:T(8,128)(4,1)S(1)} %copy-done.2, ...), kind=kLoop, calls=%fused_computation.37 | loop fusion | flops 100663296 | bytes 168951808 | tf_op jit(solution)/shard_map/reshape.45
  1673.5 40.8 %all-reduce.6 = (f32[512]{0:T(512)S(1)}, f32[512]{0:T(512)S(1)}) all-reduce(f32[512]{0:T(512)S(1)} %add.888, f32[512]{0:T(512)S(1)} %add.889), channel_id=24, replica_groups=mesh['dp'=8,'tensor'=4] {'dp','tensor'}, use_global_device_ids=true, to_apply=%region_128.131.clone | all-reduce | flops 1024 | bytes 8192
  1716.8 109.8 %reduce-scatter.72.cloned.1.call-done = f32[16,2]{1,0:T(8,128)} async-done(((f32[512,2]{1,0:T(8,128)}), f32[16,2]{1,0:T(8,128)}) %reduce-scatter.72.cloned.1.call-update) | async-done | bytes 144
  1827.9 130.3 %reduce-scatter.74.cloned.1.call-done = f32[16,2]{1,0:T(8,128)} async-done(((f32[512,2]{1,0:T(8,128)}), f32[16,2]{1,0:T(8,128)}) %reduce-scatter.74.cloned.1.call-update) | async-done | bytes 144
  1959.5 130.2 %reduce-scatter.76.cloned.1.call-done = f32[16,2]{1,0:T(8,128)} async-done(((f32[512,2]{1,0:T(8,128)}), f32[16,2]{1,0:T(8,128)}) %reduce-scatter.76.cloned.1.call-update) | async-done | bytes 144
  2091.1 130.3 %reduce-scatter.78.cloned.1.call-done = f32[16,2]{1,0:T(8,128)} async-done(((f32[512,2]{1,0:T(8,128)}), f32[16,2]{1,0:T(8,128)}) %reduce-scatter.78.cloned.1.call-update) | async-done | bytes 144
  2222.7 130.2 %reduce-scatter.80.cloned.1.call-done = f32[16,2]{1,0:T(8,128)} async-done(((f32[512,2]{1,0:T(8,128)}), f32[16,2]{1,0:T(8,128)}) %reduce-scatter.80.cloned.1.call-update) | async-done | bytes 144
  2354.2 130.1 %reduce-scatter.82.cloned.1.call-done = f32[16,2]{1,0:T(8,128)} async-done(((f32[512,2]{1,0:T(8,128)}), f32[16,2]{1,0:T(8,128)}) %reduce-scatter.82.cloned.1.call-update) | async-done | bytes 144
  2485.6 130.3 %reduce-scatter.86.cloned.1.call-done = f32[16,2]{1,0:T(8,128)} async-done(((f32[512,2]{1,0:T(8,128)}), f32[16,2]{1,0:T(8,128)}) %reduce-scatter.86.cloned.1.call-update) | async-done | bytes 144
  2617.3 131.6 %reduce-scatter.84.cloned.1.call-done = f32[64,2]{1,0:T(8,128)} async-done(((f32[2048,2]{1,0:T(8,128)}), f32[64,2]{1,0:T(8,128)}) %reduce-scatter.84.cloned.1.call-update) | async-done | bytes 528
  2750.4 134.2 %reduce-scatter.62.cloned.1.call-done = f32[2,16,512]{2,1,0:T(8,128)} async-done(((f32[2,512,512]{2,1,0:T(8,128)}), f32[2,16,512]{2,1,0:T(8,128)}) %reduce-scatter.62.cloned.1.call-update) | async-done | bytes 65552 | tf_op jit(solution)/shard_map/reduce_scatter | solution.py:555
  2884.5 116.5 %reduce-scatter.60.cloned.1.call-done = f32[2,16,1536]{2,1,0:T(8,128)} async-done(((f32[2,512,1536]{2,1,0:T(8,128)}), f32[2,16,1536]{2,1,0:T(8,128)}) %reduce-scatter.60.cloned.1.call-update) | async-done | bytes 196624 | tf_op jit(solution)/shard_map/reduce_scatter | solution.py:552
  3001.0 143.1 %reduce-scatter.68.cloned.1.call-done = f32[16,2048]{1,0:T(8,128)} async-done(((f32[512,2048]{1,0:T(8,128)}), f32[16,2048]{1,0:T(8,128)}) %reduce-scatter.68.cloned.1.call-update) | async-done | bytes 131088 | tf_op jit(solution)/shard_map/reduce_scatter | solution.py:565
  3144.1 147.8 %reduce-scatter.64.cloned.1.call-done = f32[2,16,2048]{2,1,0:T(8,128)} async-done(((f32[2,512,2048]{2,1,0:T(8,128)}), f32[2,16,2048]{2,1,0:T(8,128)}) %reduce-scatter.64.cloned.1.call-update) | async-done | bytes 262160 | tf_op jit(solution)/shard_map/reduce_scatter | solution.py:559
  3292.0 147.7 %reduce-scatter.66.cloned.1.call-done = f32[2,64,512]{2,1,0:T(8,128)} async-done(((f32[2,2048,512]{2,1,0:T(8,128)}), f32[2,64,512]{2,1,0:T(8,128)}) %reduce-scatter.66.cloned.1.call-update) | async-done | bytes 262160 | tf_op jit(solution)/shard_map/reduce_scatter | solution.py:561
  3439.7 283.4 %reduce-scatter.58.cloned.1.call-done = f32[4096,128]{1,0:T(8,128)} async-done(((f32[32768,128]{1,0:T(8,128)}), f32[4096,128]{1,0:T(8,128)}) %reduce-scatter.58.cloned.1.call-update) | async-done | bytes 2097168 | tf_op jit(solution)/shard_map/reduce_scatter | solution.py:530
  (1120 shorter events, 1287.0 us)
Async XLA Ops:
  7.2 404.3 %all-gather.22.cloned.1.call-start = ((), (), s32[]{:S(2)}) async-start(), calls=%async_computation.27 | async-start | bytes 9437184 | tf_op jit(solution)/shard_map/all_gather | solution.py:349
  7.9 429.9 %all-gather.24.cloned.1.call-start = ((), (), s32[]{:S(2)}) async-start(), calls=%async_computation.28 | async-start | bytes 3244032 | tf_op jit(solution)/shard_map/all_gather | solution.py:102
  8.7 447.8 %all-gather.26.cloned.1.call-start = ((), (), s32[]{:S(2)}) async-start(), calls=%async_computation.29 | async-start | bytes 1081344 | tf_op jit(solution)/shard_map/all_gather | solution.py:105
  9.4 449.9 %all-gather.28.cloned.1.call-start = ((), (), s32[]{:S(2)}) async-start(), calls=%async_computation.30 | async-start | bytes 4325376 | tf_op jit(solution)/shard_map/all_gather | solution.py:109
  10.0 454.8 %all-gather.30.cloned.1.call-start = ((), (), s32[]{:S(2)}) async-start(), calls=%async_computation.31 | async-start | bytes 4325376 | tf_op jit(solution)/shard_map/all_gather | solution.py:111
  10.6 523.9 %all-gather.32.cloned.1.call-start = ((), (), s32[]{:S(2)}) async-start(), calls=%async_computation.32 | async-start | bytes 2162688 | tf_op jit(solution)/shard_map/all_gather | solution.py:115
  430.8 271.3 %reduce-scatter.42.cloned.1.call-start = ((), (), s32[]{:S(2)}) async-start(), calls=%async_computation.33 | async-start | bytes 5242880 | tf_op jit(solution)/shard_map/reduce_scatter | solution.py:410
  969.7 155.7 %all-gather.40.cloned.1.call-start = ((), (), s32[]{:S(2)}) async-start(), calls=%async_computation.41 | async-start | bytes 5242880 | tf_op jit(solution)/shard_map/all_gather | solution.py:449
  1091.4 329.5 %reduce-scatter.56.cloned.1.call-start = ((), (), s32[]{:S(2)}) async-start(), calls=%async_computation.46 | async-start | bytes 327680 | tf_op jit(solution)/shard_map/reduce_scatter | solution.py:493
  1411.8 303.7 %reduce-scatter.70.cloned.1.call-start = ((), (), s32[]{:S(2)}) async-start(), calls=%async_computation.53 | async-start | bytes 270336
  1561.2 265.4 %reduce-scatter.72.cloned.1.call-start = ((), (), s32[]{:S(2)}) async-start(), calls=%async_computation.54 | async-start | bytes 270336
  1567.0 391.2 %reduce-scatter.74.cloned.1.call-start = ((), (), s32[]{:S(2)}) async-start(), calls=%async_computation.55 | async-start | bytes 270336
  1572.8 516.9 %reduce-scatter.76.cloned.1.call-start = ((), (), s32[]{:S(2)}) async-start(), calls=%async_computation.56 | async-start | bytes 270336
  1574.5 646.8 %reduce-scatter.78.cloned.1.call-start = ((), (), s32[]{:S(2)}) async-start(), calls=%async_computation.57 | async-start | bytes 270336
  1576.1 776.8 %reduce-scatter.80.cloned.1.call-start = ((), (), s32[]{:S(2)}) async-start(), calls=%async_computation.58 | async-start | bytes 270336
  1577.8 906.5 %reduce-scatter.82.cloned.1.call-start = ((), (), s32[]{:S(2)}) async-start(), calls=%async_computation.59 | async-start | bytes 270336
  1579.4 1036.6 %reduce-scatter.86.cloned.1.call-start = ((), (), s32[]{:S(2)}) async-start(), calls=%async_computation.61 | async-start | bytes 270336
  1581.1 1167.9 %reduce-scatter.84.cloned.1.call-start = ((), (), s32[]{:S(2)}) async-start(), calls=%async_computation.60 | async-start | bytes 1081344
  1585.6 1299.0 %reduce-scatter.62.cloned.1.call-start = ((), (), s32[]{:S(2)}) async-start(), calls=%async_computation.49 | async-start | bytes 2162688 | tf_op jit(solution)/shard_map/reduce_scatter | solution.py:555
  1589.7 1411.3 %reduce-scatter.60.cloned.1.call-start = ((), (), s32[]{:S(2)}) async-start(), calls=%async_computation.48 | async-start | bytes 6488064 | tf_op jit(solution)/shard_map/reduce_scatter | solution.py:552
  1598.1 1546.0 %reduce-scatter.68.cloned.1.call-start = ((), (), s32[]{:S(2)}) async-start(), calls=%async_computation.52 | async-start | bytes 4325376 | tf_op jit(solution)/shard_map/reduce_scatter | solution.py:565
  1602.6 1689.4 %reduce-scatter.64.cloned.1.call-start = ((), (), s32[]{:S(2)}) async-start(), calls=%async_computation.50 | async-start | bytes 8650752 | tf_op jit(solution)/shard_map/reduce_scatter | solution.py:559
  1612.2 1827.5 %reduce-scatter.66.cloned.1.call-start = ((), (), s32[]{:S(2)}) async-start(), calls=%async_computation.51 | async-start | bytes 8650752 | tf_op jit(solution)/shard_map/reduce_scatter | solution.py:561
  1636.8 2086.3 %reduce-scatter.58.cloned.1.call-start = ((), (), s32[]{:S(2)}) async-start(), calls=%async_computation.47 | async-start | bytes 18874368 | tf_op jit(solution)/shard_map/reduce_scatter | solution.py:530
  (314 other events, 6347.8 us)
Sparse Core Ops, SparseCore 0:
  10.2 128.6 all-gather.21
  141.8 57.2 all-gather.23
  202.1 52.3 all-gather.25
  257.3 60.9 all-gather.27
  321.1 60.6 all-gather.29
  384.5 55.7 all-gather.31
  893.4 44.5 reduce-scatter.53
  943.9 44.6 reduce-scatter.49
  991.0 44.5 reduce-scatter.43
  1561.3 133.4 reduce-scatter.69
  1697.1 129.4 reduce-scatter.71
  1828.8 129.3 reduce-scatter.73
  1960.4 129.3 reduce-scatter.75
  2092.0 129.3 reduce-scatter.77
  2223.5 129.3 reduce-scatter.79
  2355.0 129.3 reduce-scatter.81
  2486.6 129.3 reduce-scatter.85
  2618.2 130.6 reduce-scatter.83
  2751.7 132.7 reduce-scatter.61
  2890.8 110.2 reduce-scatter.59
  3004.0 140.1 reduce-scatter.67
  3147.0 144.9 reduce-scatter.63
  3295.0 144.6 reduce-scatter.65
  3444.5 278.5 reduce-scatter.57
  (11 shorter events, 376.2 us)
where the time goes:
time: 3740 us; the launch traced here: 3730 us
  waiting for transfers between devices  2300 us (61%)
  matrix products  596 us (16%)
  blocking collectives  436 us (12%)
  other arithmetic  198 us (5%)
  local copies, waits for them, and re-layouts  168 us (4%)
    unnamed x44, waiting for transfers between devices  1030 us
    reduce_scatter x1, waiting for transfers between devices, local(): lax.psum_scatter(table_accum, 'dp', scatter_dimension=0, tiled=True)  283 us
    dot_general x32, matrix products, matmul_right_t(): lax.dot_general(left, right, (((1,), (1,)), ((), ())), preferred_element_...  194 us
    reduce_scatter x1, waiting for transfers between devices, local(): lax.psum_scatter(grad_inner, ('dp', 'tensor'), scatter_dimension=1, tiled...  148 us
    reduce_scatter x1, waiting for transfers between devices, local(): lax.psum_scatter(grad_outer, ('dp', 'tensor'), scatter_dimension=1, tiled...  148 us
    reduce_scatter x1, waiting for transfers between devices, local(): lax.psum_scatter(grad_proj, ('dp', 'tensor'), scatter_dimension=0, tiled=...  143 us
    reduce_scatter x1, waiting for transfers between devices, local(): lax.psum_scatter(grad_attn_out, ('dp', 'tensor'), scatter_dimension=1, ti...  134 us
    dot_general x32, matrix products, matmul(): return jnp.dot(left, right, preferred_element_type=jnp.float32)  133 us
  transfers between devices with their start and end apart: 39, of which 27 were waited for; matrix products, arithmetic and copies ran while one was open for 13% of the time, Pallas kernels for 0%

commit v1 on v0

v1 whole, which is shorter than its diff:
```python
import jax
import jax.numpy as jnp
from jax import lax
from jax.experimental import pallas as pl
from jax.experimental.pallas import tpu as pltpu
from jax.sharding import PartitionSpec as P

HEAD_DIM = 64
EPS_NORM = 1e-05
HIGH = lax.Precision.HIGHEST
SQRT_HALF = 0.7071067811865476
INV_SQRT_TAU = 0.3989422804014327
BOTH = ("dp", "tensor")
F32 = jnp.float32
BF16 = jnp.bfloat16


def matmul(left, right):
    return jnp.dot(left, right, preferred_element_type=F32)


def matmul_right_t(left, right):
    return lax.dot_general(left, right, (((1,), (1,)), ((), ())), preferred_element_type=F32)


def matmul_left_t(left, right):
    return lax.dot_general(left, right, (((0,), (0,)), ((), ())), preferred_element_type=F32)


def split_two(values):
    high = lax.reduce_precision(values, 8, 7)
    return high.astype(BF16), (values - high).astype(BF16)


def norm_parts(values):
    centered = values - jnp.mean(values, axis=-1, keepdims=True)
    inverse = lax.rsqrt(jnp.mean(centered * centered, axis=-1, keepdims=True) + EPS_NORM)
    return (centered * inverse, inverse)


def norm_back(normed, inverse, grad_scaled):
    return inverse * (
        grad_scaled
        - jnp.mean(grad_scaled, axis=-1, keepdims=True)
        - normed * jnp.mean(grad_scaled * normed, axis=-1, keepdims=True)
    )


def rms_parts(values):
    return lax.rsqrt(jnp.mean(values * values, axis=-1, keepdims=True) + EPS_NORM)


def rms_back(values, inverse, grad_scaled):
    return inverse * grad_scaled - values * inverse**3 * jnp.mean(
        grad_scaled * values, axis=-1, keepdims=True
    )


def rotary_tables(seq_length):
    half_dim = HEAD_DIM // 2
    freqs = 10000.0 ** (-jnp.arange(half_dim, dtype=F32) * 2.0 / HEAD_DIM)
    angles = jnp.arange(seq_length, dtype=F32)[:, None] * freqs[None, :]
    angles = jnp.concatenate([angles, angles], axis=-1)
    return (jnp.cos(angles), jnp.sin(angles))


def half_turn(values):
    half_dim = HEAD_DIM // 2
    return jnp.concatenate([-values[..., half_dim:], values[..., :half_dim]], axis=-1)


def rotate(values, cosine, sine):
    return values * cosine[:, None, :] + half_turn(values) * sine[:, None, :]


def unrotate(grads, cosine, sine):
    return grads * cosine[:, None, :] - half_turn(grads * sine[:, None, :])


def swap(values, axis, bit):
    size = lax.axis_size(axis)
    return lax.ppermute(values, axis, [(i, i ^ bit) for i in range(size)])


def ordered_pair(own, other, index):
    first = jnp.where(index == 0, own, other)
    second = jnp.where(index == 0, other, own)
    return jnp.stack([first, second])


def gather_tensor(values, core):
    from_core = swap(values, "tensor", 1)
    from_chip = swap(values, "tensor", 2)
    from_both = swap(from_chip, "tensor", 1)
    return ordered_pair(values, from_core, core), ordered_pair(from_chip, from_both, core)


def scatter_chip(partial, core):
    sent = lax.dynamic_index_in_dim(partial, 1 - core, 0, keepdims=False)
    kept = lax.dynamic_index_in_dim(partial, core, 0, keepdims=False)
    return kept.astype(F32) + swap(sent, "tensor", 1).astype(F32)


def scatter_tensor(own_chip, other_chip, core):
    away = scatter_chip(other_chip, core).astype(BF16)
    arrived = swap(away, "tensor", 2)
    return scatter_chip(own_chip, core) + arrived.astype(F32)


def gather_dp(values):
    size = lax.axis_size("dp")
    index = lax.axis_index("dp")
    bits = size.bit_length() - 1
    held = values[(None,) * bits]
    for bit in range(bits - 1, -1, -1):
        axis = bits - 1 - bit
        other = swap(held, "dp", 1 << bit)
        side = (index >> bit) & 1
        low = jnp.where(side == 0, held, other)
        high = jnp.where(side == 0, other, held)
        held = jnp.concatenate([low, high], axis=axis)
    return held.reshape((size,) + values.shape)


def lookup_kernel(ids_ref, table_ref, out_ref):
    rows = ids_ref.shape[0]
    height = table_ref.shape[0]
    places = lax.broadcasted_iota(jnp.int32, (rows, height), 1)
    chosen = jnp.where(ids_ref[...] == places, 1.0, 0.0).astype(BF16)
    out_ref[...] = matmul(chosen, table_ref[...]).astype(BF16)


def lookup(ids, table):
    count = ids.shape[0]
    height, width = table.shape
    rows = 512
    return pl.pallas_call(
        lookup_kernel,
        grid=(count // rows,),
        in_specs=[
            pl.BlockSpec((rows, 1), lambda i: (i, 0)),
            pl.BlockSpec((height, width), lambda i: (0, 0)),
        ],
        out_specs=pl.BlockSpec((rows, width), lambda i: (i, 0)),
        out_shape=jax.ShapeDtypeStruct((count, width), BF16),
        compiler_params=pltpu.CompilerParams(vmem_limit_bytes=48 << 20),
        cost_estimate=pl.CostEstimate(
            flops=2 * count * height * width, bytes_accessed=4 * count * width, transcendentals=0
        ),
        name="lookup",
    )(ids[:, None], table)


def collect_kernel(ids_ref, rows_ref, out_ref):
    @pl.when(pl.program_id(0) == 0)
    def _():
        out_ref[...] = jnp.zeros_like(out_ref)

    height = out_ref.shape[0]
    places = lax.broadcasted_iota(jnp.int32, (height, ids_ref.shape[1]), 0)
    chosen = jnp.where(ids_ref[...] == places, 1.0, 0.0).astype(BF16)
    out_ref[...] += matmul(chosen, rows_ref[...])


def collect(ids, values, height):
    count, width = values.shape
    rows = 512
    return pl.pallas_call(
        collect_kernel,
        grid=(count // rows,),
        in_specs=[
            pl.BlockSpec((1, rows), lambda i: (0, i)),
            pl.BlockSpec((rows, width), lambda i: (i, 0)),
        ],
        out_specs=pl.BlockSpec((height, width), lambda i: (0, 0)),
        out_shape=jax.ShapeDtypeStruct((height, width), F32),
        compiler_params=pltpu.CompilerParams(vmem_limit_bytes=48 << 20),
        cost_estimate=pl.CostEstimate(
            flops=2 * count * height * width, bytes_accessed=4 * count * width, transcendentals=0
        ),
        name="collect",
    )(ids[None, :], values)


def hyper_forward(hidden_rows, valid_keys, weights):
    (
        gain_one,
        shift_one,
        qkv_weight,
        query_bias,
        value_bias,
        out_weight,
        out_bias,
        gain_two,
        shift_two,
        inner_weight,
        inner_bias,
        outer_weight,
        outer_bias,
    ) = weights
    entry_count, slot_count = valid_keys.shape
    width = hidden_rows.shape[1]
    normed_one, inverse_one = norm_parts(hidden_rows)
    normed_in = (normed_one * gain_one.astype(jnp.float32) + shift_one.astype(jnp.float32)).astype(
        jnp.bfloat16
    )
    mixed = matmul(normed_in, qkv_weight)
    queries = (mixed[:, :width] + query_bias.astype(jnp.float32)).reshape(
        entry_count, slot_count, -1, HEAD_DIM
    )
    keys_all = mixed[:, width : 2 * width].reshape(entry_count, slot_count, -1, HEAD_DIM)
    values_all = (mixed[:, 2 * width :] + value_bias.astype(jnp.float32)).reshape(
        entry_count, slot_count, -1, HEAD_DIM
    )
    scores = jnp.einsum("bqhd,bkhd->bhqk", queries, keys_all, precision=HIGH) * HEAD_DIM ** (-0.5)
    scores = jnp.where(valid_keys[:, None, None, :], scores, -1e30)
    weights_soft = jnp.exp(scores - jnp.max(scores, axis=-1, keepdims=True))
    weights_soft = weights_soft / jnp.sum(weights_soft, axis=-1, keepdims=True)
    context = jnp.einsum("bhqk,bkhd->bqhd", weights_soft, values_all, precision=HIGH).reshape(
        entry_count * slot_count, width
    )
    context_low = context.astype(jnp.bfloat16)
    middle = hidden_rows + matmul(context_low, out_weight) + out_bias.astype(jnp.float32)
    normed_two, inverse_two = norm_parts(middle)
    normed_mid = (normed_two * gain_two.astype(jnp.float32) + shift_two.astype(jnp.float32)).astype(
        jnp.bfloat16
    )
    inner = matmul(normed_mid, inner_weight) + inner_bias.astype(jnp.float32)
    activated = jax.nn.gelu(inner, approximate=False).astype(jnp.bfloat16)
    result = middle + matmul(activated, outer_weight) + outer_bias.astype(jnp.float32)
    kept = (
        normed_one,
        inverse_one,
        normed_in,
        queries,
        keys_all,
        values_all,
        weights_soft,
        context_low,
        normed_two,
        inverse_two,
        normed_mid,
        inner,
        activated,
    )
    return (result, kept)


def hyper_backward(grad_rows, kept, weights):
    (
        gain_one,
        shift_one,
        qkv_weight,
        query_bias,
        value_bias,
        out_weight,
        out_bias,
        gain_two,
        shift_two,
        inner_weight,
        inner_bias,
        outer_weight,
        outer_bias,
    ) = weights
    (
        normed_one,
        inverse_one,
        normed_in,
        queries,
        keys_all,
        values_all,
        weights_soft,
        context_low,
        normed_two,
        inverse_two,
        normed_mid,
        inner,
        activated,
    ) = kept
    width = grad_rows.shape[1]
    grad_outer_bias = jnp.sum(grad_rows, axis=0)
    grad_rows_low = grad_rows.astype(jnp.bfloat16)
    grad_outer = matmul_left_t(activated, grad_rows_low)
    grad_active = matmul_right_t(grad_rows_low, outer_weight)
    slope = (
        0.5 * (1.0 + lax.erf(inner * SQRT_HALF))
        + inner * jnp.exp(-0.5 * inner * inner) * INV_SQRT_TAU
    )
    grad_inner = grad_active * slope
    grad_inner_bias = jnp.sum(grad_inner, axis=0)
    grad_inner_low = grad_inner.astype(jnp.bfloat16)
    grad_inner_weight = matmul_left_t(normed_mid, grad_inner_low)
    grad_normed_mid = matmul_right_t(grad_inner_low, inner_weight)
    grad_gain_two = jnp.sum(grad_normed_mid * normed_two, axis=0)
    grad_shift_two = jnp.sum(grad_normed_mid, axis=0)
    grad_middle = grad_rows + norm_back(
        normed_two, inverse_two, grad_normed_mid * gain_two.astype(jnp.float32)
    )
    grad_out_bias = jnp.sum(grad_middle, axis=0)
    grad_middle_low = grad_middle.astype(jnp.bfloat16)
    grad_out_weight = matmul_left_t(context_low, grad_middle_low)
    grad_context = matmul_right_t(grad_middle_low, out_weight).reshape(queries.shape)
    grad_soft = jnp.einsum("bqhd,bkhd->bhqk", grad_context, values_all, precision=HIGH)
    grad_scores = (
        weights_soft
        * (grad_soft - jnp.sum(weights_soft * grad_soft, axis=-1, keepdims=True))
        * HEAD_DIM ** (-0.5)
    )
    grad_values = jnp.einsum("bhqk,bqhd->bkhd", weights_soft, grad_context, precision=HIGH).reshape(
        -1, width
    )
    grad_queries = jnp.einsum("bhqk,bkhd->bqhd", grad_scores, keys_all, precision=HIGH).reshape(
        -1, width
    )
    grad_keys = jnp.einsum("bhqk,bqhd->bkhd", grad_scores, queries, precision=HIGH).reshape(
        -1, width
    )
    grad_query_bias = jnp.sum(grad_queries, axis=0)
    grad_value_bias = jnp.sum(grad_values, axis=0)
    grad_mixed_low = jnp.concatenate([grad_queries, grad_keys, grad_values], axis=1).astype(
        jnp.bfloat16
    )
    grad_qkv = matmul_left_t(normed_in, grad_mixed_low)
    grad_normed_in = matmul_right_t(grad_mixed_low, qkv_weight)
    grad_gain_one = jnp.sum(grad_normed_in * normed_one, axis=0)
    grad_shift_one = jnp.sum(grad_normed_in, axis=0)
    grad_below = grad_middle + norm_back(
        normed_one, inverse_one, grad_normed_in * gain_one.astype(jnp.float32)
    )
    return (
        grad_below,
        (
            grad_gain_one,
            grad_shift_one,
            grad_qkv,
            grad_query_bias,
            grad_value_bias,
            grad_out_weight,
            grad_out_bias,
            grad_gain_two,
            grad_shift_two,
            grad_inner_weight,
            grad_inner_bias,
            grad_outer,
            grad_outer_bias,
        ),
    )


VECTORS = 8


def pack_params(shards):
    (g1, b1, w_qkv, bq, bv, w_ao, bao, g2, b2, w_in, bin_, w_out, bout, fg, fb, w_proj) = shards
    layers, own, _ = w_qkv.shape
    width = w_ao.shape[2]
    pieces = []
    for layer in range(layers):
        pieces += [w_qkv[layer, :, i * width : (i + 1) * width] for i in range(3)]
        pieces += [w_ao[layer]]
        pieces += [w_in[layer, :, i * width : (i + 1) * width] for i in range(4)]
        pieces += [w_out[layer]]
    pieces += [w_proj[:, i * width : (i + 1) * width] for i in range(4)]
    small = jnp.concatenate(
        [jnp.stack([g1, b1, bq, bv, bao, g2, b2, bout]).reshape(-1), fg, fb, bin_.reshape(-1)]
    )
    small = jnp.pad(small, (0, 16 * width - small.shape[0])).reshape(16, width)
    return jnp.concatenate(pieces + [small], axis=0)


def unpack_params(gathered, own, layers):
    devices, _, width = gathered.shape
    at = [0]

    def take(rows):
        part = gathered[:, at[0] : at[0] + rows].reshape(devices * rows, width)
        at[0] += rows
        return part

    weights = []
    for layer in range(layers):
        qkv = [take(own) for _ in range(3)]
        attn_out = take(own)
        inner = [take(own) for _ in range(4)]
        outer = take(4 * own)
        weights.append((qkv, attn_out, inner, outer))
    proj = [take(own) for _ in range(4)]
    small = gathered[:, at[0] : at[0] + 16].reshape(devices, 16 * width)
    count = VECTORS * layers + 2
    vectors = small[:, : count * own].reshape(devices, count, own).transpose(1, 0, 2)
    vectors = vectors.reshape(count, devices * own)
    inner_bias = small[:, count * own : count * own + layers * 4 * own]
    inner_bias = inner_bias.reshape(devices, layers, 4 * own).transpose(1, 0, 2)
    return weights, proj, vectors, inner_bias.reshape(layers, -1)


def local(
    piece_table,
    piece_ids,
    piece_counts,
    text_ids,
    cotangent,
    rms_gain_one,
    w_query,
    w_key,
    w_value,
    w_output,
    rms_gain_two,
    w_gate,
    w_up,
    w_down,
    *shard_params,
):
    tensor_index = lax.axis_index("tensor")
    dp_index = lax.axis_index("dp")
    tensor_size = lax.axis_size("tensor")
    dp_size = lax.axis_size("dp")
    devices = tensor_size * dp_size
    chip = tensor_index // 2
    core = tensor_index % 2
    micro_count, group_entries, slot_count = piece_ids.shape
    own_entries = group_entries // tensor_size
    seq_length = text_ids.shape[1]
    share = cotangent.shape[1]
    layer_count, own, _ = shard_params[2].shape
    width = shard_params[5].shape[2]
    lm_width = cotangent.shape[2]
    table_rows, table_cols = piece_table.shape
    gain_first = rms_gain_one.astype(F32)
    gain_second = rms_gain_two.astype(F32)
    cosine, sine = rotary_tables(seq_length)
    positions = jnp.arange(seq_length)
    causal = positions[:, None] >= positions[None, :]
    scale = HEAD_DIM ** (-0.5)

    gathered = lax.all_gather(pack_params(shard_params), BOTH, axis=0)

    ids_all = gather_dp(piece_ids)
    ids_all = ids_all.reshape(dp_size, micro_count, tensor_size, own_entries, slot_count)
    ids_all = ids_all.transpose(0, 2, 1, 3, 4).reshape(-1) - dp_index * table_rows
    own_rows = micro_count * own_entries * slot_count
    looked = lookup(ids_all, piece_table).reshape(devices, own_rows, table_cols)
    looked = lax.all_to_all(looked, BOTH, split_axis=0, concat_axis=0, tiled=True)
    looked = jnp.sum(
        looked.reshape(dp_size, tensor_size, own_rows, table_cols).astype(F32), axis=0
    )
    hidden_rows = looked.transpose(1, 0, 2).reshape(own_rows, width)

    weights, proj, vectors, inner_bias = unpack_params(gathered, own, layer_count)
    layer_weights = []
    for layer in range(layer_count):
        qkv, attn_out, inner, outer = weights[layer]
        vec = [vectors[i * layer_count + layer] for i in range(VECTORS)]
        layer_weights.append(
            (
                vec[0],
                vec[1],
                jnp.concatenate(qkv, axis=1),
                vec[2],
                vec[3],
                attn_out,
                vec[4],
                vec[5],
                vec[6],
                jnp.concatenate(inner, axis=1),
                inner_bias[layer],
                outer,
                vec[7],
            )
        )
    final_gain = vectors[VECTORS * layer_count].astype(F32)
    final_bias = vectors[VECTORS * layer_count + 1].astype(F32)
    proj = jnp.concatenate(proj, axis=1)

    counts_own = lax.dynamic_slice_in_dim(piece_counts, tensor_index * own_entries, own_entries, 1)
    valid_keys = jnp.arange(slot_count)[None, :] < counts_own.reshape(-1)[:, None]
    saved = []
    for layer in range(layer_count):
        hidden_rows, kept = hyper_forward(hidden_rows, valid_keys, layer_weights[layer])
        saved.append(kept)
    pooled = hidden_rows.reshape(micro_count * own_entries, slot_count, width)[:, 0]
    normed_final, inverse_final = norm_parts(pooled)
    pooled_norm = (normed_final * final_gain + final_bias).astype(BF16)
    embeds = matmul(pooled_norm, proj).astype(BF16)
    own_pair, other_pair = gather_tensor(embeds, core)
    embeds_all = ordered_pair(own_pair, other_pair, chip)
    embeds_all = embeds_all.reshape(tensor_size, micro_count, own_entries, lm_width)

    chip_rows = 2 * share
    out_parts = []
    grad_embeds = []
    for micro in range(micro_count):
        embeds_group = embeds_all[:, micro].reshape(group_entries, lm_width)
        token_ids = text_ids[micro]
        onehot = token_ids[:, None] == jnp.arange(group_entries)[None, :]
        onehot_low = onehot.astype(BF16)
        onehot_share = lax.dynamic_slice_in_dim(onehot_low, tensor_index * share, share, 0)
        embeds_wide = embeds_group.astype(F32)
        inverse_first = rms_parts(embeds_wide)
        normed_first = (embeds_wide * inverse_first * gain_first).astype(BF16)
        mixed = jnp.concatenate(
            [matmul(normed_first, w_query), matmul(normed_first, w_key), matmul(normed_first, w_value)],
            axis=1,
        )
        mixed_high, mixed_low = split_two(mixed)
        mixed = matmul(onehot_low, mixed_high) + matmul(onehot_low, mixed_low)
        q_width = w_query.shape[1]
        k_width = w_key.shape[1]
        queries = rotate(
            mixed[:, :q_width].reshape(seq_length, -1, HEAD_DIM), cosine, sine
        ).astype(BF16)
        keys_rot = rotate(
            mixed[:, q_width : q_width + k_width].reshape(seq_length, -1, HEAD_DIM), cosine, sine
        ).astype(BF16)
        values_lm = mixed[:, q_width + k_width :].astype(BF16).reshape(seq_length, -1, HEAD_DIM)
        kv_local = keys_rot.shape[1]
        queries = queries.reshape(seq_length, kv_local, -1, HEAD_DIM)
        scores = (
            jnp.einsum("sjgd,tjd->jgst", queries, keys_rot, preferred_element_type=F32) * scale
        )
        scores = jnp.where(causal, scores, -1e30)
        row_max = jnp.max(scores, axis=-1, keepdims=True)
        expon = jnp.exp(scores - row_max)
        row_total = jnp.sum(expon, axis=-1, keepdims=True)
        log_total = row_max + jnp.log(row_total)
        soft_low = (expon / row_total).astype(BF16)
        context = (
            jnp.einsum("jgst,tjd->sjgd", soft_low, values_lm, preferred_element_type=F32)
            .astype(BF16)
            .reshape(2, chip_rows, -1)
        )

        def by_core(values):
            return values.astype(BF16).reshape(2, share, -1)

        def half(values, which):
            return lax.dynamic_index_in_dim(values, which, 0, keepdims=False)

        other_part = by_core(matmul(half(context, 1 - chip), w_output))
        own_part = by_core(matmul(half(context, chip), w_output))
        attn_share = scatter_tensor(own_part, other_part, core)
        tokens_share = matmul(onehot_share, embeds_group)
        hidden_share = tokens_share + attn_share
        inverse_second = rms_parts(hidden_share)
        normed_second = (hidden_share * inverse_second * gain_second).astype(BF16)
        grad_output = cotangent[micro]
        normed_halves = gather_tensor(normed_second, core)
        output_halves = gather_tensor(grad_output.astype(BF16), core)
        mlp_parts = []
        grad_parts = []
        for normed_half, grad_half in zip(normed_halves, output_halves):
            normed_half = normed_half.reshape(chip_rows, lm_width)
            grad_half = grad_half.reshape(chip_rows, lm_width)
            grad_active = matmul_right_t(grad_half, w_down)
            gate = matmul(normed_half, w_gate)
            upward = matmul(normed_half, w_up)
            sigmoid_gate = jax.nn.sigmoid(gate)
            silu_gate = gate * sigmoid_gate
            activated = (silu_gate * upward).astype(BF16)
            mlp_parts.append(by_core(matmul(activated, w_down)))
            slope_silu = sigmoid_gate * (1.0 + gate * (1.0 - sigmoid_gate))
            grad_gate = (grad_active * upward * slope_silu).astype(BF16)
            grad_upward = (grad_active * silu_gate).astype(BF16)
            grad_parts.append(
                by_core(matmul_right_t(grad_gate, w_gate) + matmul_right_t(grad_upward, w_up))
            )
        grad_normed_second = scatter_tensor(grad_parts[0], grad_parts[1], core)
        mlp_share = scatter_tensor(mlp_parts[0], mlp_parts[1], core)
        out_parts.append((hidden_share + mlp_share).astype(BF16))
        grad_hidden = grad_output + rms_back(
            hidden_share, inverse_second, grad_normed_second * gain_second
        )
        grad_hidden_low = grad_hidden.astype(BF16)
        attn_halves = gather_tensor(grad_hidden_low, core)
        context_halves = [
            matmul_right_t(part.reshape(chip_rows, lm_width), w_output).astype(BF16)
            for part in attn_halves
        ]
        grad_context = ordered_pair(context_halves[0], context_halves[1], chip)
        grad_context = grad_context.reshape(queries.shape)
        scores_again = (
            jnp.einsum("sjgd,tjd->jgst", queries, keys_rot, preferred_element_type=F32) * scale
        )
        soft_again = jnp.where(causal, jnp.exp(scores_again - log_total), 0.0)
        grad_soft = jnp.einsum(
            "sjgd,tjd->jgst", grad_context, values_lm, preferred_element_type=F32
        )
        grad_scores = (
            soft_again * (grad_soft - jnp.sum(soft_again * grad_soft, axis=-1, keepdims=True))
        ).astype(BF16)
        grad_values = jnp.einsum(
            "jgst,sjgd->tjd", soft_again.astype(BF16), grad_context, preferred_element_type=F32
        )
        grad_queries = (
            jnp.einsum("jgst,tjd->sjgd", grad_scores, keys_rot, preferred_element_type=F32) * scale
        )
        grad_keys = (
            jnp.einsum("jgst,sjgd->tjd", grad_scores, queries, preferred_element_type=F32) * scale
        )
        grad_queries = unrotate(grad_queries.reshape(seq_length, -1, HEAD_DIM), cosine, sine)
        grad_keys = unrotate(grad_keys, cosine, sine)
        grad_mixed = jnp.concatenate(
            [
                grad_queries.reshape(seq_length, -1).astype(BF16),
                grad_keys.reshape(seq_length, -1).astype(BF16),
                grad_values.reshape(seq_length, -1).astype(BF16),
            ],
            axis=1,
        )
        grad_mixed = jnp.concatenate(split_two(matmul_left_t(onehot_low, grad_mixed)), axis=0)
        grad_normed_first = (
            matmul_right_t(grad_mixed[:, :q_width], w_query)
            + matmul_right_t(grad_mixed[:, q_width : q_width + k_width], w_key)
            + matmul_right_t(grad_mixed[:, q_width + k_width :], w_value)
        )
        grad_normed_first = grad_normed_first[:group_entries] + grad_normed_first[group_entries:]
        grad_entries = rms_back(
            embeds_wide, inverse_first, grad_normed_first * gain_first
        ) + matmul_left_t(onehot_share, grad_hidden_low)
        grad_entries = grad_entries.astype(BF16).reshape(2, 2, own_entries, lm_width)
        grad_embeds.append(
            scatter_tensor(half(grad_entries, chip), half(grad_entries, 1 - chip), core).astype(BF16)
        )

    grad_embeds = jnp.concatenate(grad_embeds, axis=0)
    grad_projection = matmul_left_t(pooled_norm, grad_embeds)
    grad_pooled_norm = matmul_right_t(grad_embeds, proj)
    grad_gain_final = jnp.sum(grad_pooled_norm * normed_final, axis=0)
    grad_bias_final = jnp.sum(grad_pooled_norm, axis=0)
    grad_pooled = norm_back(normed_final, inverse_final, grad_pooled_norm * final_gain)
    grad_rows = jnp.concatenate(
        [
            grad_pooled[:, None, :],
            jnp.zeros((micro_count * own_entries, slot_count - 1, width), F32),
        ],
        axis=1,
    ).reshape(own_rows, width)
    layer_grads = [None] * layer_count
    for layer in range(layer_count - 1, -1, -1):
        grad_rows, layer_grads[layer] = hyper_backward(grad_rows, saved[layer], layer_weights[layer])

    pieces = grad_rows.astype(BF16).reshape(own_rows, tensor_size, table_cols).transpose(1, 0, 2)
    arrived = lax.all_to_all(pieces, "tensor", split_axis=0, concat_axis=0, tiled=True)
    arrived = gather_dp(arrived).reshape(-1, table_cols)
    table_grad = collect(ids_all, arrived, table_rows)

    def rows_of(values):
        return values.astype(BF16).reshape(devices, -1, values.shape[-1])

    pieces = []
    for layer in range(layer_count):
        grads = layer_grads[layer]
        pieces += [rows_of(grads[2][:, i * width : (i + 1) * width]) for i in range(3)]
        pieces += [rows_of(grads[5])]
        pieces += [rows_of(grads[9][:, i * width : (i + 1) * width]) for i in range(4)]
        pieces += [rows_of(grads[11])]
    pieces += [rows_of(grad_projection[:, i * width : (i + 1) * width]) for i in range(4)]
    small = [layer_grads[layer][i] for i in (0, 1, 3, 4, 6, 7, 8, 12) for layer in range(layer_count)]
    small = jnp.stack(small + [grad_gain_final, grad_bias_final])
    small = small.reshape(-1, devices, own).transpose(1, 0, 2).reshape(devices, -1)
    inner_small = jnp.stack([layer_grads[layer][10] for layer in range(layer_count)])
    inner_small = inner_small.reshape(layer_count, devices, -1).transpose(1, 0, 2)
    small = jnp.concatenate([small, inner_small.reshape(devices, -1)], axis=1).astype(BF16)
    small = jnp.pad(small, ((0, 0), (0, 16 * width - small.shape[1])))
    pieces += [small.reshape(devices, 16, width)]
    reduced = lax.psum_scatter(
        jnp.concatenate(pieces, axis=1), BOTH, scatter_dimension=0, tiled=True
    )[0]
    reduced = reduced.astype(F32)
    at = 0
    outs = {"qkv": [], "attn_out": [], "inner": [], "outer": []}
    for layer in range(layer_count):
        for name, count, rows in (("qkv", 3, own), ("attn_out", 1, own), ("inner", 4, own), ("outer", 1, 4 * own)):
            outs[name].append(
                jnp.concatenate([reduced[at + i * rows : at + (i + 1) * rows] for i in range(count)], axis=1)
            )
            at += count * rows
    out_proj = jnp.concatenate([reduced[at + i * own : at + (i + 1) * own] for i in range(4)], axis=1)
    at += 4 * own
    small = reduced[at : at + 16].reshape(-1)
    count = VECTORS * layer_count
    vec = small[: count * own].reshape(VECTORS, layer_count, own)
    out_final_gain = small[count * own : (count + 1) * own]
    out_final_bias = small[(count + 1) * own : (count + 2) * own]
    out_inner_bias = small[(count + 2) * own : (count + 2 + 4 * layer_count) * own].reshape(layer_count, 4 * own)
    stacked = {name: jnp.stack(value) for name, value in outs.items()}
    return (
        jnp.stack(out_parts),
        table_grad,
        vec[0],
        vec[1],
        stacked["qkv"],
        vec[2],
        vec[3],
        stacked["attn_out"],
        vec[4],
        vec[5],
        vec[6],
        stacked["inner"],
        out_inner_bias,
        stacked["outer"],
        vec[7],
        out_final_gain,
        out_final_bias,
        out_proj,
    )


def solution(mesh):
    return jax.shard_map(
        local,
        mesh=mesh,
        in_specs=(
            P("dp", "tensor"),
            P(None, "dp", None),
            P(None, "dp"),
            P(None, "dp"),
            P(None, ("dp", "tensor"), None),
            P(),
            P(None, "tensor"),
            P(None, "tensor"),
            P(None, "tensor"),
            P("tensor", None),
            P(),
            P(None, "tensor"),
            P(None, "tensor"),
            P("tensor", None),
            P(None, ("dp", "tensor")),
            P(None, ("dp", "tensor")),
            P(None, ("dp", "tensor"), None),
            P(None, ("dp", "tensor")),
            P(None, ("dp", "tensor")),
            P(None, ("dp", "tensor"), None),
            P(None, ("dp", "tensor")),
            P(None, ("dp", "tensor")),
            P(None, ("dp", "tensor")),
            P(None, ("dp", "tensor"), None),
            P(None, ("dp", "tensor")),
            P(None, ("dp", "tensor"), None),
            P(None, ("dp", "tensor")),
            P(("dp", "tensor")),
            P(("dp", "tensor")),
            P(("dp", "tensor"), None),
        ),
        out_specs=(
            P(None, ("dp", "tensor"), None),
            P("dp", "tensor"),
            P(None, ("dp", "tensor")),
            P(None, ("dp", "tensor")),
            P(None, ("dp", "tensor"), None),
            P(None, ("dp", "tensor")),
            P(None, ("dp", "tensor")),
            P(None, ("dp", "tensor"), None),
            P(None, ("dp", "tensor")),
            P(None, ("dp", "tensor")),
            P(None, ("dp", "tensor")),
            P(None, ("dp", "tensor"), None),
            P(None, ("dp", "tensor")),
            P(None, ("dp", "tensor"), None),
            P(None, ("dp", "tensor")),
            P(("dp", "tensor")),
            P(("dp", "tensor")),
            P(("dp", "tensor"), None),
        ),
        check_vma=False,
    )
```

time: 3740 us -> 1320 us (0.35)
  waiting for transfers between devices: 2300 us -> 375 us
  blocking collectives: 436 us -> 15 us
  matrix products: 596 us -> 460 us
  Pallas kernels: 0 us -> 43.4 us
    reduce_scatter x14 -> x1, waiting for transfers between devices: 1140 us -> 47.8 us  [local(): lax.psum_scatter(jnp.concatenate(pieces, axis=1), BOTH, scatter_dimension...]
    unnamed x44 -> x2, waiting for transfers between devices: 1030 us -> 0.03 us
    all_gather x11 -> x0, blocking collectives: 350 us -> none  [the longest x1 39.3 us: fetch_params(): lax.all_gather(bias_attn_out, ('dp', 'tensor'), axis=1, tiled=True)]
    ppermute x0 -> x51, waiting for transfers between devices: none -> 234 us  [swap(): return lax.ppermute(values, axis, [(i, i ^ bit) for i in range(size)])]
    all_gather x12 -> x1, waiting for transfers between devices: 124 us -> 20.5 us  [local(): gathered = lax.all_gather(pack_params(shard_params), BOTH, axis=0)]
    unnamed x2 -> x0, blocking collectives: 85.9 us -> none
    dot_general x32 -> x31, matrix products: 194 us -> 117 us  [matmul_right_t(): lax.dot_general(left, right, (((1,), (1,)), ((), ())), preferred_element_...]
    all_to_all x4 -> x1, waiting for transfers between devices: 5.29 us -> 71.9 us  [local(): lax.all_to_all(looked, BOTH, split_axis=0, concat_axis=0, tiled=True)]
  transfers between devices with their start and end apart: 39 -> 54, of which waited for: 27 -> 25; matrix products, arithmetic and copies ran while one was open for 13% -> 37% of each run, Pallas kernels for 0% -> 3%
where the time goes in v1:
time: 1320 us; the launch traced here: 1310 us
  matrix products  460 us (35%)
  waiting for transfers between devices  375 us (28%)
  local copies, waits for them, and re-layouts  193 us (15%)
  other arithmetic  167 us (13%)
  Pallas kernels  43.4 us (3%)
  starting transfers between devices  39.2 us (3%)
  between operations  18.4 us (1%)
  blocking collectives  15 us (1%)
    ppermute x51, waiting for transfers between devices, swap(): return lax.ppermute(values, axis, [(i, i ^ bit) for i in range(size)])  234 us
    dot_general x31, matrix products, matmul_right_t(): lax.dot_general(left, right, (((1,), (1,)), ((), ())), preferred_element_...  117 us
    dot_general x37, matrix products, matmul(): return jnp.dot(left, right, preferred_element_type=F32)  94.6 us
    all_to_all x1, waiting for transfers between devices, local(): lax.all_to_all(looked, BOTH, split_axis=0, concat_axis=0, tiled=True)  71.9 us
    unnamed x620, local copies, waits for them, and re-layouts  68.1 us
    dot_general x2, matrix products, local(): jnp.einsum('sjgd,tjd->jgst', grad_context, values_lm, preferred_element_t...  60.1 us
    another operation x1, other arithmetic  55.3 us
    reduce_scatter x1, waiting for transfers between devices, local(): lax.psum_scatter(jnp.concatenate(pieces, axis=1), BOTH, scatter_dimension...  47.8 us
  transfers between devices with their start and end apart: 54, of which 25 were waited for; matrix products, arithmetic and copies ran while one was open for 37% of the time, Pallas kernels for 3%

profile of v1, /device:TPU:0, one launch (start us, length us, event | category | flops | bytes accessed | tf_op | source)
XLA Modules:
  0.0 1310.4 jit_solution(10779361577244257588)
XLA Ops:
  51.1 21.8 %lookup.1 = bf16[8192,128]{1,0:T(8,128)(2,1)S(1)} custom-call(s32[8192,1]{1,0:T(8,128)} %sub.364.ids_ref, bf16[4096,128]{1,0:T(8,128)(2,1)S(1)} %copy-done.2), custom_call_target="tpu_custom_call" | custom-call | flops 8589934592 | bytes 4194304 | tf_op jit(solution)/shard_map/lookup/pallas_call | solution.py:137
  89.0 71.9 %all-to-all-done = bf16[32,256,128]{2,1,0:T(8,128)(2,1)} async-done(((bf16[32,256,128]{2,1,0:T(8,128)(2,1)}), bf16[32,256,128]{2,1,0:T(8,128)(2,1)}, u32[]{:S(2)}, u32[]{:S(2)}) %all-to-all-start) | async-done | bytes 2097184 | tf_op jit(solution)/shard_map/all_to_all | solution.py:443
  165.3 20.5 %all-gather.3.cloned.1.call-done = bf16[14848,512]{1,0:T(8,128)(2,1)} async-done(((bf16[464,512]{1,0:T(8,128)(2,1)}), bf16[14848,512]{1,0:T(8,128)(2,1)}) %all-gather.3.cloned.1.call-update) | async-done | bytes 15204368 | tf_op jit(solution)/shard_map/all_gather | solution.py:436
  314.3 14.2 %fusion.12 = f32[8,1024]{1,0:T(8,128)S(1)} fusion(f32[1024,1024,8]{1,0,2:T(8,128)} %get-tuple-element.290, f32[8,1024]{1,0:T(8,128)S(1)} %get-tuple-element.289, pred[1024,1024]{0,1:T(8,128)(4,1)S(1)} %iota_compare_fusion), kind=kLoop, calls=%fused_computation.24 | loop fusion | flops 33546240 | bytes 34668544 | tf_op jit(solution)/shard_map/reduce_sum | solution.py:524
  328.5 15.6 %fusion.113 = bf16[1024,1,8,64]{0,3,2,1:T(8,128)(2,1)} fusion(f32[8,1024]{1,0:T(8,128)S(1)} %fusion.12, f32[8,1024]{1,0:T(8,128)S(1)} %get-tuple-element.289, f32[1024,1024,8]{1,0,2:T(8,128)} %get-tuple-element.290, pred[1024,1024]{0,1:T(8,128)(4,1)S(1)} %iota_compare_fusion, f32[1024,640]{0,1:T(8,128)S(1)} %convolution_add_fusion.9), kind=kOutput, calls=%fused_computation.247 | convolution fusion | flops 1116209152 | bytes 35848192 | tf_op jit(solution)/shard_map/jgst,tjd->sjgd/dot_general | solution.py:528
  376.7 14.6 %collective-permute-done.8 = bf16[256,2048]{1,0:T(8,128)(2,1)S(1)} collective-permute-done((bf16[256,2048]{1,0:T(8,128)(2,1)S(1)}, bf16[256,2048]{1,0:T(8,128)(2,1)S(1)}, u32[]{:S(2)}, u32[]{:S(2)}) %collective-permute-start.8) | collective-permute-done | bytes 1048608 | tf_op jit(solution)/shard_map/ppermute | solution.py:82
  476.9 22.5 %collective-permute-done.29 = bf16[256,2048]{1,0:T(8,128)(2,1)S(1)} collective-permute-done((bf16[256,2048]{1,0:T(8,128)(2,1)S(1)}, bf16[256,2048]{1,0:T(8,128)(2,1)S(1)}, u32[]{:S(2)}, u32[]{:S(2)}) %collective-permute-start.29) | collective-permute-done | bytes 1048608 | tf_op jit(solution)/shard_map/ppermute | solution.py:82
  500.0 20.9 %collective-permute-done.14 = bf16[256,2048]{1,0:T(8,128)(2,1)S(1)} collective-permute-done((bf16[256,2048]{1,0:T(8,128)(2,1)S(1)}, bf16[256,2048]{1,0:T(8,128)(2,1)S(1)}, u32[]{:S(2)}, u32[]{:S(2)}) %collective-permute-start.14) | collective-permute-done | bytes 1048608 | tf_op jit(solution)/shard_map/ppermute | solution.py:82
  559.9 36.9 %fusion.5 = (f32[8,1024]{1,0:T(8,128)}, f32[8,1024]{1,0:T(8,128)S(1)}, f32[1024,1024,8]{1,0,2:T(8,128)}) fusion(f32[1024,1024,8]{1,0,2:T(8,128)} %get-tuple-element.290, f32[8,1024]{1,0:T(8,128)S(1)} %log_add_fusion.1, pred[1024,1024]{0,1:T(8,128)(4,1)S(1)} %copy-done.4, f32[1024,1024,8]{1,0,2:T(8,128)} %fusion.420, bf16[1024,8,64]{0,2,1:T(8,128)(2,1)} %reshape.1503, ...), kind=kOutput, calls=%fused_computation.11 | convolution fusion | flops 1140834304 | bytes 102989824 | tf_op jit(solution)/shard_map/sjgd,tjd->jgst/dot_general | solution.py:585
  596.8 14.2 %fusion.13 = f32[8,1024]{1,0:T(8,128)S(1)} fusion(f32[1024,1024,8]{1,0,2:T(8,128)} %fusion.420, f32[8,1024]{1,0:T(8,128)S(1)} %get-tuple-element.27, pred[1024,1024]{0,1:T(8,128)(4,1)S(1)} %copy-done.4), kind=kLoop, calls=%fused_computation.25 | loop fusion | flops 33546240 | bytes 34668544 | tf_op jit(solution)/shard_map/reduce_sum | solution.py:524
  611.0 16.5 %fusion.110 = bf16[1024,1,8,64]{0,3,2,1:T(8,128)(2,1)} fusion(f32[8,1024]{1,0:T(8,128)S(1)} %fusion.13, f32[8,1024]{1,0:T(8,128)S(1)} %get-tuple-element.27, f32[1024,1024,8]{1,0,2:T(8,128)} %fusion.420, pred[1024,1024]{0,1:T(8,128)(4,1)S(1)} %copy-done.4, f32[1024,640]{0,1:T(8,128)} %copy-done.9), kind=kOutput, calls=%fused_computation.246 | convolution fusion | flops 1116209152 | bytes 35848192 | tf_op jit(solution)/shard_map/jgst,tjd->sjgd/dot_general | solution.py:528
  664.5 15.8 %collective-permute-done.17 = bf16[256,2048]{1,0:T(8,128)(2,1)S(1)} collective-permute-done((bf16[256,2048]{1,0:T(8,128)(2,1)S(1)}, bf16[256,2048]{1,0:T(8,128)(2,1)S(1)}, u32[]{:S(2)}, u32[]{:S(2)}) %collective-permute-start.17) | collective-permute-done | bytes 1048608 | tf_op jit(solution)/shard_map/ppermute | solution.py:82
  766.1 20.7 %collective-permute-done.41 = bf16[256,2048]{1,0:T(8,128)(2,1)} collective-permute-done((bf16[256,2048]{1,0:T(8,128)(2,1)}, bf16[256,2048]{1,0:T(8,128)(2,1)}, u32[]{:S(2)}, u32[]{:S(2)}) %collective-permute-start.41) | collective-permute-done | bytes 1048608 | tf_op jit(solution)/shard_map/ppermute | solution.py:82
  790.0 18.5 %collective-permute-done.23 = bf16[256,2048]{1,0:T(8,128)(2,1)} collective-permute-done((bf16[256,2048]{1,0:T(8,128)(2,1)}, bf16[256,2048]{1,0:T(8,128)(2,1)}, u32[]{:S(2)}, u32[]{:S(2)}) %collective-permute-start.23) | collective-permute-done | bytes 1048608 | tf_op jit(solution)/shard_map/ppermute | solution.py:82
  815.7 15.2 %fusion.156 = bf16[1024,64]{0,1:T(8,128)(2,1)} fusion(bf16[1024,8,64]{0,2,1:T(8,128)(2,1)} %reshape.1503, f32[1024,1024,8]{1,0,2:T(8,128)} %get-tuple-element.290, f32[8,1024]{1,0:T(8,128)S(1)} %copy-done.100, pred[1024,1024]{0,1:T(8,128)(4,1)S(1)} %copy-done.4), kind=kOutput, calls=%fused_computation.294 | convolution fusion | flops 1107361792 | bytes 35815424 | tf_op jit(solution)/shard_map/jgst,sjgd->tjd/dot_general | solution.py:591
  852.9 14.9 %fusion.153 = bf16[1024,64]{0,1:T(8,128)(2,1)} fusion(bf16[1024,8,64]{0,2,1:T(8,128)(2,1)} %reshape.1515, f32[1024,1024,8]{1,0,2:T(8,128)} %fusion.420, f32[8,1024]{1,0:T(8,128)S(1)} %log_add_fusion, pred[1024,1024]{0,1:T(8,128)(4,1)S(1)} %copy-done.4), kind=kOutput, calls=%fused_computation.293 | convolution fusion | flops 1107361792 | bytes 35815424 | tf_op jit(solution)/shard_map/jgst,sjgd->tjd/dot_general | solution.py:591
  867.7 23.2 %fusion = (f32[8,1024]{1,0:T(8,128)S(1)}, f32[1024,1024,8]{1,0,2:T(8,128)}) fusion(f32[1024,1024,8]{1,0,2:T(8,128)} %fusion.420, f32[8,1024]{1,0:T(8,128)S(1)} %log_add_fusion, pred[1024,1024]{0,1:T(8,128)(4,1)S(1)} %copy-done.4, bf16[1024,8,64]{0,2,1:T(8,128)(2,1)} %reshape.1515, f32[1024,640]{0,1:T(8,128)} %copy-done.9), kind=kOutput, calls=%fused_computation.2 | convolution fusion | flops 1115676672 | bytes 69402624 | tf_op jit(solution)/shard_map/sjgd,tjd->jgst/dot_general | solution.py:585
  890.9 55.3 %fusion.19 = (bf16[8,1024,1024]{1,2,0:T(8,128)(2,1)}, bf16[8,1024,1024]{1,2,0:T(8,128)(2,1)}) fusion(f32[1024,1024,8]{1,0,2:T(8,128)} %get-tuple-element.293, f32[1024,1024,8]{1,0,2:T(8,128)} %fusion.420, f32[8,1024]{1,0:T(8,128)S(1)} %get-tuple-element.292, f32[8,1024]{1,0:T(8,128)S(1)} %log_add_fusion, pred[1024,1024]{0,1:T(8,128)(4,1)S(1)} %copy-done.4, ...), kind=kLoop, calls=%fused_computation.31 | loop fusion | flops 100663296 | bytes 168951808 | tf_op jit(solution)/shard_map/reshape.84
  1125.9 15.0 %all_to_all.10 = bf16[4,256,128]{2,1,0:T(8,128)(2,1)S(1)} all-to-all(bf16[4,256,128]{2,1,0:T(8,128)(2,1)S(1)} %bitcast_bitcast_fusion), channel_id=1, replica_groups=mesh['dp'=8,'tensor'=4] {'tensor'}, dimensions={0} | all-to-all | bytes 524288 | tf_op jit(solution)/shard_map/all_to_all | solution.py:643
  1143.0 14.7 %collective-permute-done.48 = bf16[1,1,1,4,256,128]{5,4,3,2,1,0:T(8,128)(2,1)S(1)} collective-permute-done((bf16[1,1,1,4,256,128]{5,4,3,2,1,0:T(8,128)(2,1)S(1)}, bf16[1,1,1,4,256,128]{5,4,3,2,1,0:T(8,128)(2,1)S(1)}, u32[]{:S(2)}, u32[]{:S(2)}) %collective-permute-start.48) | collective-permute-done | bytes 262176 | tf_op jit(solution)/shard_map/ppermute | solution.py:82
  1160.8 17.0 %collective-permute-done.49 = bf16[2,1,1,4,256,128]{5,4,3,2,1,0:T(8,128)(2,1)S(1)} collective-permute-done((bf16[2,1,1,4,256,128]{5,4,3,2,1,0:T(8,128)(2,1)S(1)}, bf16[2,1,1,4,256,128]{5,4,3,2,1,0:T(8,128)(2,1)S(1)}, u32[]{:S(2)}, u32[]{:S(2)}) %collective-permute-start.49) | collective-permute-done | bytes 524320 | tf_op jit(solution)/shard_map/ppermute | solution.py:82
  1182.5 42.9 %collective-permute-done.50 = bf16[2,2,1,4,256,128]{5,4,3,2,1,0:T(8,128)(2,1)} collective-permute-done((bf16[2,2,1,4,256,128]{5,4,3,2,1,0:T(8,128)(2,1)}, bf16[2,2,1,4,256,128]{5,4,3,2,1,0:T(8,128)(2,1)}, u32[]{:S(2)}, u32[]{:S(2)}) %collective-permute-start.50) | collective-permute-done | bytes 1048608 | tf_op jit(solution)/shard_map/ppermute | solution.py:82
  1227.0 21.7 %collect.1 = f32[4096,128]{1,0:T(8,128)} custom-call(s32[1,8192]{1,0:T(1,128)S(1)} %sub.322.ids_ref, bf16[8192,128]{1,0:T(8,128)(2,1)S(1)} %bitcast.921), custom_call_target="tpu_custom_call" | custom-call | flops 8589934592 | bytes 4194304 | tf_op jit(solution)/shard_map/collect/pallas_call | solution.py:168
  1248.7 47.8 %reduce-scatter.2.cloned.1.call-done = bf16[1,464,512]{2,1,0:T(8,128)(2,1)} async-done(((bf16[32,464,512]{2,1,0:T(8,128)(2,1)}), bf16[1,464,512]{2,1,0:T(8,128)(2,1)}) %reduce-scatter.2.cloned.1.call-update) | async-done | bytes 475152 | tf_op jit(solution)/shard_map/reduce_scatter | solution.py:666
  (1130 shorter events, 699.7 us)
Async XLA Ops:
  7.2 178.6 %all-gather.3.cloned.1.call-start = ((), (), s32[]{:S(2)}) async-start(), calls=%async_computation.4 | async-start | bytes 15679488 | tf_op jit(solution)/shard_map/all_gather | solution.py:436
  74.1 86.8 %all-to-all-start = ((bf16[32,256,128]{2,1,0:T(8,128)(2,1)}), bf16[32,256,128]{2,1,0:T(8,128)(2,1)}, u32[]{:S(2)}, u32[]{:S(2)}) async-start(bf16[32,256,128]{2,1,0:T(8,128)(2,1)} %bitcast.920), calls=%async_computation | async-start | bytes 4194304 | tf_op jit(solution)/shard_map/all_to_all | solution.py:443
  80.6 1215.9 %reduce-scatter.2.cloned.1.call-start = ((), (), s32[]{:S(2)}) async-start(), calls=%async_computation.3 | async-start | bytes 15679488 | tf_op jit(solution)/shard_map/reduce_scatter | solution.py:666
  84.5 189.7 %collective-permute-start.26 = (bf16[256,2048]{1,0:T(8,128)(2,1)}, bf16[256,2048]{1,0:T(8,128)(2,1)}, u32[]{:S(2)}, u32[]{:S(2)}) collective-permute-start(bf16[256,2048]{1,0:T(8,128)(2,1)} %get-tuple-element.78), channel_id=1, source_target_pairs={{0,2},{1,3},{2,0},{3,1},{4,6},{5,7},{6,4},{7,5},{8,10},{9,11},{10,... | collective-permute-start | bytes 3145736 | tf_op jit(solution)/shard_map/ppermute | solution.py:82
  86.2 268.6 %collective-permute-start.24 = (bf16[256,2048]{1,0:T(8,128)(2,1)}, bf16[256,2048]{1,0:T(8,128)(2,1)}, u32[]{:S(2)}, u32[]{:S(2)}) collective-permute-start(bf16[256,2048]{1,0:T(8,128)(2,1)} %get-tuple-element.78), channel_id=1, source_target_pairs={{0,1},{1,0},{2,3},{3,2},{4,5},{5,4},{6,7},{7,6},{8,9},{9,8},{10,11... | collective-permute-start | bytes 3145736 | tf_op jit(solution)/shard_map/ppermute | solution.py:82
  86.2 390.1 %collective-permute-start.38 = (bf16[256,2048]{1,0:T(8,128)(2,1)}, bf16[256,2048]{1,0:T(8,128)(2,1)}, u32[]{:S(2)}, u32[]{:S(2)}) collective-permute-start(bf16[256,2048]{1,0:T(8,128)(2,1)} %get-tuple-element.77), channel_id=1, source_target_pairs={{0,2},{1,3},{2,0},{3,1},{4,6},{5,7},{6,4},{7,5},{8,10},{9,11},{10,... | collective-permute-start | bytes 3145736 | tf_op jit(solution)/shard_map/ppermute | solution.py:82
  274.2 98.5 %collective-permute-start.27 = (bf16[256,2048]{1,0:T(8,128)(2,1)}, bf16[256,2048]{1,0:T(8,128)(2,1)}, u32[]{:S(2)}, u32[]{:S(2)}) collective-permute-start(bf16[256,2048]{1,0:T(8,128)(2,1)} %collective-permute-done.26), channel_id=1, source_target_pairs={{0,1},{1,0},{2,3},{3,2},{4,5},{5,4},{6,7},{7,6},{8,9},{9,8},{10,11... | collective-permute-start | bytes 3145736 | tf_op jit(solution)/shard_map/ppermute | solution.py:82
  366.0 25.3 %collective-permute-start.8 = (bf16[256,2048]{1,0:T(8,128)(2,1)S(1)}, bf16[256,2048]{1,0:T(8,128)(2,1)S(1)}, u32[]{:S(2)}, u32[]{:S(2)}) collective-permute-start(bf16[256,2048]{1,0:T(8,128)(2,1)S(1)} %fusion.75), channel_id=1, source_target_pairs={{0,2},{1,3},{2,0},{3,1},{4,6},{5,7},{6,4},{7,5},{8,10},{9,11},{10,... | collective-permute-start | bytes 3145736 | tf_op jit(solution)/shard_map/ppermute | solution.py:82
  400.5 25.4 %collective-permute-start.11 = (bf16[256,2048]{1,0:T(8,128)(2,1)S(1)}, bf16[256,2048]{1,0:T(8,128)(2,1)S(1)}, u32[]{:S(2)}, u32[]{:S(2)}) collective-permute-start(bf16[256,2048]{1,0:T(8,128)(2,1)S(1)} %multiply_convert_fusion.13), channel_id=1, source_target_pairs={{0,2},{1,3},{2,0},{3,1},{4,6},{5,7},{6,4},{7,5},{8,10},{9,11},{10,... | collective-permute-start | bytes 3145736 | tf_op jit(solution)/shard_map/ppermute | solution.py:82
  445.6 28.8 %collective-permute-start.13 = (bf16[256,2048]{1,0:T(8,128)(2,1)S(1)}, bf16[256,2048]{1,0:T(8,128)(2,1)S(1)}, u32[]{:S(2)}, u32[]{:S(2)}) collective-permute-start(bf16[256,2048]{1,0:T(8,128)(2,1)S(1)} %dynamic-slice_bitcast_fusion.8), channel_id=1, source_target_pairs={{0,1},{1,0},{2,3},{3,2},{4,5},{5,4},{6,7},{7,6},{8,9},{9,8},{10,11... | collective-permute-start | bytes 3145736 | tf_op jit(solution)/shard_map/ppermute | solution.py:82
  473.3 26.1 %collective-permute-start.29 = (bf16[256,2048]{1,0:T(8,128)(2,1)S(1)}, bf16[256,2048]{1,0:T(8,128)(2,1)S(1)}, u32[]{:S(2)}, u32[]{:S(2)}) collective-permute-start(bf16[256,2048]{1,0:T(8,128)(2,1)S(1)} %fusion.61), channel_id=1, source_target_pairs={{0,2},{1,3},{2,0},{3,1},{4,6},{5,7},{6,4},{7,5},{8,10},{9,11},{10,... | collective-permute-start | bytes 3145736 | tf_op jit(solution)/shard_map/ppermute | solution.py:82
  474.3 25.7 %collective-permute-start.10 = (bf16[256,2048]{1,0:T(8,128)(2,1)S(1)}, bf16[256,2048]{1,0:T(8,128)(2,1)S(1)}, u32[]{:S(2)}, u32[]{:S(2)}) collective-permute-start(bf16[256,2048]{1,0:T(8,128)(2,1)S(1)} %dynamic-slice_bitcast_fusion.9), channel_id=1, source_target_pairs={{0,1},{1,0},{2,3},{3,2},{4,5},{5,4},{6,7},{7,6},{8,9},{9,8},{10,11... | collective-permute-start | bytes 3145736 | tf_op jit(solution)/shard_map/ppermute | solution.py:82
  474.8 46.1 %collective-permute-start.14 = (bf16[256,2048]{1,0:T(8,128)(2,1)S(1)}, bf16[256,2048]{1,0:T(8,128)(2,1)S(1)}, u32[]{:S(2)}, u32[]{:S(2)}) collective-permute-start(bf16[256,2048]{1,0:T(8,128)(2,1)S(1)} %fusion.71), channel_id=1, source_target_pairs={{0,2},{1,3},{2,0},{3,1},{4,6},{5,7},{6,4},{7,5},{8,10},{9,11},{10,... | collective-permute-start | bytes 3145736 | tf_op jit(solution)/shard_map/ppermute | solution.py:82
  476.3 166.5 %collective-permute-start.36 = (bf16[256,2048]{1,0:T(8,128)(2,1)}, bf16[256,2048]{1,0:T(8,128)(2,1)}, u32[]{:S(2)}, u32[]{:S(2)}) collective-permute-start(bf16[256,2048]{1,0:T(8,128)(2,1)} %get-tuple-element.77), channel_id=1, source_target_pairs={{0,1},{1,0},{2,3},{3,2},{4,5},{5,4},{6,7},{7,6},{8,9},{9,8},{10,11... | collective-permute-start | bytes 3145736 | tf_op jit(solution)/shard_map/ppermute | solution.py:82
  476.6 185.6 %collective-permute-start.39 = (bf16[256,2048]{1,0:T(8,128)(2,1)}, bf16[256,2048]{1,0:T(8,128)(2,1)}, u32[]{:S(2)}, u32[]{:S(2)}) collective-permute-start(bf16[256,2048]{1,0:T(8,128)(2,1)} %collective-permute-done.38), channel_id=1, source_target_pairs={{0,1},{1,0},{2,3},{3,2},{4,5},{5,4},{6,7},{7,6},{8,9},{9,8},{10,11... | collective-permute-start | bytes 3145736 | tf_op jit(solution)/shard_map/ppermute | solution.py:82
  524.0 24.2 %collective-permute-start.31 = (bf16[256,2048]{1,0:T(8,128)(2,1)S(1)}, bf16[256,2048]{1,0:T(8,128)(2,1)S(1)}, u32[]{:S(2)}, u32[]{:S(2)}) collective-permute-start(bf16[256,2048]{1,0:T(8,128)(2,1)S(1)} %get-tuple-element.108), channel_id=1, source_target_pairs={{0,2},{1,3},{2,0},{3,1},{4,6},{5,7},{6,4},{7,5},{8,10},{9,11},{10,... | collective-permute-start | bytes 3145736 | tf_op jit(solution)/shard_map/ppermute | solution.py:82
  655.0 25.3 %collective-permute-start.17 = (bf16[256,2048]{1,0:T(8,128)(2,1)S(1)}, bf16[256,2048]{1,0:T(8,128)(2,1)S(1)}, u32[]{:S(2)}, u32[]{:S(2)}) collective-permute-start(bf16[256,2048]{1,0:T(8,128)(2,1)S(1)} %fusion.68), channel_id=1, source_target_pairs={{0,2},{1,3},{2,0},{3,1},{4,6},{5,7},{6,4},{7,5},{8,10},{9,11},{10,... | collective-permute-start | bytes 3145736 | tf_op jit(solution)/shard_map/ppermute | solution.py:82
  686.7 25.6 %collective-permute-start.20 = (bf16[256,2048]{1,0:T(8,128)(2,1)S(1)}, bf16[256,2048]{1,0:T(8,128)(2,1)S(1)}, u32[]{:S(2)}, u32[]{:S(2)}) collective-permute-start(bf16[256,2048]{1,0:T(8,128)(2,1)S(1)} %multiply_convert_fusion.12), channel_id=1, source_target_pairs={{0,2},{1,3},{2,0},{3,1},{4,6},{5,7},{6,4},{7,5},{8,10},{9,11},{10,... | collective-permute-start | bytes 3145736 | tf_op jit(solution)/shard_map/ppermute | solution.py:82
  731.8 30.7 %collective-permute-start.22 = (bf16[256,2048]{1,0:T(8,128)(2,1)S(1)}, bf16[256,2048]{1,0:T(8,128)(2,1)S(1)}, u32[]{:S(2)}, u32[]{:S(2)}) collective-permute-start(bf16[256,2048]{1,0:T(8,128)(2,1)S(1)} %dynamic-slice_bitcast_fusion.4), channel_id=1, source_target_pairs={{0,1},{1,0},{2,3},{3,2},{4,5},{5,4},{6,7},{7,6},{8,9},{9,8},{10,11... | collective-permute-start | bytes 3145736 | tf_op jit(solution)/shard_map/ppermute | solution.py:82
  760.5 26.3 %collective-permute-start.41 = (bf16[256,2048]{1,0:T(8,128)(2,1)}, bf16[256,2048]{1,0:T(8,128)(2,1)}, u32[]{:S(2)}, u32[]{:S(2)}) collective-permute-start(bf16[256,2048]{1,0:T(8,128)(2,1)} %fusion.58), channel_id=1, source_target_pairs={{0,2},{1,3},{2,0},{3,1},{4,6},{5,7},{6,4},{7,5},{8,10},{9,11},{10,... | collective-permute-start | bytes 3145736 | tf_op jit(solution)/shard_map/ppermute | solution.py:82
  762.5 27.5 %collective-permute-start.19 = (bf16[256,2048]{1,0:T(8,128)(2,1)}, bf16[256,2048]{1,0:T(8,128)(2,1)}, u32[]{:S(2)}, u32[]{:S(2)}) collective-permute-start(bf16[256,2048]{1,0:T(8,128)(2,1)} %dynamic-slice_bitcast_fusion.5), channel_id=1, source_target_pairs={{0,1},{1,0},{2,3},{3,2},{4,5},{5,4},{6,7},{7,6},{8,9},{9,8},{10,11... | collective-permute-start | bytes 3145736 | tf_op jit(solution)/shard_map/ppermute | solution.py:82
  763.9 44.6 %collective-permute-start.23 = (bf16[256,2048]{1,0:T(8,128)(2,1)}, bf16[256,2048]{1,0:T(8,128)(2,1)}, u32[]{:S(2)}, u32[]{:S(2)}) collective-permute-start(bf16[256,2048]{1,0:T(8,128)(2,1)} %fusion.64), channel_id=1, source_target_pairs={{0,2},{1,3},{2,0},{3,1},{4,6},{5,7},{6,4},{7,5},{8,10},{9,11},{10,... | collective-permute-start | bytes 3145736 | tf_op jit(solution)/shard_map/ppermute | solution.py:82
  814.8 24.6 %collective-permute-start.43 = (bf16[256,2048]{1,0:T(8,128)(2,1)}, bf16[256,2048]{1,0:T(8,128)(2,1)}, u32[]{:S(2)}, u32[]{:S(2)}) collective-permute-start(bf16[256,2048]{1,0:T(8,128)(2,1)} %get-tuple-element.101), channel_id=1, source_target_pairs={{0,2},{1,3},{2,0},{3,1},{4,6},{5,7},{6,4},{7,5},{8,10},{9,11},{10,... | collective-permute-start | bytes 3145736 | tf_op jit(solution)/shard_map/ppermute | solution.py:82
  1179.0 46.4 %collective-permute-start.50 = (bf16[2,2,1,4,256,128]{5,4,3,2,1,0:T(8,128)(2,1)}, bf16[2,2,1,4,256,128]{5,4,3,2,1,0:T(8,128)(2,1)}, u32[]{:S(2)}, u32[]{:S(2)}) collective-permute-start(bf16[2,2,1,4,256,128]{5,4,3,2,1,0:T(8,128)(2,1)} %pad_maximum_fusion.23), channel_id=1, source_target_pairs={{0,4},{4,0},{8,12},{12,8},{16,20},{20,16},{24,28},{28,24},{1,5},{5... | collective-permute-start | bytes 3145736 | tf_op jit(solution)/shard_map/ppermute | solution.py:82
  (301 other events, 3319.6 us)
Sparse Core Ops, SparseCore 0:
  31.3 154.4 all-gather.2
  1124.0 172.3 reduce-scatter.1

commit v2 on v1

v2 whole, which is shorter than its diff:
```python
import jax
import jax.numpy as jnp
from jax import lax
from jax.experimental import pallas as pl
from jax.experimental.pallas import tpu as pltpu
from jax.sharding import PartitionSpec as P

HEAD_DIM = 64
EPS_NORM = 1e-05
HIGH = lax.Precision.HIGHEST
SQRT_HALF = 0.7071067811865476
INV_SQRT_TAU = 0.3989422804014327
BOTH = ("dp", "tensor")
F32 = jnp.float32
BF16 = jnp.bfloat16


def matmul(left, right):
    return jnp.dot(left, right, preferred_element_type=F32)


def matmul_right_t(left, right):
    return lax.dot_general(left, right, (((1,), (1,)), ((), ())), preferred_element_type=F32)


def matmul_left_t(left, right):
    return lax.dot_general(left, right, (((0,), (0,)), ((), ())), preferred_element_type=F32)


def norm_parts(values):
    centered = values - jnp.mean(values, axis=-1, keepdims=True)
    inverse = lax.rsqrt(jnp.mean(centered * centered, axis=-1, keepdims=True) + EPS_NORM)
    return (centered * inverse, inverse)


def norm_back(normed, inverse, grad_scaled):
    return inverse * (
        grad_scaled
        - jnp.mean(grad_scaled, axis=-1, keepdims=True)
        - normed * jnp.mean(grad_scaled * normed, axis=-1, keepdims=True)
    )


def rms_parts(values):
    return lax.rsqrt(jnp.mean(values * values, axis=-1, keepdims=True) + EPS_NORM)


def rms_back(values, inverse, grad_scaled):
    return inverse * grad_scaled - values * inverse**3 * jnp.mean(
        grad_scaled * values, axis=-1, keepdims=True
    )


def rotary_tables(seq_length):
    half_dim = HEAD_DIM // 2
    freqs = 10000.0 ** (-jnp.arange(half_dim, dtype=F32) * 2.0 / HEAD_DIM)
    angles = jnp.arange(seq_length, dtype=F32)[:, None] * freqs[None, :]
    angles = jnp.concatenate([angles, angles], axis=-1)
    return (jnp.cos(angles), jnp.sin(angles))


def swap(values, axis, bit):
    size = lax.axis_size(axis)
    return lax.ppermute(values, axis, [(i, i ^ bit) for i in range(size)])


def lookup_kernel(ids_ref, table_ref, out_ref):
    rows = ids_ref.shape[0]
    height = table_ref.shape[0]
    places = lax.broadcasted_iota(jnp.int32, (rows, height), 1)
    chosen = jnp.where(ids_ref[...] == places, 1.0, 0.0).astype(BF16)
    out_ref[...] = matmul(chosen, table_ref[...]).astype(BF16)


def lookup(ids, table):
    count = ids.shape[0]
    height, width = table.shape
    rows = 512
    return pl.pallas_call(
        lookup_kernel,
        grid=(count // rows,),
        in_specs=[
            pl.BlockSpec((rows, 1), lambda i: (i, 0)),
            pl.BlockSpec((height, width), lambda i: (0, 0)),
        ],
        out_specs=pl.BlockSpec((rows, width), lambda i: (i, 0)),
        out_shape=jax.ShapeDtypeStruct((count, width), BF16),
        compiler_params=pltpu.CompilerParams(vmem_limit_bytes=48 << 20),
        cost_estimate=pl.CostEstimate(
            flops=4 * count * height * width, bytes_accessed=4 * count * width, transcendentals=0
        ),
        name="lookup",
    )(ids[:, None], table)


def collect_kernel(ids_ref, rows_ref, base_ref, out_ref):
    @pl.when(pl.program_id(0) == 0)
    def _():
        out_ref[...] = jnp.zeros_like(out_ref) if base_ref is None else base_ref[...]

    height = out_ref.shape[0]
    places = lax.broadcasted_iota(jnp.int32, (height, ids_ref.shape[1]), 0)
    chosen = jnp.where(ids_ref[...] == places, 1.0, 0.0).astype(BF16)
    out_ref[...] += matmul(chosen, rows_ref[...])


def collect(ids, values, height, base):
    count, width = values.shape
    rows = 512
    whole = pl.BlockSpec((height, width), lambda i: (0, 0))
    kernel = collect_kernel
    if base is None:
        kernel = lambda ids_ref, rows_ref, out_ref: collect_kernel(ids_ref, rows_ref, None, out_ref)
    return pl.pallas_call(
        kernel,
        grid=(count // rows,),
        in_specs=[
            pl.BlockSpec((1, rows), lambda i: (0, i)),
            pl.BlockSpec((rows, width), lambda i: (i, 0)),
        ]
        + ([] if base is None else [whole]),
        out_specs=whole,
        out_shape=jax.ShapeDtypeStruct((height, width), F32),
        compiler_params=pltpu.CompilerParams(vmem_limit_bytes=48 << 20),
        cost_estimate=pl.CostEstimate(
            flops=4 * count * height * width, bytes_accessed=4 * count * width, transcendentals=0
        ),
        name="collect",
    )(ids[None, :], values, *([] if base is None else [base]))


QUERY_ROWS = 256
ENTRY_LANES = 64
VMEM_LIMIT = 56 << 20


def turn_rows(values):
    half_dim = HEAD_DIM // 2
    return jnp.concatenate([-values[half_dim:], values[:half_dim]], axis=0)


def two_parts(values):
    high = values.astype(BF16)
    return jnp.concatenate([high, (values - high.astype(F32)).astype(BF16)], axis=1)


def entry_table(columns):
    return two_parts(jnp.concatenate([columns, turn_rows(columns)], axis=0))


def spread(table, onehot, trig):
    both = matmul(table, onehot) * trig
    return both[:HEAD_DIM] + both[HEAD_DIM:]


def ahead_mask(rows):
    shape = (rows, rows)
    return lax.broadcasted_iota(jnp.int32, shape, 0) <= lax.broadcasted_iota(jnp.int32, shape, 1)


def attend_kernel(
    place, part0, part1, part2, part3, gain, w_query, w_kv, ids, trig, _after_one, _after_two,
    near, far, context_t, log_total, table_q, table_kv, embeds,
    normed, onehot, keys, values_t,
):
    tokens = ids.shape[1]

    @pl.when(pl.program_id(0) == 0)
    def _():
        own = part0.shape[1]
        for k, part in enumerate((part0, part1, part2, part3)):
            embeds[k * own : (k + 1) * own, :] = part[0]
        wide = embeds[...].astype(F32)
        normed[...] = (wide * rms_parts(wide) * gain[...].astype(F32)).astype(BF16)
        places = lax.broadcasted_iota(jnp.int32, onehot.shape, 0)
        places = jnp.where(places >= ENTRY_LANES, places - ENTRY_LANES, places)
        onehot[...] = jnp.where(places == ids[...], 1.0, 0.0).astype(BF16)
        mixed = matmul(normed[...], w_kv[...]).T
        table_kv[0] = entry_table(mixed[:HEAD_DIM])
        table_kv[1] = entry_table(mixed[HEAD_DIM:])
        keys[...] = spread(table_kv[0], onehot[...], trig[...]).T.astype(BF16)
        values_t[...] = matmul(table_kv[1], onehot[...])[:HEAD_DIM].astype(BF16)

    queries = matmul(normed[...], w_query[...]).T * HEAD_DIM ** (-0.5)
    ahead = ahead_mask(QUERY_ROWS)
    turned = []
    for j in range(2):
        table_q[0, j] = entry_table(queries[j * HEAD_DIM : (j + 1) * HEAD_DIM])
        turned.append(spread(table_q[0, j], onehot[...], trig[...]).astype(BF16))
    odd = place[0] % 2
    rows_out = []
    for block in range(tokens // QUERY_ROWS):
        start, stop = block * QUERY_ROWS, (block + 1) * QUERY_ROWS
        done = []
        for j in range(2):
            scores = matmul(keys[:stop], turned[j][:, start:stop])
            last = jnp.where(ahead, scores[start:], -1e30)
            highest = jnp.max(last, axis=0, keepdims=True)
            if block:
                highest = jnp.maximum(highest, jnp.max(scores[:start], axis=0, keepdims=True))
            last = jnp.exp(last - highest)
            total = jnp.sum(last, axis=0, keepdims=True)
            summed = matmul(values_t[:, start:stop], last.astype(BF16))
            if block:
                first = jnp.exp(scores[:start] - highest)
                total = total + jnp.sum(first, axis=0, keepdims=True)
                summed = summed + matmul(values_t[:, :start], first.astype(BF16))
            done.append(summed / total)
            log_total[0, j : j + 1, start:stop] = highest + jnp.log(total)
        done = jnp.concatenate(done, axis=0)
        context_t[:, start:stop] = done.astype(BF16)
        rows_out.append(done.T.astype(BF16))
        if block % 2:
            even_rows, odd_rows = rows_out[-2:]
            target = (block // 2) ^ (place[0] // 2)
            near[target] = jnp.where(odd == 0, even_rows, odd_rows)
            far[target] = jnp.where(odd == 0, odd_rows, even_rows)


def attend(place, micro, parts, gain, w_query, w_kv, ids, trig, after):
    assert ids.shape[1] == 4 * QUERY_ROWS
    _, own, width = parts[0].shape
    entries = own * len(parts)
    tokens = ids.shape[1]
    pairs = w_query.shape[1] // (2 * HEAD_DIM)
    lanes = 2 * HEAD_DIM
    whole = lambda *shape: pl.BlockSpec(shape, lambda i: (0,) * len(shape))
    return pl.pallas_call(
        attend_kernel,
        grid=(pairs,),
        in_specs=[pl.BlockSpec(memory_space=pltpu.SMEM)]
        + [pl.BlockSpec((1, own, width), lambda i: (micro, 0, 0))] * len(parts)
        + [
            whole(1, width),
            pl.BlockSpec((width, lanes), lambda i: (0, i)),
            whole(width, lanes),
            whole(1, tokens),
            whole(lanes, tokens),
        ]
        + [pl.BlockSpec(memory_space=pl.ANY)] * 2,
        out_specs=[
            pl.BlockSpec((2, QUERY_ROWS, lanes), lambda i: (0, 0, i)),
            pl.BlockSpec((2, QUERY_ROWS, lanes), lambda i: (0, 0, i)),
            pl.BlockSpec((lanes, tokens), lambda i: (i, 0)),
            pl.BlockSpec((1, 2, tokens), lambda i: (i, 0, 0)),
            pl.BlockSpec((1, 2, lanes, lanes), lambda i: (i, 0, 0, 0)),
            whole(2, lanes, lanes),
            whole(entries, width),
        ],
        out_shape=[
            jax.ShapeDtypeStruct((2, QUERY_ROWS, pairs * lanes), BF16),
            jax.ShapeDtypeStruct((2, QUERY_ROWS, pairs * lanes), BF16),
            jax.ShapeDtypeStruct((pairs * lanes, tokens), BF16),
            jax.ShapeDtypeStruct((pairs, 2, tokens), F32),
            jax.ShapeDtypeStruct((pairs, 2, lanes, lanes), BF16),
            jax.ShapeDtypeStruct((2, lanes, lanes), BF16),
            jax.ShapeDtypeStruct((entries, width), BF16),
        ],
        scratch_shapes=[
            pltpu.VMEM((entries, width), BF16),
            pltpu.VMEM((lanes, tokens), BF16),
            pltpu.VMEM((tokens, HEAD_DIM), BF16),
            pltpu.VMEM((HEAD_DIM, tokens), BF16),
        ],
        compiler_params=pltpu.CompilerParams(vmem_limit_bytes=VMEM_LIMIT),
        cost_estimate=pl.CostEstimate(
            flops=12 * 10**9, bytes_accessed=8 * 10**6, transcendentals=5 * 10**6
        ),
        name="attend",
    )(place, *parts, gain, w_query, w_kv, ids, trig, *after)


def attend_back_kernel(
    place, part0, part1, part2, part3, context_t, log_total, table_q, table_kv, ids, ids_share, trig,
    w_query, w_kv, embeds, gain, grad_hidden, _after_one, _after_two, _after_three, grad_entries,
    onehot, columns, keys, keys_t, values, grad_keys, grad_values, total, grad_context,
):
    tokens = ids.shape[1]
    share = part0.shape[0]
    for k, part in enumerate((part0, part1, part2, part3)):
        first = pl.multiple_of((place[0] ^ k) * share, share)
        grad_context[pl.ds(first, share), :] = part[...]
    entries = embeds.shape[0]
    cosine, sine = trig[:HEAD_DIM], trig[HEAD_DIM:]

    @pl.when(pl.program_id(0) == 0)
    def _():
        places = lax.broadcasted_iota(jnp.int32, onehot.shape, 0)
        places = jnp.where(places >= ENTRY_LANES, places - ENTRY_LANES, places)
        chosen = jnp.where(places == ids[...], 1.0, 0.0)
        onehot[...] = chosen.astype(BF16)
        columns[...] = chosen.T.astype(BF16)
        turned = spread(table_kv[0], onehot[...], trig[...])
        keys_t[...] = turned.astype(BF16)
        keys[...] = turned.T.astype(BF16)
        values[...] = matmul(table_kv[1], onehot[...])[:HEAD_DIM].T.astype(BF16)
        grad_keys[...] = jnp.zeros_like(grad_keys)
        grad_values[...] = jnp.zeros_like(grad_values)
        total[...] = jnp.zeros_like(total)

    def to_entries(grads, cos_part, sin_part, rows):
        straight = matmul((grads * cos_part).astype(BF16), rows)
        crossed = matmul((grads * sin_part).astype(BF16), rows)
        return straight, crossed

    def two_stacked(grads):
        high = grads.astype(BF16)
        rest = (grads - high.astype(F32)).astype(BF16)
        lane = lax.broadcasted_iota(jnp.int32, grads.shape, 1)
        return jnp.where(lane < ENTRY_LANES, high.astype(F32), rest.astype(F32)).T.astype(BF16)

    ahead = ahead_mask(QUERY_ROWS)
    grad_t = grad_context[...].astype(F32).T
    products = grad_t * context_t[...].astype(F32)
    grad_t = grad_t.astype(BF16)
    per_head = []
    for j in range(2):
        head = slice(j * HEAD_DIM, (j + 1) * HEAD_DIM)
        turned = spread(table_q[0, j], onehot[...], trig[...])
        queries_t = turned.astype(BF16)
        queries = turned.T.astype(BF16)
        offset = jnp.sum(products[head], axis=0, keepdims=True)
        straight = jnp.zeros((HEAD_DIM, columns.shape[1]), F32)
        crossed = jnp.zeros((HEAD_DIM, columns.shape[1]), F32)
        for block in range(tokens // QUERY_ROWS):
            start, stop = block * QUERY_ROWS, (block + 1) * QUERY_ROWS
            scores = matmul(keys[:stop], queries_t[:, start:stop])
            soft = jnp.exp(scores - log_total[0, j : j + 1, start:stop])
            last = jnp.where(ahead, soft[start:], 0.0)
            soft = jnp.concatenate([soft[:start], last], axis=0) if block else last
            grad_soft = matmul(values[:stop], grad_t[head, start:stop])
            grad_scores = (soft * (grad_soft - offset[:, start:stop])).astype(BF16)
            grad_values[:stop] += matmul(soft.astype(BF16), grad_context[start:stop, head])
            grad_keys[:stop] += matmul(grad_scores, queries[start:stop])
            grad_queries = matmul(keys_t[:, :stop], grad_scores) * HEAD_DIM ** (-0.5)
            parts = to_entries(
                grad_queries, cosine[:, start:stop], sine[:, start:stop], columns[start:stop]
            )
            straight, crossed = straight + parts[0], crossed + parts[1]
        per_head.append(straight - turn_rows(crossed))
    total[...] += matmul_right_t(two_stacked(jnp.concatenate(per_head, axis=0)), w_query[...])

    @pl.when(pl.program_id(0) == pl.num_programs(0) - 1)
    def _():
        grads = jnp.concatenate([grad_keys[...], grad_values[...]], axis=1).T
        straight, crossed = to_entries(grads[:HEAD_DIM], cosine, sine, columns[...])
        summed = matmul(grads[HEAD_DIM:].astype(BF16), columns[...])
        both = jnp.concatenate([straight - turn_rows(crossed), summed], axis=0)
        full = total[...] + matmul_right_t(two_stacked(both), w_kv[...])
        scaled = (full[:entries] + full[entries:]) * gain[...].astype(F32)
        wide = embeds[...].astype(F32)
        places = lax.broadcasted_iota(jnp.int32, (entries, ids_share.shape[1]), 0)
        own = jnp.where(places == ids_share[...], 1.0, 0.0).astype(BF16)
        result = rms_back(wide, rms_parts(wide), scaled) + matmul(own, grad_hidden[...])
        grad_entries[...] = result.astype(BF16)


def attend_back(
    place, parts, kept, ids, ids_share, trig, w_query, w_kv, gain, grad_hidden, after
):
    context_t, log_total, table_q, table_kv, embeds = kept
    share = parts[0].shape[0]
    entries, width = embeds.shape
    tokens = ids.shape[1]
    pairs = w_query.shape[1] // (2 * HEAD_DIM)
    lanes = 2 * HEAD_DIM
    whole = lambda *shape: pl.BlockSpec(shape, lambda i: (0,) * len(shape))
    return pl.pallas_call(
        attend_back_kernel,
        grid=(pairs,),
        in_specs=[pl.BlockSpec(memory_space=pltpu.SMEM)]
        + [pl.BlockSpec((share, lanes), lambda i: (0, i))] * len(parts)
        + [
            pl.BlockSpec((lanes, tokens), lambda i: (i, 0)),
            pl.BlockSpec((1, 2, tokens), lambda i: (i, 0, 0)),
            pl.BlockSpec((1, 2, lanes, lanes), lambda i: (i, 0, 0, 0)),
            whole(2, lanes, lanes),
            whole(1, tokens),
            whole(*ids_share.shape),
            whole(lanes, tokens),
            pl.BlockSpec((width, lanes), lambda i: (0, i)),
            whole(width, lanes),
            whole(entries, width),
            whole(1, width),
            whole(*grad_hidden.shape),
        ]
        + [pl.BlockSpec(memory_space=pl.ANY)] * 3,
        out_specs=whole(entries, width),
        out_shape=jax.ShapeDtypeStruct((entries, width), BF16),
        scratch_shapes=[
            pltpu.VMEM((lanes, tokens), BF16),
            pltpu.VMEM((tokens, lanes), BF16),
            pltpu.VMEM((tokens, HEAD_DIM), BF16),
            pltpu.VMEM((HEAD_DIM, tokens), BF16),
            pltpu.VMEM((tokens, HEAD_DIM), BF16),
            pltpu.VMEM((tokens, HEAD_DIM), F32),
            pltpu.VMEM((tokens, HEAD_DIM), F32),
            pltpu.VMEM((2 * entries, width), F32),
            pltpu.VMEM((tokens, lanes), BF16),
        ],
        compiler_params=pltpu.CompilerParams(vmem_limit_bytes=VMEM_LIMIT),
        cost_estimate=pl.CostEstimate(
            flops=25 * 10**9, bytes_accessed=8 * 10**6, transcendentals=5 * 10**6
        ),
        name="attend_back",
    )(
        place, *parts, context_t, log_total, table_q, table_kv, ids, ids_share, trig,
        w_query, w_kv, embeds, gain, grad_hidden, *after,
    )


ANY_SPEC = pl.BlockSpec(memory_space=pl.ANY)


def pick_rows(ids, entries):
    places = lax.broadcasted_iota(jnp.int32, (entries, ids.shape[1]), 0)
    return jnp.where(places == ids[...], 1.0, 0.0).astype(BF16)


def hidden_kernel(
    embeds, ids_own, ids_peer, gain, c0, c1, c2, c3, w0, w1, w2, w3, _after_one, _after_two,
    normed_own, normed_peer, hidden,
):
    share = normed_own.shape[0]
    for own, ids, normed in ((False, ids_peer, normed_peer), (True, ids_own, normed_own)):
        total = matmul_left_t(pick_rows(ids, embeds.shape[0]), embeds[...])
        for k, (part, weight) in enumerate(((c0, w0), (c1, w1), (c2, w2), (c3, w3))):
            total = total + matmul(part[int(own == (k >= 2))], weight[...])
        normed[...] = (total * rms_parts(total) * gain[...].astype(F32)).astype(BF16)
        if own:
            hidden[...] = total


def hidden_rows_of(embeds, ids_own, ids_peer, gain, parts, weights, after):
    rows, width = ids_own.shape[1], embeds.shape[1]
    vmem = pl.BlockSpec(memory_space=pltpu.VMEM)
    return pl.pallas_call(
        hidden_kernel,
        in_specs=[vmem] * 12 + [ANY_SPEC] * 2,
        out_specs=[vmem] * 3,
        out_shape=[
            jax.ShapeDtypeStruct((rows, width), BF16),
            jax.ShapeDtypeStruct((rows, width), BF16),
            jax.ShapeDtypeStruct((rows, width), F32),
        ],
        compiler_params=pltpu.CompilerParams(vmem_limit_bytes=VMEM_LIMIT),
        cost_estimate=pl.CostEstimate(
            flops=6 * 10**9, bytes_accessed=18 * 10**6, transcendentals=0
        ),
        name="hidden",
    )(embeds, ids_own, ids_peer, gain, *parts, *weights, *after)


def hidden_back_kernel(
    cotangent, hidden, kept, from_core, from_chip, gain, w0, w1, w2, w3,
    low, p0, p1, p2, p3,
):
    grads = kept[...].astype(F32) + from_core[...].astype(F32) + from_chip[...].astype(F32)
    rows = hidden[...]
    scaled = grads * gain[...].astype(F32)
    total = cotangent[0] + rms_back(rows, rms_parts(rows), scaled)
    total = total.astype(BF16)
    low[...] = total
    for part, weight in ((p2, w2), (p3, w3), (p1, w1), (p0, w0)):
        part[...] = matmul_right_t(total, weight[...]).astype(BF16)


def hidden_back(micro, cotangent, hidden, kept, from_core, from_chip, gain, weights):
    rows, width = hidden.shape
    heads = weights[0].shape[0]
    whole = lambda *shape: pl.BlockSpec(shape, lambda i: (0,) * len(shape))
    return pl.pallas_call(
        hidden_back_kernel,
        grid=(1,),
        in_specs=[pl.BlockSpec((1, rows, width), lambda i: (micro, 0, 0))]
        + [whole(rows, width)] * 4
        + [whole(1, width)]
        + [whole(heads, width)] * 4,
        out_specs=[whole(rows, width)] + [whole(rows, heads)] * 4,
        out_shape=[jax.ShapeDtypeStruct((rows, width), BF16)]
        + [jax.ShapeDtypeStruct((rows, heads), BF16)] * 4,
        compiler_params=pltpu.CompilerParams(vmem_limit_bytes=VMEM_LIMIT),
        cost_estimate=pl.CostEstimate(
            flops=2 * 10**9, bytes_accessed=16 * 10**6, transcendentals=0
        ),
        name="hidden_back",
    )(cotangent, hidden, kept, from_core, from_chip, gain, *weights)


def mlp_kernel(
    x_mine, x_other, grad_mine_in, grad_other_in, gate_hbm, up_hbm, down_hbm, _after_one, _after_two, _after_three,
    out_mine, out_other, grad_mine, grad_other,
    w_gate, w_up, w_down, sems,
):
    copies = [
        pltpu.make_async_copy(source, target, sems.at[i])
        for i, (source, target) in enumerate(
            ((gate_hbm, w_gate), (up_hbm, w_up), (down_hbm, w_down))
        )
    ]
    for copy in copies:
        copy.start()
    for first, (rows, cots, out, grad) in enumerate(
        ((x_other, grad_other_in, out_other, grad_other), (x_mine, grad_mine_in, out_mine, grad_mine))
    ):
        if first == 0:
            copies[0].wait()
        gate = matmul(rows[...], w_gate[...])
        if first == 0:
            copies[1].wait()
        upward = matmul(rows[...], w_up[...])
        if first == 0:
            copies[2].wait()
        grad_active = matmul_right_t(cots[...], w_down[...])
        sigmoid = 1.0 / (1.0 + jnp.exp(-gate))
        silu = gate * sigmoid
        activated = (silu * upward).astype(BF16)
        grad_gate = grad_active * upward * (sigmoid * (1.0 + gate * (1.0 - sigmoid)))
        grad_up = (grad_active * silu).astype(BF16)
        out[...] = matmul(activated, w_down[...]).astype(BF16)
        total = matmul_right_t(grad_gate.astype(BF16), w_gate[...])
        grad[...] = (total + matmul_right_t(grad_up, w_up[...])).astype(BF16)


def mlp(x_mine, x_other, cot_mine, cot_other, w_gate, w_up, w_down, after):
    rows, width = x_mine.shape
    units = w_gate.shape[1]
    vmem = pl.BlockSpec(memory_space=pltpu.VMEM)
    return pl.pallas_call(
        mlp_kernel,
        in_specs=[vmem] * 4 + [ANY_SPEC] * 6,
        out_specs=[vmem] * 4,
        out_shape=[jax.ShapeDtypeStruct((rows, width), BF16)] * 4,
        scratch_shapes=[
            pltpu.VMEM((width, units), BF16),
            pltpu.VMEM((width, units), BF16),
            pltpu.VMEM((units, width), BF16),
            pltpu.SemaphoreType.DMA((3,)),
        ],
        compiler_params=pltpu.CompilerParams(vmem_limit_bytes=VMEM_LIMIT),
        cost_estimate=pl.CostEstimate(
            flops=24 * rows * width * units, bytes_accessed=26 * 10**6, transcendentals=2 * rows * units
        ),
        name="mlp",
    )(x_mine, x_other, cot_mine, cot_other, w_gate, w_up, w_down, *after)


def add_kernel(left, right, _after, out):
    out[...] = (left[...].astype(F32) + right[...].astype(F32)).astype(BF16)


def add_after(left, right, after):
    vmem = pl.BlockSpec(memory_space=pltpu.VMEM)
    return pl.pallas_call(
        add_kernel,
        in_specs=[vmem, vmem, ANY_SPEC],
        out_specs=vmem,
        out_shape=jax.ShapeDtypeStruct(left.shape, BF16),
        name="add_after",
    )(left, right, after)


def cast_kernel(values, _after, out):
    out[...] = values[0].astype(BF16)


def cast_after(micro, values, after):
    _, rows, width = values.shape
    return pl.pallas_call(
        cast_kernel,
        grid=(1,),
        in_specs=[pl.BlockSpec((1, rows, width), lambda i: (micro, 0, 0)), ANY_SPEC],
        out_specs=pl.BlockSpec((rows, width), lambda i: (0, 0)),
        out_shape=jax.ShapeDtypeStruct((rows, width), BF16),
        name="cast_after",
    )(values, after)


BLOCKS = 32
UNIT = 16
LAYER_UNITS = 12
VECTORS = 8


def square(ref):
    blocks, rows, width = ref.shape
    return ref[...].reshape(blocks * rows, width)


def entry_bias(valid, rows, slots):
    shape = (rows, rows)
    same = lax.broadcasted_iota(jnp.int32, shape, 0) // slots == lax.broadcasted_iota(
        jnp.int32, shape, 1
    ) // slots
    return jnp.where(jnp.logical_and(same, valid > 0.5), 0.0, -1e30)


def entry_soft(queries, keys, bias):
    scores = matmul_right_t(queries, keys) * HEAD_DIM ** (-0.5) + bias
    expon = jnp.exp(scores - jnp.max(scores, axis=1, keepdims=True))
    return expon / jnp.sum(expon, axis=1, keepdims=True)


def bell(values):
    return 0.5 * (1.0 + lax.erf(values * SQRT_HALF))


def hyper_kernel(
    slots, place, _after, part0, part1, part2, part3, valid, vectors, inner_bias, outer, w_q, w_k, w_v, w_o, in0, in1, in2, in3,
    pr0, pr1, pr2, pr3,
    below, mixed, context, middle, inner, pooled, pooled_norm, embeds,
    state, joined,
):
    layer = pl.program_id(0)
    layers = pl.num_programs(0)
    rows, width = state.shape

    @pl.when(layer == 0)
    def _():
        columns = part0.shape[1]
        for k, part in enumerate((part0, part1, part2, part3)):
            at = pl.multiple_of((place[0] ^ k) * columns, columns)
            state[:, pl.ds(at, columns)] = part[...].astype(F32)

    def vector(index):
        return vectors[pl.ds(index * layers + layer, 1), :]

    hidden = state[...]
    below[0] = hidden
    normed, _ = norm_parts(hidden)
    normed_in = (normed * vector(0) + vector(1)).astype(BF16)
    queries = (matmul(normed_in, square(w_q)) + vector(2)).astype(BF16)
    keys = matmul(normed_in, square(w_k)).astype(BF16)
    values = (matmul(normed_in, square(w_v)) + vector(3)).astype(BF16)
    mixed[0, :, :width] = queries
    mixed[0, :, width : 2 * width] = keys
    mixed[0, :, 2 * width :] = values
    bias = entry_bias(valid[...], rows, slots)
    for head in range(width // HEAD_DIM):
        at = slice(head * HEAD_DIM, (head + 1) * HEAD_DIM)
        soft = entry_soft(queries[:, at], keys[:, at], bias)
        joined[:, at] = matmul(soft.astype(BF16), values[:, at])
    context_low = joined[...].astype(BF16)
    context[0] = context_low
    centre = hidden + matmul(context_low, square(w_o)) + vector(4)
    middle[0] = centre
    normed, _ = norm_parts(centre)
    normed_mid = (normed * vector(5) + vector(6)).astype(BF16)
    total = centre + vector(7)
    for j, piece in enumerate((in0, in1, in2, in3)):
        at = slice(j * width, (j + 1) * width)
        part = matmul(normed_mid, square(piece)) + inner_bias[pl.ds(layer, 1), at]
        inner[0, :, at] = part
        activated = (part * bell(part)).astype(BF16)
        blocks = BLOCKS // 4
        total = total + matmul(
            activated, outer[j * blocks : (j + 1) * blocks].reshape(width, width)
        )
    state[...] = total

    @pl.when(layer == layers - 1)
    def _():
        slot = lax.broadcasted_iota(jnp.int32, (rows, width), 0) % slots
        first = jnp.where(slot == 0, total, 0.0).reshape(rows // slots, slots, width)
        first = jnp.sum(first, axis=1)
        pooled[...] = first
        normed, _ = norm_parts(first)
        low = (normed * vectors[VECTORS * layers : VECTORS * layers + 1, :]
               + vectors[VECTORS * layers + 1 : VECTORS * layers + 2, :]).astype(BF16)
        pooled_norm[...] = low
        for j, piece in enumerate((pr0, pr1, pr2, pr3)):
            embeds[:, j * width : (j + 1) * width] = matmul(low, square(piece)).astype(BF16)


def layer_specs(width, which):
    specs = [pl.BlockSpec((BLOCKS, 4 * UNIT, width), lambda i: (0, which(i) * LAYER_UNITS // 4, 0))]
    for j in range(4, LAYER_UNITS):
        specs.append(
            pl.BlockSpec((BLOCKS, UNIT, width), lambda i, j=j: (0, which(i) * LAYER_UNITS + j, 0))
        )
    return specs


def proj_specs(width, layers):
    return [
        pl.BlockSpec((BLOCKS, UNIT, width), lambda i, j=j: (0, layers * LAYER_UNITS + j, 0))
        for j in range(4)
    ]


def whole_spec(*shape):
    return pl.BlockSpec(shape, lambda i: (0,) * len(shape))


def hyper_forward(where, after, parts, valid, vectors, inner_bias, packed, slots):
    rows, width = parts[0].shape[0], len(parts) * parts[0].shape[1]
    layers, inner_width = inner_bias.shape
    entries = rows // slots
    by_layer = lambda *shape: pl.BlockSpec((1,) + shape, lambda i: (i,) + (0,) * len(shape))
    return pl.pallas_call(
        lambda *refs: hyper_kernel(slots, *refs),
        grid=(layers,),
        in_specs=[pl.BlockSpec(memory_space=pltpu.SMEM)]
        + [pl.BlockSpec(memory_space=pl.ANY)]
        + [whole_spec(*part.shape) for part in parts]
        + [
            whole_spec(1, rows),
            whole_spec(*vectors.shape),
            whole_spec(layers, inner_width),
        ]
        + layer_specs(width, lambda i: i)
        + proj_specs(width, layers),
        out_specs=[
            by_layer(rows, width),
            by_layer(rows, 3 * width),
            by_layer(rows, width),
            by_layer(rows, width),
            by_layer(rows, inner_width),
            whole_spec(entries, width),
            whole_spec(entries, width),
            whole_spec(entries, 4 * width),
        ],
        out_shape=[
            jax.ShapeDtypeStruct((layers, rows, width), F32),
            jax.ShapeDtypeStruct((layers, rows, 3 * width), BF16),
            jax.ShapeDtypeStruct((layers, rows, width), BF16),
            jax.ShapeDtypeStruct((layers, rows, width), F32),
            jax.ShapeDtypeStruct((layers, rows, inner_width), F32),
            jax.ShapeDtypeStruct((entries, width), F32),
            jax.ShapeDtypeStruct((entries, width), BF16),
            jax.ShapeDtypeStruct((entries, 4 * width), BF16),
        ],
        scratch_shapes=[pltpu.VMEM((rows, width), F32), pltpu.VMEM((rows, width), F32)],
        compiler_params=pltpu.CompilerParams(vmem_limit_bytes=VMEM_LIMIT),
        cost_estimate=pl.CostEstimate(
            flops=8 * 10**9, bytes_accessed=25 * 10**6, transcendentals=4 * 10**6
        ),
        name="hyper",
    )(where, after, *parts, valid, vectors, inner_bias, *([packed] * (LAYER_UNITS - 3 + 4)))


def hyper_back_kernel(
    slots, layer, layers, last,
    *refs,
):
    place, refs = refs[0], refs[1:]
    if last:
        grad_embeds, pooled, pooled_norm, pr0, pr1, pr2, pr3 = refs[:7]
        refs = refs[7:]
    else:
        grad_start = refs[0]
        refs = refs[1:]
    valid, vectors, below, mixed, context, middle, inner = refs[1:8]
    outer, w_q, w_k, w_v, w_o, in0, in1, in2, in3 = refs[8:17]
    refs = refs[17:]
    if layer == 0:
        small_above, inner_above = refs[:2]
        refs = refs[2:]
    packed = refs[:4]
    grad_below, small, inner_small, grad_mixed = refs[4:8]
    _, rows, width = below.shape
    blocks = BLOCKS // 4
    core, chip, side, line = place[0], place[1], place[2], place[3]
    half = packed[0].shape[3]

    def vector(index):
        at = index * layers + layer
        return vectors[at : at + 1, :]

    def put_rows(lines, at, rows_each, values):
        for i, z in enumerate(lines):
            for x in range(2):
                for y in range(2):
                    left, right = values[i, x, y, 0], values[i, x, y, 1]
                    mine = jnp.where(core == 0, left, right)
                    other = jnp.where(core == 0, right, left)
                    for kind, part in enumerate((mine, other)):
                        if at < half:
                            where = pl.ds(at, rows_each)
                            packed[kind][y ^ chip, x ^ side, (z - line) & 3, where, :] = part
                        else:
                            where = pl.ds(at - half, rows_each)
                            packed[2 + kind][x ^ side, y ^ chip, (z - line) & 3, where, :] = part

    def put(unit, grads):
        grads = grads.astype(BF16).reshape(4, 2, 2, 2, UNIT, width)
        put_rows(range(4), unit * UNIT, UNIT, grads)

    def column_sum(values):
        return jnp.sum(values, axis=0, keepdims=True)

    if last:
        normed, inverse = norm_parts(pooled[...])
        grad_norm = jnp.zeros(normed.shape, F32)
        for j, piece in enumerate((pr0, pr1, pr2, pr3)):
            part = grad_embeds[:, j * width : (j + 1) * width]
            put(LAYER_UNITS + j, matmul_left_t(pooled_norm[...], part))
            grad_norm = grad_norm + matmul_right_t(part, square(piece))
        small[VECTORS : VECTORS + 1, :] = column_sum(grad_norm * normed)
        small[VECTORS + 1 : VECTORS + 2, :] = column_sum(grad_norm)
        final_gain = vectors[VECTORS * layers : VECTORS * layers + 1, :]
        grad_pooled = norm_back(normed, inverse, grad_norm * final_gain)
        slot = lax.broadcasted_iota(jnp.int32, (rows, width), 0) % slots
        grad_rows = jnp.broadcast_to(grad_pooled[:, None, :], (rows // slots, slots, width))
        grad_rows = jnp.where(slot == 0, grad_rows.reshape(rows, width), 0.0)
    else:
        grad_rows = grad_start[...]

    low = grad_rows.astype(BF16)
    small[7:8, :] = column_sum(grad_rows)
    normed_two, inverse_two = norm_parts(middle[0])
    normed_mid = (normed_two * vector(5) + vector(6)).astype(BF16)
    grad_mid = jnp.zeros(grad_rows.shape, F32)
    for j, piece in enumerate((in0, in1, in2, in3)):
        at = slice(j * width, (j + 1) * width)
        part = inner[0, :, at]
        share = bell(part)
        activated = (part * share).astype(BF16)
        slope = share + part * jnp.exp(-0.5 * part * part) * INV_SQRT_TAU
        where = slice(j * blocks, (j + 1) * blocks)
        grad_outer = matmul_left_t(activated, low).astype(BF16)
        put_rows((j,), 0, 4 * UNIT, grad_outer.reshape(1, 2, 2, 2, 4 * UNIT, width))
        grad_part = matmul_right_t(low, outer[where].reshape(width, width)) * slope
        inner_small[:, at] = column_sum(grad_part)
        grad_part = grad_part.astype(BF16)
        put(8 + j, matmul_left_t(normed_mid, grad_part))
        grad_mid = grad_mid + matmul_right_t(grad_part, square(piece))
    small[5:6, :] = column_sum(grad_mid * normed_two)
    small[6:7, :] = column_sum(grad_mid)
    grad_rows = grad_rows + norm_back(normed_two, inverse_two, grad_mid * vector(5))
    small[4:5, :] = column_sum(grad_rows)
    low = grad_rows.astype(BF16)
    put(7, matmul_left_t(context[0], low))
    grad_context = matmul_right_t(low, square(w_o)).astype(BF16)
    bias = entry_bias(valid[...], rows, slots)
    for head in range(width // HEAD_DIM):
        at, key_at, value_at = (
            slice(i * width + head * HEAD_DIM, i * width + (head + 1) * HEAD_DIM) for i in range(3)
        )
        queries, keys, values = mixed[0, :, at], mixed[0, :, key_at], mixed[0, :, value_at]
        soft = entry_soft(queries, keys, bias)
        grad_head = grad_context[:, at]
        grad_soft = matmul_right_t(grad_head, values)
        offset = jnp.sum(soft * grad_soft, axis=1, keepdims=True)
        grad_scores = (soft * (grad_soft - offset) * HEAD_DIM ** (-0.5)).astype(BF16)
        grad_mixed[:, at] = matmul(grad_scores, keys)
        grad_mixed[:, key_at] = matmul_left_t(grad_scores, queries)
        grad_mixed[:, value_at] = matmul_left_t(soft.astype(BF16), grad_head)
    normed_one, inverse_one = norm_parts(below[0])
    normed_in = (normed_one * vector(0) + vector(1)).astype(BF16)
    grad_in = jnp.zeros(grad_rows.shape, F32)
    for i, piece in enumerate((w_q, w_k, w_v)):
        part = grad_mixed[:, i * width : (i + 1) * width]
        if i != 1:
            small[2 + i // 2 : 3 + i // 2, :] = column_sum(part)
        part = part.astype(BF16)
        put(4 + i, matmul_left_t(normed_in, part))
        grad_in = grad_in + matmul_right_t(part, square(piece))
    small[0:1, :] = column_sum(grad_in * normed_one)
    small[1:2, :] = column_sum(grad_in)
    grad_rows = grad_rows + norm_back(normed_one, inverse_one, grad_in * vector(0))
    if layer == 0:
        part = grad_rows.astype(BF16)
        columns = grad_below.shape[2]
        for t in range(grad_below.shape[0]):
            grad_below[t ^ (2 * chip + core)] = part[:, t * columns : (t + 1) * columns]
        wide = refs[8]
        wide[...] = jnp.zeros_like(wide)
        own = small[...]
        above = small_above[...]
        for b in range(BLOCKS):
            at = slice(b * UNIT, (b + 1) * UNIT)
            for i in range(layers):
                source = own if i == 0 else above
                wide[b, i * VECTORS : (i + 1) * VECTORS, 0:UNIT] = source[:VECTORS, at]
            wide[b, VECTORS * layers : VECTORS * layers + 2, 0:UNIT] = above[VECTORS:, at]
            at = slice(b * 4 * UNIT, (b + 1) * 4 * UNIT)
            wide[b, VECTORS * layers + 2 : VECTORS * layers + 3, 0 : 4 * UNIT] = inner_small[:, at]
            wide[b, VECTORS * layers + 3 : VECTORS * layers + 4, 0 : 4 * UNIT] = inner_above[:, at]
        base = LAYER_UNITS * UNIT
        spare = jnp.zeros((BLOCKS, 2 * UNIT, width - wide.shape[2]), F32)
        full = jnp.concatenate([wide[...], spare], axis=2).astype(BF16)
        put_rows(range(4), base, 2 * UNIT, full.reshape(4, 2, 2, 2, 2 * UNIT, width))
    else:
        grad_below[...] = grad_rows


def hyper_backward(place, layer, source, valid, vectors, kept, packed, slots, above, columns, after):
    below, mixed, context, middle, inner = kept
    layers, rows, width = below.shape
    inner_width = inner.shape[2]
    last = layer == layers - 1
    at_layer = lambda *shape: pl.BlockSpec((1,) + shape, lambda i: (layer,) + (0,) * len(shape))
    inputs, specs = [place], [pl.BlockSpec(memory_space=pltpu.SMEM)]
    if last:
        grad_embeds, pooled, pooled_norm = source
        inputs += [grad_embeds, pooled, pooled_norm] + [packed] * 4
        specs += [whole_spec(*grad_embeds.shape), whole_spec(*pooled.shape)]
        specs += [whole_spec(*pooled_norm.shape)] + proj_specs(width, layers)
    else:
        inputs += [source]
        specs += [whole_spec(rows, width)]
    inputs += [after, valid, vectors, below, mixed, context, middle, inner]
    specs += [pl.BlockSpec(memory_space=pl.ANY)]
    specs += [whole_spec(1, rows), whole_spec(*vectors.shape), at_layer(rows, width)]
    specs += [at_layer(rows, 3 * width), at_layer(rows, width), at_layer(rows, width)]
    specs += [at_layer(rows, inner_width)]
    inputs += [packed] * (LAYER_UNITS - 3)
    specs += layer_specs(width, lambda i: layer)
    scratch = [pltpu.VMEM((rows, 3 * width), F32)]
    units = LAYER_UNITS + (4 if last else 0) + (2 if layer == 0 else 0)
    below_shape = jax.ShapeDtypeStruct((rows, width), F32)
    if layer == 0:
        inputs += list(above)
        specs += [whole_spec(*part.shape) for part in above]
        below_shape = jax.ShapeDtypeStruct((width // columns, rows, columns), BF16)
        scratch.append(pltpu.VMEM((BLOCKS, 2 * UNIT, 128), F32))
    half = units // 2 * UNIT
    out_shape = [
        jax.ShapeDtypeStruct((2, 2, 4, half, width), BF16),
        jax.ShapeDtypeStruct((2, 2, 4, half, width), BF16),
        jax.ShapeDtypeStruct((2, 2, 4, units * UNIT - half, width), BF16),
        jax.ShapeDtypeStruct((2, 2, 4, units * UNIT - half, width), BF16),
        below_shape,
        jax.ShapeDtypeStruct((VECTORS + (2 if last else 0), width), F32),
        jax.ShapeDtypeStruct((1, inner_width), F32),
    ]
    return pl.pallas_call(
        lambda *refs: hyper_back_kernel(slots, layer, layers, last, *refs),
        grid=(1,),
        in_specs=specs,
        out_specs=[whole_spec(*shape.shape) for shape in out_shape],
        out_shape=out_shape,
        scratch_shapes=scratch,
        compiler_params=pltpu.CompilerParams(vmem_limit_bytes=VMEM_LIMIT),
        cost_estimate=pl.CostEstimate(
            flops=8 * 10**9, bytes_accessed=25 * 10**6, transcendentals=4 * 10**6
        ),
        name="hyper_back",
    )(*inputs)


def pack_kernel(layers, *refs):
    (g1, b1, w_qkv, bq, bv, w_ao, bao, g2, b2, w_in, b_in, w_out, bout, fg, fb, w_proj) = refs[:16]
    packed, wide = refs[16:]
    width = packed.shape[1]
    for layer in range(layers):
        base = layer * LAYER_UNITS * UNIT
        packed[base : base + 4 * UNIT] = w_out[layer]
        for j in range(3):
            at = base + (4 + j) * UNIT
            packed[at : at + UNIT] = w_qkv[layer, :, j * width : (j + 1) * width]
        packed[base + 7 * UNIT : base + 8 * UNIT] = w_ao[layer]
        for j in range(4):
            at = base + (8 + j) * UNIT
            packed[at : at + UNIT] = w_in[layer, :, j * width : (j + 1) * width]
    base = layers * LAYER_UNITS * UNIT
    for j in range(4):
        packed[base + j * UNIT : base + (j + 1) * UNIT] = w_proj[:, j * width : (j + 1) * width]
    wide[...] = jnp.zeros_like(wide)
    for j, ref in enumerate((g1, b1, bq, bv, bao, g2, b2, bout)):
        wide[j * layers : (j + 1) * layers, 0:UNIT] = ref[...].astype(F32)
    at = VECTORS * layers
    wide[at : at + 1, 0:UNIT] = fg[...].astype(F32)
    wide[at + 1 : at + 2, 0:UNIT] = fb[...].astype(F32)
    wide[at + 2 : at + 2 + layers, 0 : 4 * UNIT] = b_in[...].astype(F32)
    base = base + 4 * UNIT
    packed[base:] = jnp.zeros((2 * UNIT, width), BF16)
    packed[base:, : wide.shape[1]] = wide[...].astype(BF16)


def pack_shards(shards):
    (g1, b1, w_qkv, bq, bv, w_ao, bao, g2, b2, w_in, b_in, w_out, bout, fg, fb, w_proj) = shards
    layers, own, _ = w_qkv.shape
    width = w_ao.shape[2]
    if own == UNIT:
        inputs = list(shards)
        inputs[13], inputs[14] = fg[None], fb[None]
        return pl.pallas_call(
            lambda *refs: pack_kernel(layers, *refs),
            out_shape=jax.ShapeDtypeStruct(((layers * LAYER_UNITS + 6) * UNIT, width), BF16),
            scratch_shapes=[pltpu.VMEM((2 * UNIT, 128), F32)],
            name="pack",
        )(*inputs)
    pieces = []
    for layer in range(layers):
        pieces += [w_out[layer]]
        pieces += [w_qkv[layer, :, i * width : (i + 1) * width] for i in range(3)]
        pieces += [w_ao[layer]]
        pieces += [w_in[layer, :, i * width : (i + 1) * width] for i in range(4)]
    pieces += [w_proj[:, i * width : (i + 1) * width] for i in range(4)]
    small = [jnp.concatenate([g1, b1, bq, bv, bao, g2, b2, bout, fg[None], fb[None]]), b_in]
    small = [jnp.pad(part, ((0, 0), (0, width - part.shape[1]))) for part in small]
    small = jnp.concatenate(small)
    small = jnp.pad(small, ((0, 2 * UNIT - small.shape[0]), (0, 0)))
    return jnp.concatenate(pieces + [small])


def piece_rows(layers, own, first_layer=0, last_layer=None):
    return [4 * own] + [own] * (LAYER_UNITS - 4)


def canonical(gathered, own, layers):
    devices, _, width = gathered.shape
    count = VECTORS * layers + 2
    small = gathered[:, -2 * UNIT :]
    vectors = small[:, :count, :own].transpose(1, 0, 2).reshape(count, devices * own)
    inner_bias = small[:, count : count + layers, : 4 * own].transpose(1, 0, 2)
    inner_bias = inner_bias.reshape(layers, devices * 4 * own)
    if own != UNIT:
        pieces, at = [], 0
        for rows in piece_rows(layers, own) * layers + [own] * 4:
            part = gathered[:, at : at + rows].reshape(BLOCKS, -1, width)
            pieces.append(part)
            at += rows
        gathered = jnp.concatenate(pieces, axis=1)
    return gathered, vectors.astype(F32), inner_bias.astype(F32)


def to_devices(packed, devices, rows_list, vector_rows):
    if devices == BLOCKS:
        return packed
    width = packed.shape[2]
    split = devices // BLOCKS
    pieces, at = [], 0
    for rows in rows_list:
        pieces.append(packed[:, at : at + rows].reshape(devices, rows // split, width))
        at += rows
    if vector_rows:
        small = packed[:, at : at + vector_rows]
        narrow = small[:, : vector_rows - 14, :UNIT].reshape(BLOCKS, -1, split, UNIT // split)
        broad = small[:, vector_rows - 14 : vector_rows - 12, : 4 * UNIT]
        broad = broad.reshape(BLOCKS, -1, split, 4 * UNIT // split)
        parts = []
        for part in (narrow, broad):
            part = part.transpose(0, 2, 1, 3).reshape(devices, part.shape[1], part.shape[3])
            parts.append(jnp.pad(part, ((0, 0), (0, 0), (0, width - part.shape[2]))))
        small = jnp.concatenate(parts, axis=1)
        pieces.append(jnp.pad(small, ((0, 0), (0, vector_rows - small.shape[1]), (0, 0))))
    return jnp.concatenate(pieces, axis=1)


def unpack_kernel(layers, above, below, g_qkv, g_ao, g_in, g_out, g_proj, *vectors):
    width = above.shape[1]
    for layer, ref in ((0, below), (1, above)):
        g_out[layer] = ref[: 4 * UNIT].astype(F32)
        for j in range(3):
            at = (4 + j) * UNIT
            g_qkv[layer, :, j * width : (j + 1) * width] = ref[at : at + UNIT].astype(F32)
        g_ao[layer] = ref[7 * UNIT : 8 * UNIT].astype(F32)
        for j in range(4):
            at = (8 + j) * UNIT
            g_in[layer, :, j * width : (j + 1) * width] = ref[at : at + UNIT].astype(F32)
    base = LAYER_UNITS * UNIT
    for j in range(4):
        at = base + j * UNIT
        g_proj[:, j * width : (j + 1) * width] = above[at : at + UNIT].astype(F32)
    small = below[base : base + 2 * UNIT, :128].astype(F32)
    for j in range(VECTORS):
        for i in range(layers):
            vectors[j][i : i + 1, :] = small[i * VECTORS + j : i * VECTORS + j + 1, :UNIT]
    count = VECTORS * layers
    vectors[VECTORS][...] = small[count : count + 1, :UNIT]
    vectors[VECTORS + 1][...] = small[count + 1 : count + 2, :UNIT]
    vectors[VECTORS + 2][...] = small[count + 2 : count + 2 + layers, : 4 * UNIT]


def unpack_grads(above, below, own, layers):
    width = above.shape[1]
    count = VECTORS * layers
    if own == UNIT:
        shapes = [
            (layers, own, 3 * width),
            (layers, own, width),
            (layers, own, 4 * width),
            (layers, 4 * own, width),
            (own, 4 * width),
        ]
        shapes += [(layers, own)] * VECTORS + [(1, own), (1, own), (layers, 4 * own)]
        outs = pl.pallas_call(
            lambda *refs: unpack_kernel(layers, *refs),
            out_shape=[jax.ShapeDtypeStruct(shape, F32) for shape in shapes],
            name="unpack",
        )(above, below)
        return outs[:5], outs[5:13], outs[13][0], outs[14][0], outs[15]
    parts = []
    for ref in (below, above):
        cuts, at = [], 0
        for rows in piece_rows(layers, own):
            cuts.append(ref[at : at + rows].astype(F32))
            at += rows
        parts.append(cuts)
    mats = [
        jnp.stack([jnp.concatenate(cuts[1:4], axis=1) for cuts in parts]),
        jnp.stack([cuts[4] for cuts in parts]),
        jnp.stack([jnp.concatenate(cuts[5:9], axis=1) for cuts in parts]),
        jnp.stack([cuts[0] for cuts in parts]),
        jnp.concatenate(
            [above[at + i * own : at + (i + 1) * own].astype(F32) for i in range(4)], axis=1
        ),
    ]
    small = below[at : at + 2 * UNIT, :128].astype(F32)
    vectors = [
        jnp.stack([small[i * VECTORS + j, :own] for i in range(layers)]) for j in range(VECTORS)
    ]
    inner_bias = small[count + 2 : count + 2 + layers, : 4 * own]
    return mats, vectors, small[count, :own], small[count + 1, :own], inner_bias


def pair_swap(values, bit):
    return swap(values, "tensor", bit)


def scatter_start(mine, other, first):
    held = mine.astype(F32) + pair_swap(other, 1).astype(F32)
    return held, held[1].astype(BF16)


def scatter_rest(held, sent, first, second):
    held = held[0] + swap(sent, *first).astype(F32)
    return held[0] + swap(held[1].astype(BF16), *second).astype(F32)


def next_on_line(values):
    size = lax.axis_size("dp")
    return lax.ppermute(values, "dp", [(i, (i + 2) % size) for i in range(size)])


def scatter_line(held):
    total = held[3]
    for ahead in (2, 1, 0):
        total = held[ahead] + next_on_line(total.astype(BF16)).astype(F32)
    return total


def gather_line(values):
    parts = [values]
    for _ in range(lax.axis_size("dp") // 2 - 1):
        parts.append(next_on_line(parts[-1]))
    return jnp.stack(parts)


def sum_grads(packed, rows_list, vector_rows):
    dp_size = lax.axis_size("dp")
    if dp_size == 8:
        x, y = ("dp", 1), ("tensor", 2)
        held_a, sent_a = scatter_start(packed[0], packed[1], y)
        held_b, sent_b = scatter_start(packed[2], packed[3], x)

        def rest():
            halves = [scatter_rest(held_a, sent_a, y, x), scatter_rest(held_b, sent_b, x, y)]
            return scatter_line(jnp.concatenate(halves, axis=1))

        return sent_b, rest
    packed_a = jnp.stack(packed[:2]).transpose(3, 2, 1, 0, 4, 5)
    packed_b = jnp.stack(packed[2:]).transpose(3, 1, 2, 0, 4, 5)
    packed = jnp.concatenate([packed_a, packed_b], axis=4)
    packed = packed.reshape((BLOCKS,) + packed.shape[4:])
    packed = to_devices(packed, 4 * dp_size, rows_list, vector_rows)
    summed = lax.psum_scatter(packed, BOTH, scatter_dimension=0, tiled=True)[0]
    return packed, lambda: summed


def dp_bits():
    size = lax.axis_size("dp")
    return [1 << i for i in range(size.bit_length() - 1)]


def dp_places():
    bits = dp_bits()
    return [
        sum(bit for i, bit in enumerate(reversed(bits)) if (place >> i) & 1)
        for place in range(lax.axis_size("dp"))
    ]


def gather_relative(values, first, last):
    for bit in list(reversed(dp_bits()))[first:last]:
        values = jnp.concatenate([values, swap(values, "dp", bit)])
    return values


def reduce_relative(keep, send):
    bits = dp_bits()
    keep = keep + swap(send, "dp", bits[0])
    for bit in bits[1:]:
        half = keep.shape[0] // 2
        keep = keep[:half] + swap(keep[half:], "dp", bit)
    return keep[0]


def exchange_relative(first, second, third):
    return [pair_swap(first, 1), pair_swap(second, 2), pair_swap(third, 3)]


def local(
    piece_table,
    piece_ids,
    piece_counts,
    text_ids,
    cotangent,
    rms_gain_one,
    w_query,
    w_key,
    w_value,
    w_output,
    rms_gain_two,
    w_gate,
    w_up,
    w_down,
    *shard_params,
):
    tensor_index = lax.axis_index("tensor")
    dp_index = lax.axis_index("dp")
    tensor_size = lax.axis_size("tensor")
    dp_size = lax.axis_size("dp")
    devices = tensor_size * dp_size
    micro_count, group_entries, slot_count = piece_ids.shape
    own_entries = group_entries // tensor_size
    seq_length = text_ids.shape[1]
    share = cotangent.shape[1]
    layer_count, own, _ = shard_params[2].shape
    width = shard_params[5].shape[2]
    lm_width = cotangent.shape[2]
    table_rows, table_cols = piece_table.shape
    gain_first = rms_gain_one[None, :]
    gain_second = rms_gain_two[None, :]
    cosine, sine = rotary_tables(seq_length)
    trig = jnp.concatenate([cosine.T, sine.T], axis=0)
    w_kv = jnp.concatenate([w_key, w_value], axis=1)

    where = tensor_index.astype(jnp.int32)[None]

    gathered = lax.all_gather(pack_shards(shard_params), BOTH, axis=0)

    stages = len(dp_bits())
    ids_rel = gather_relative(piece_ids[None], 0, stages)
    ids_rel = ids_rel.reshape(dp_size, micro_count, tensor_size, own_entries, slot_count)
    ids_rel = jnp.take(ids_rel, tensor_index ^ jnp.arange(tensor_size), axis=2)
    ids_rel = ids_rel.transpose(0, 2, 1, 3, 4) - dp_index * table_rows
    places = jnp.asarray(dp_places())
    ids_back = jnp.zeros_like(ids_rel).at[dp_index ^ places].set(ids_rel)
    if dp_size == 8:
        behind = (dp_index + dp_size - 2 * jnp.arange(dp_size // 2)) % dp_size
        ids_back = jnp.take(ids_back, jnp.concatenate([behind, behind ^ 1]), axis=0)
    ids_back = ids_back.reshape(2, -1)
    ids_rel = ids_rel.reshape(2, -1)
    own_rows = micro_count * own_entries * slot_count
    looked = [
        lookup(ids_rel[i], piece_table).reshape(dp_size // 2, tensor_size, own_rows, table_cols)
        for i in (1, 0)
    ]
    looked = reduce_relative(looked[1], looked[0])
    pieces = [looked[0], *exchange_relative(*looked[1:])]

    packed, vectors, inner_bias = canonical(gathered, own, layer_count)
    counts_own = lax.dynamic_slice_in_dim(piece_counts, tensor_index * own_entries, own_entries, 1)
    valid = jnp.arange(slot_count)[None, :] < counts_own.reshape(-1)[:, None]
    valid = valid.astype(F32).reshape(1, own_rows)
    w_out = [w_output, pair_swap(w_output, 1), pair_swap(w_output, 2)]
    *kept_hyper, pooled, pooled_norm, embeds = hyper_forward(
        where, w_out[2], pieces, valid, vectors, inner_bias, packed, slot_count
    )

    w_out.append(pair_swap(w_out[2], 1))
    embeds = embeds.reshape(micro_count, own_entries, lm_width)
    embeds = [embeds, pair_swap(embeds, 1), pair_swap(embeds, 2)]
    embeds.append(pair_swap(embeds[2], 1))
    text_rel = text_ids ^ (tensor_index * own_entries)

    micros = range(micro_count)
    ids_row, ids_own, ids_peer = [], [], []
    for micro in micros:
        row = text_rel[micro][None, :]
        ids_row.append(row)
        ids_own.append(lax.dynamic_slice_in_dim(row, tensor_index * share, share, 1))
        ids_peer.append(lax.dynamic_slice_in_dim(row, (tensor_index ^ 2) * share, share, 1))

    def cots_of(micro, after):
        own = cast_after(micro, cotangent, after)
        peer = pair_swap(own, 2)
        return (own, pair_swap(own, 1)), (peer, pair_swap(peer, 1))

    kept_attn, contexts = [], []
    after = (embeds[0], embeds[0])
    cots_near, cots_peer = cots_of(0, embeds[3])
    for micro in micros:
        near, far, *kept = attend(
            where, micro, embeds, gain_first, w_query, w_kv, ids_row[micro], trig, after
        )
        kept_attn.append(kept)
        contexts.append([near, *exchange_relative(far, near, far)])
        after = (near, cots_peer[0])

    def after_attention(micro, after):
        own, peer, rows = hidden_rows_of(
            kept_attn[micro][-1], ids_own[micro], ids_peer[micro], gain_second,
            contexts[micro], w_out, after,
        )
        return (own, pair_swap(own, 1)), (peer, pair_swap(peer, 1)), rows

    def feed_forward(normed, cots, *after):
        after = (after + after[:1] * 2)[:3]
        return mlp(*normed, *cots, w_gate, w_up, w_down, after)

    def travel(part):
        away = (part[2].astype(F32) + pair_swap(part[3], 1).astype(F32)).astype(BF16)
        return away, pair_swap(away, 2)

    def back_of(micro, rows, near, arrived):
        low, *parts = hidden_back(
            micro, cotangent, rows, near[2], pair_swap(near[3], 1), arrived, gain_second, w_out
        )
        return low, [parts[0], *exchange_relative(*parts[1:])]

    def result_of(rows, near, peer, after):
        away = add_after(peer[0], pair_swap(peer[1], 1), after)
        total = rows + near[0].astype(F32) + pair_swap(near[1], 1).astype(F32)
        return (total + pair_swap(away, 2).astype(F32)).astype(BF16)

    near_in, peer_in, rows_a = after_attention(0, (contexts[1][0], contexts[1][0]))
    near_a = feed_forward(near_in, cots_near, rows_a)
    cots_near_b, cots_peer_b = cots_of(1, near_a[2])
    peer_a = feed_forward(peer_in, cots_peer, near_a[2], contexts[1][2], contexts[1][3])
    away_a, arrived_a = travel(peer_a)
    near_in, peer_in, rows_b = after_attention(1, (away_a, cots_peer_b[0]))
    out_a = result_of(rows_a, near_a, peer_a, rows_b)
    peer_b = feed_forward(peer_in, cots_peer_b, rows_b)
    away_b, arrived_b = travel(peer_b)
    low_a, parts_a = back_of(0, rows_a, near_a, arrived_a)
    near_b = feed_forward(near_in, cots_near_b, low_a, out_a, away_b)
    low_b, parts_b = back_of(1, rows_b, near_b, arrived_b)
    out_b = result_of(rows_b, near_b, peer_b, low_b)

    place = jnp.stack([tensor_index % 2, tensor_index // 2, dp_index % 2, dp_index // 2])
    place = place.astype(jnp.int32)
    grad_embeds = []
    after = (low_b, low_b, low_b)
    for micro, parts, low in ((0, parts_a, low_a), (1, parts_b, low_b)):
        grads = attend_back(
            where, parts, kept_attn[micro], ids_row[micro], ids_own[micro], trig,
            w_query, w_kv, gain_first, low, after,
        )
        after = (grads, out_b, out_b)
        grads = grads.reshape(2, 2, own_entries, lm_width)
        arrived = pair_swap(grads[:, 1], 1).astype(F32) + grads[:, 0].astype(F32)
        arrived = arrived[0] + pair_swap(arrived[1].astype(BF16), 2).astype(F32)
        grad_embeds.append(arrived.astype(BF16))

    if dp_size != 8:
        place = place * 0
    source = (jnp.concatenate(grad_embeds, axis=0), pooled, pooled_norm)
    above, after = (), pooled
    rest = [None] * layer_count
    for layer in range(layer_count - 1, -1, -1):
        *parts, source, small, inner_small = hyper_backward(
            place, layer, source, valid, vectors, kept_hyper, packed, slot_count, above,
            table_cols, after,
        )
        above = (small, inner_small)
        rows_list = piece_rows(layer_count, UNIT) + ([UNIT] * 4 if layer == layer_count - 1 else [])
        after, rest[layer] = sum_grads(parts, rows_list, 2 * UNIT if layer == 0 else 0)
    reduced = [part() for part in rest]

    if dp_size != 8:
        source = jnp.take(source, tensor_index ^ jnp.arange(tensor_size), axis=0)
    arrived = jnp.stack([source[0], *exchange_relative(*source[1:])])
    if dp_size == 8:
        arrived = gather_line(arrived)
        halves = [arrived, swap(arrived, "dp", 1)]
    else:
        halves = jnp.split(lax.all_gather(arrived, "dp", axis=0), 2)
    table_grad = None
    for ids, rows in zip(ids_back, halves):
        table_grad = collect(ids, rows.reshape(-1, table_cols), table_rows, table_grad)

    mats, vecs, out_final_gain, out_final_bias, out_inner_bias = unpack_grads(
        reduced[1], reduced[0], own, layer_count
    )
    return (
        jnp.stack([out_a, out_b]),
        table_grad,
        vecs[0],
        vecs[1],
        mats[0],
        vecs[2],
        vecs[3],
        mats[1],
        vecs[4],
        vecs[5],
        vecs[6],
        mats[2],
        out_inner_bias,
        mats[3],
        vecs[7],
        out_final_gain,
        out_final_bias,
        mats[4],
    )


def solution(mesh):
    return jax.shard_map(
        local,
        mesh=mesh,
        in_specs=(
            P("dp", "tensor"),
            P(None, "dp", None),
            P(None, "dp"),
            P(None, "dp"),
            P(None, ("dp", "tensor"), None),
            P(),
            P(None, "tensor"),
            P(None, "tensor"),
            P(None, "tensor"),
            P("tensor", None),
            P(),
            P(None, "tensor"),
            P(None, "tensor"),
            P("tensor", None),
            P(None, ("dp", "tensor")),
            P(None, ("dp", "tensor")),
            P(None, ("dp", "tensor"), None),
            P(None, ("dp", "tensor")),
            P(None, ("dp", "tensor")),
            P(None, ("dp", "tensor"), None),
            P(None, ("dp", "tensor")),
            P(None, ("dp", "tensor")),
            P(None, ("dp", "tensor")),
            P(None, ("dp", "tensor"), None),
            P(None, ("dp", "tensor")),
            P(None, ("dp", "tensor"), None),
            P(None, ("dp", "tensor")),
            P(("dp", "tensor")),
            P(("dp", "tensor")),
            P(("dp", "tensor"), None),
        ),
        out_specs=(
            P(None, ("dp", "tensor"), None),
            P("dp", "tensor"),
            P(None, ("dp", "tensor")),
            P(None, ("dp", "tensor")),
            P(None, ("dp", "tensor"), None),
            P(None, ("dp", "tensor")),
            P(None, ("dp", "tensor")),
            P(None, ("dp", "tensor"), None),
            P(None, ("dp", "tensor")),
            P(None, ("dp", "tensor")),
            P(None, ("dp", "tensor")),
            P(None, ("dp", "tensor"), None),
            P(None, ("dp", "tensor")),
            P(None, ("dp", "tensor"), None),
            P(None, ("dp", "tensor")),
            P(("dp", "tensor")),
            P(("dp", "tensor")),
            P(("dp", "tensor"), None),
        ),
        check_vma=False,
    )
```

time: 1320 us -> 692 us (0.52)
  matrix products: 460 us -> 0 us
  Pallas kernels: 43.4 us -> 352 us
  waiting for transfers between devices: 375 us -> 186 us
  local copies, waits for them, and re-layouts: 193 us -> 33 us
  other arithmetic: 167 us -> 36.4 us
  starting transfers between devices: 39.2 us -> 59.8 us
  blocking collectives: 15 us -> 0 us
    dot_general x105 -> x0, matrix products: 460 us -> none  [the longest x31 117 us: matmul_right_t(): lax.dot_general(left, right, (((1,), (1,)), ((), ())), preferred_element_...]
    pallas_call x1 -> x23, Pallas kernels: 21.7 us -> 330 us  [the longest x4 107 us: mlp(): pl.pallas_call(mlp_kernel, in_specs=[vmem] * 4 + [ANY_SPEC] * 6, out_spec...]
    ppermute x51 -> x69, waiting for transfers between devices: 234 us -> 123 us  [swap(): return lax.ppermute(values, axis, [(i, i ^ bit) for i in range(size)])]
    another operation x40 -> x4, other arithmetic: 84.4 us -> 2.27 us  [the longest x1 1.5 us: local(): jnp.stack([out_a, out_b])]
    all_to_all x1 -> x0, waiting for transfers between devices: 71.9 us -> none  [local(): lax.all_to_all(looked, BOTH, split_axis=0, concat_axis=0, tiled=True)]
    unnamed x620 -> x130, local copies, waits for them, and re-layouts: 68.1 us -> 15.8 us
    reduce_scatter x1 -> x0, waiting for transfers between devices: 47.8 us -> none  [local(): lax.psum_scatter(jnp.concatenate(pieces, axis=1), BOTH, scatter_dimension...]
    reduce_sum x22 -> x0, other arithmetic: 43.6 us -> none  [the longest x2 28.4 us: local(): row_total = jnp.sum(expon, axis=-1, keepdims=True)]
  transfers between devices with their start and end apart: 54 -> 79, of which waited for: 25 -> 33; matrix products, arithmetic and copies ran while one was open for 37% -> 8% of each run, Pallas kernels for 3% -> 44%
where the time goes in v2:
time: 692 us; the launch traced here: 682 us
  Pallas kernels  352 us (51%)
  waiting for transfers between devices  186 us (27%)
  starting transfers between devices  59.8 us (9%)
  other arithmetic  36.4 us (5%)
  local copies, waits for them, and re-layouts  33 us (5%)
  between operations  15.5 us (2%)
    ppermute x69, waiting for transfers between devices, swap(): return lax.ppermute(values, axis, [(i, i ^ bit) for i in range(size)])  123 us
    pallas_call x4, Pallas kernels, mlp(): pl.pallas_call(mlp_kernel, in_specs=[vmem] * 4 + [ANY_SPEC] * 6, out_spec...  107 us
    ppermute x69, starting transfers between devices, swap(): return lax.ppermute(values, axis, [(i, i ^ bit) for i in range(size)])  52.1 us
    pallas_call x2, Pallas kernels, attend_back(): pl.pallas_call(attend_back_kernel, grid=(pairs,), in_specs=[pl.BlockSpec(...  51.6 us
    pallas_call x2, Pallas kernels, attend(): pl.pallas_call(attend_kernel, grid=(pairs,), in_specs=[pl.BlockSpec(memor...  41.5 us
    pallas_call x2, Pallas kernels, hyper_backward(): pl.pallas_call(lambda *refs: hyper_back_kernel(slots, layer, layers, last...  35.4 us
    ppermute x9, waiting for transfers between devices, next_on_line(): lax.ppermute(values, 'dp', [(i, (i + 2) % size) for i in range(size)])  33.5 us
    all_gather x1, waiting for transfers between devices, local(): gathered = lax.all_gather(pack_shards(shard_params), BOTH, axis=0)  29.3 us
  transfers between devices with their start and end apart: 79, of which 33 were waited for; matrix products, arithmetic and copies ran while one was open for 8% of the time, Pallas kernels for 44%

profile of v2, /device:TPU:0, one launch (start us, length us, event | category | flops | bytes accessed | tf_op | source)
XLA Modules:
  0.0 682.3 jit_solution(7386243545891039160)
XLA Ops:
  26.6 11.1 %lookup.3 = bf16[4096,128]{1,0:T(8,128)(2,1)} custom-call(s32[4096,1]{1,0:T(8,128)S(1)} %broadcast_in_dim_squeeze.9.ids_ref, bf16[4096,128]{1,0:T(8,128)(2,1)S(1)} %copy-done.2), custom_call_target="tpu_custom_call" | custom-call | flops 8589934592 | bytes 2097152 | tf_op jit(solution)/shard_map/lookup/pallas_call | solution.py:79
  41.9 10.4 %lookup.2 = bf16[4096,128]{1,0:T(8,128)(2,1)S(1)} custom-call(s32[4096,1]{1,0:T(8,128)S(1)} %broadcast_in_dim_squeeze.8.ids_ref, bf16[4096,128]{1,0:T(8,128)(2,1)S(1)} %copy-done.2), custom_call_target="tpu_custom_call" | custom-call | flops 8589934592 | bytes 2097152 | tf_op jit(solution)/shard_map/lookup/pallas_call | solution.py:79
  52.3 21.5 %collective-permute-done.4 = bf16[4,4,256,128]{3,2,1,0:T(8,128)(2,1)} collective-permute-done((bf16[4,4,256,128]{3,2,1,0:T(8,128)(2,1)}, bf16[4,4,256,128]{3,2,1,0:T(8,128)(2,1)}, u32[]{:S(2)}, u32[]{:S(2)}) %collective-permute-start.4) | collective-permute-done | bytes 1048608 | tf_op jit(solution)/shard_map/ppermute | solution.py:64
  77.3 11.9 %collective-permute-done.5 = bf16[2,4,256,128]{3,2,1,0:T(8,128)(2,1)S(1)} collective-permute-done((bf16[2,4,256,128]{3,2,1,0:T(8,128)(2,1)S(1)}, bf16[2,4,256,128]{3,2,1,0:T(8,128)(2,1)S(1)}, u32[]{:S(2)}, u32[]{:S(2)}) %collective-permute-start.5) | collective-permute-done | bytes 524320 | tf_op jit(solution)/shard_map/ppermute | solution.py:64
  96.4 18.4 %collective-permute-done.6 = bf16[1,4,256,128]{3,2,1,0:T(8,128)(2,1)S(1)} collective-permute-done((bf16[1,4,256,128]{3,2,1,0:T(8,128)(2,1)S(1)}, bf16[1,4,256,128]{3,2,1,0:T(8,128)(2,1)S(1)}, u32[]{:S(2)}, u32[]{:S(2)}) %collective-permute-start.6) | collective-permute-done | bytes 262176 | tf_op jit(solution)/shard_map/ppermute | solution.py:64
  117.3 29.3 %all-gather.3.cloned.1.call-done = bf16[15360,512]{1,0:T(8,128)(2,1)} async-done(((bf16[480,512]{1,0:T(8,128)(2,1)}), bf16[15360,512]{1,0:T(8,128)(2,1)}) %all-gather.3.cloned.1.call-update) | async-done | bytes 15728656 | tf_op jit(solution)/shard_map/all_gather | solution.py:1234
  150.6 16.3 %hyper.1 = (f32[2,256,512]{2,1,0:T(8,128)}, bf16[2,256,1536]{2,1,0:T(8,128)(2,1)}, bf16[2,256,512]{2,1,0:T(8,128)(2,1)}, f32[2,256,512]{2,1,0:T(8,128)}, f32[2,2...) custom-call(s32[1]{0:T(128)} %bitcast.refs_0_.place, ...), custom_call_target="tpu_custom_call" | custom-call | flops 8000000000 | bytes 25000000 | tf_op jit(solution)/shard_map/hyper/pallas_call | solution.py:700
  181.6 20.7 %attend.2 = (bf16[2,256,512]{2,1,0:T(8,128)(2,1)}, bf16[2,256,512]{2,1,0:T(8,128)(2,1)}, bf16[512,1024]{1,0:T(8,128)(2,1)}, f32[4,2,1024]{2,1,0:T(2,128)}, bf16[...) custom-call(s32[1]{0:T(128)} %bitcast.refs_0_.place, ...), custom_call_target="tpu_custom_call" | custom-call | flops 12000000000 | bytes 8000000 | tf_op jit(solution)/shard_map/attend/pallas_call | solution.py:228
  206.4 20.8 %attend.3 = (bf16[2,256,512]{2,1,0:T(8,128)(2,1)}, bf16[2,256,512]{2,1,0:T(8,128)(2,1)}, bf16[512,1024]{1,0:T(8,128)(2,1)}, f32[4,2,1024]{2,1,0:T(2,128)}, bf16[...) custom-call(s32[1]{0:T(128)} %bitcast.refs_0_.place, ...), custom_call_target="tpu_custom_call" | custom-call | flops 12000000000 | bytes 8000000 | tf_op jit(solution)/shard_map/attend/pallas_call | solution.py:228
  229.2 11.1 %hidden.2 = (bf16[256,2048]{1,0:T(8,128)(2,1)}, bf16[256,2048]{1,0:T(8,128)(2,1)}, f32[256,2048]{1,0:T(8,128)}) custom-call(bf16[64,2048]{1,0:T(8,128)(2,1)} %get-tuple-element.101.embeds, s32[1,256]{1,0:T(1,128)} %get-tuple-element.201.ids_own.ids_share, s32[1,256]{1,0:T(1,128)} %get-tuple-element.200.ids_peer, bf16[1,2048]{1,0:T(2,128)(2,1)} %broadcast_in_dim.54.gain, ...), custom_call_target="tpu_custom_call" | custom-call | flops 6000000000 | bytes 18000000 | tf_op jit(solution)/shard_map/hidden/pallas_call | solution.py:437
  244.3 26.7 %mlp.4 = (bf16[256,2048]{1,0:T(8,128)(2,1)}, bf16[256,2048]{1,0:T(8,128)(2,1)}, bf16[256,2048]{1,0:T(8,128)(2,1)}, bf16[256,2048]{1,0:T(8,128)(2,1)}) custom-call(bf16[256,2048]{1,0:T(8,128)(2,1)} %get-tuple-element.106.x_mine, bf16[256,2048]{1,0:T(8,128)(2,1)} %copy-done.47, bf16[256,2048]{1,0:T(8,128)(2,1)} %cast_after.2.grad_mine_in, ...), custom_call_target="tpu_custom_call" | custom-call | flops 17716740096 | bytes 26000000 | tf_op jit(solution)/shard_map/mlp/pallas_call | solution.py:529
  276.6 26.7 %mlp.5 = (bf16[256,2048]{1,0:T(8,128)(2,1)}, bf16[256,2048]{1,0:T(8,128)(2,1)}, bf16[256,2048]{1,0:T(8,128)(2,1)}, bf16[256,2048]{1,0:T(8,128)(2,1)}) custom-call(bf16[256,2048]{1,0:T(8,128)(2,1)} %get-tuple-element.109.x_mine, bf16[256,2048]{1,0:T(8,128)(2,1)} %copy-done.45, bf16[256,2048]{1,0:T(8,128)(2,1)} %copy-done.40, bf16[256,2048]{1,0:T(8,128)(2,1)} %copy-done.46, ...), custom_call_target="tpu_custom_call" | custom-call | flops 17716740096 | bytes 26000000 | tf_op jit(solution)/shard_map/mlp/pallas_call | solution.py:529
  309.5 11.1 %hidden.3 = (bf16[256,2048]{1,0:T(8,128)(2,1)}, bf16[256,2048]{1,0:T(8,128)(2,1)}, f32[256,2048]{1,0:T(8,128)}) custom-call(bf16[64,2048]{1,0:T(8,128)(2,1)} %get-tuple-element.114.embeds, s32[1,256]{1,0:T(1,128)} %get-tuple-element.203.ids_own.ids_share, s32[1,256]{1,0:T(1,128)} %get-tuple-element.202.ids_peer, bf16[1,2048]{1,0:T(2,128)(2,1)} %broadcast_in_dim.54.gain, ...), custom_call_target="tpu_custom_call" | custom-call | flops 6000000000 | bytes 18000000 | tf_op jit(solution)/shard_map/hidden/pallas_call | solution.py:437
  326.1 26.8 %mlp.6 = (bf16[256,2048]{1,0:T(8,128)(2,1)}, bf16[256,2048]{1,0:T(8,128)(2,1)}, bf16[256,2048]{1,0:T(8,128)(2,1)}, bf16[256,2048]{1,0:T(8,128)(2,1)}) custom-call(bf16[256,2048]{1,0:T(8,128)(2,1)} %get-tuple-element.121.x_mine, bf16[256,2048]{1,0:T(8,128)(2,1)} %collective-permute-done.35.x_other, ...), custom_call_target="tpu_custom_call" | custom-call | flops 17716740096 | bytes 26000000 | tf_op jit(solution)/shard_map/mlp/pallas_call | solution.py:529
  354.5 9.8 %hidden_back.2 = (bf16[256,2048]{1,0:T(8,128)(2,1)}, bf16[256,512]{1,0:T(8,128)(2,1)}, bf16[256,512]{1,0:T(8,128)(2,1)}, bf16[256,512]{1,0:T(8,128)(2,1)}, bf16[256,512]{1,0:T(8,128)(2,1)}) custom-call(f32[2,256,2048]{2,1,0:T(8,128)} %cotangent.3, f32[256,2048]{1,0:T(8,128)} %get-tuple-element.105._after_one._after_two._after_three.hidden, ...), custom_call_target="tpu_custom_call" | custom-call | flops 2000000000 | bytes 16000000 | tf_op jit(solution)/shard_map/hidden_back/pallas_call | solution.py:472
  375.1 26.8 %mlp.7 = (bf16[256,2048]{1,0:T(8,128)(2,1)}, bf16[256,2048]{1,0:T(8,128)(2,1)}, bf16[256,2048]{1,0:T(8,128)(2,1)}, bf16[256,2048]{1,0:T(8,128)(2,1)}) custom-call(bf16[256,2048]{1,0:T(8,128)(2,1)} %get-tuple-element.118.x_mine, bf16[256,2048]{1,0:T(8,128)(2,1)} %copy-done.44, bf16[256,2048]{1,0:T(8,128)(2,1)} %cast_after.3.grad_mine_in, ...), custom_call_target="tpu_custom_call" | custom-call | flops 17716740096 | bytes 26000000 | tf_op jit(solution)/shard_map/mlp/pallas_call | solution.py:529
  406.4 9.7 %hidden_back.3 = (bf16[256,2048]{1,0:T(8,128)(2,1)}, bf16[256,512]{1,0:T(8,128)(2,1)}, bf16[256,512]{1,0:T(8,128)(2,1)}, bf16[256,512]{1,0:T(8,128)(2,1)}, bf16[256,512]{1,0:T(8,128)(2,1)}) custom-call(f32[2,256,2048]{2,1,0:T(8,128)} %cotangent.3, f32[256,2048]{1,0:T(8,128)} %get-tuple-element.117._after._after_one._after_two._after_three.hidden, ...), custom_call_target="tpu_custom_call" | custom-call | flops 2000000000 | bytes 16000000 | tf_op jit(solution)/shard_map/hidden_back/pallas_call | solution.py:472
  421.7 25.7 %attend_back.2._after_one = bf16[64,2048]{1,0:T(8,128)(2,1)} custom-call(s32[1]{0:T(128)} %bitcast.refs_0_.place, bf16[256,512]{1,0:T(8,128)(2,1)} %get-tuple-element.131.part0, bf16[256,512]{1,0:T(8,128)(2,1)} %copy-done.55, bf16[256,512]{1,0:T(8,128)(2,1)} %copy-done.56, bf16[256,512]{1,0:T(8,128)(2,1)} %copy-done.57, ...), custom_call_target="tpu_custom_call" | custom-call | flops 24999999488 | bytes 8000000 | tf_op jit(solution)/shard_map/attend_back/pallas_call | solution.py:368
  463.4 25.8 %attend_back.3 = bf16[64,2048]{1,0:T(8,128)(2,1)} custom-call(s32[1]{0:T(128)} %bitcast.refs_0_.place, bf16[256,512]{1,0:T(8,128)(2,1)} %get-tuple-element.139.part0, bf16[256,512]{1,0:T(8,128)(2,1)} %copy-done.58, bf16[256,512]{1,0:T(8,128)(2,1)} %copy-done.59, bf16[256,512]{1,0:T(8,128)(2,1)} %copy-done.60, ...), custom_call_target="tpu_custom_call" | custom-call | flops 24999999488 | bytes 8000000 | tf_op jit(solution)/shard_map/attend_back/pallas_call | solution.py:368
  498.1 18.7 %hyper_back.2 = (bf16[2,2,4,128,512]{4,3,2,1,0:T(8,128)(2,1)}, bf16[2,2,4,128,512]{4,3,2,1,0:T(8,128)(2,1)}, bf16[2,2,4,128,512]{4,3,2,1,0:T(8,128)(2,1)}, bf16[...) custom-call(s32[4]{0:T(128)} %pad_add_fusion.3.refs_0_, ...), custom_call_target="tpu_custom_call" | custom-call | flops 8000000000 | bytes 25000000 | tf_op jit(solution)/shard_map/hyper_back/pallas_call | solution.py:928
  526.8 16.7 %hyper_back.3 = (bf16[2,2,4,112,512]{4,3,2,1,0:T(8,128)(2,1)}, bf16[2,2,4,112,512]{4,3,2,1,0:T(8,128)(2,1)}, bf16[2,2,4,112,512]{4,3,2,1,0:T(8,128)(2,1)}, bf16[...) custom-call(s32[4]{0:T(128)} %pad_add_fusion.3.refs_0_, ...), custom_call_target="tpu_custom_call" | custom-call | flops 8000000000 | bytes 25000000 | tf_op jit(solution)/shard_map/hyper_back/pallas_call | solution.py:928
  578.0 10.4 %collect.2.base_ref = f32[4096,128]{1,0:T(8,128)S(1)} custom-call(s32[1,4096]{1,0:T(1,128)S(1)} %unstack.61.ids_ref, bf16[4096,128]{1,0:T(8,128)(2,1)S(1)} %bitcast.206), custom_call_target="tpu_custom_call" | custom-call | flops 8589934592 | bytes 2097152 | tf_op jit(solution)/shard_map/collect/pallas_call | solution.py:114
  614.5 12.3 %collective-permute-done.70 = bf16[2,4,112,512]{3,2,1,0:T(8,128)(2,1)S(1)} collective-permute-done((bf16[2,4,112,512]{3,2,1,0:T(8,128)(2,1)S(1)}, bf16[2,4,112,512]{3,2,1,0:T(8,128)(2,1)S(1)}, u32[]{:S(2)}, u32[]{:S(2)}) %collective-permute-start.70) | collective-permute-done | bytes 917536 | tf_op jit(solution)/shard_map/ppermute | solution.py:64
  652.8 11.6 %collect.3 = f32[4096,128]{1,0:T(8,128)} custom-call(s32[1,4096]{1,0:T(1,128)S(1)} %unstack.53.ids_ref, bf16[4096,128]{1,0:T(8,128)(2,1)S(1)} %bitcast.207, f32[4096,128]{1,0:T(8,128)S(1)} %collect.2.base_ref), custom_call_target="tpu_custom_call" | custom-call | flops 8589934592 | bytes 2097152 | tf_op jit(solution)/shard_map/collect/pallas_call | solution.py:114
  (400 shorter events, 236.7 us)
Async XLA Ops:
  7.2 139.4 %all-gather.3.cloned.1.call-start = ((), (), s32[]{:S(2)}) async-start(), calls=%async_computation | async-start | bytes 16220160 | tf_op jit(solution)/shard_map/all_gather | solution.py:1234
  37.7 36.1 %collective-permute-start.4 = (bf16[4,4,256,128]{3,2,1,0:T(8,128)(2,1)}, bf16[4,4,256,128]{3,2,1,0:T(8,128)(2,1)}, u32[]{:S(2)}, u32[]{:S(2)}) collective-permute-start(bf16[4,4,256,128]{3,2,1,0:T(8,128)(2,1)} %bitcast.5), channel_id=1, source_target_pairs={{0,4},{4,0},{8,12},{12,8},{16,20},{20,16},{24,28},{28,24},{1,5},{5... | collective-permute-start | bytes 3145736 | tf_op jit(solution)/shard_map/ppermute | solution.py:64
  39.8 187.4 %collective-permute-start.16 = (bf16[512,2048]{1,0:T(8,128)(2,1)}, bf16[512,2048]{1,0:T(8,128)(2,1)}, u32[]{:S(2)}, u32[]{:S(2)}) collective-permute-start(bf16[512,2048]{1,0:T(8,128)(2,1)} %w0.7), channel_id=1, source_target_pairs={{0,1},{1,0},{2,3},{3,2},{4,5},{5,4},{6,7},{7,6},{8,9},{9,8},{10,11... | collective-permute-start | bytes 6291464 | tf_op jit(solution)/shard_map/ppermute | solution.py:64
  39.8 110.2 %collective-permute-start = (bf16[512,2048]{1,0:T(8,128)(2,1)}, bf16[512,2048]{1,0:T(8,128)(2,1)}, u32[]{:S(2)}, u32[]{:S(2)}) collective-permute-start(bf16[512,2048]{1,0:T(8,128)(2,1)} %w0.7), channel_id=1, source_target_pairs={{0,2},{1,3},{2,0},{3,1},{4,6},{5,7},{6,4},{7,5},{8,10},{9,11},{10,... | collective-permute-start | bytes 6291464 | tf_op jit(solution)/shard_map/ppermute | solution.py:64
  115.4 34.5 %collective-permute-start.9 = (bf16[256,128]{1,0:T(8,128)(2,1)S(1)}, bf16[256,128]{1,0:T(8,128)(2,1)S(1)}, u32[]{:S(2)}, u32[]{:S(2)}) collective-permute-start(bf16[256,128]{1,0:T(8,128)(2,1)S(1)} %get-tuple-element.190), channel_id=1, source_target_pairs={{0,3},{1,2},{2,1},{3,0},{4,7},{5,6},{6,5},{7,4},{8,11},{9,10},{10,... | collective-permute-start | bytes 196616 | tf_op jit(solution)/shard_map/ppermute | solution.py:64
  115.4 34.5 %collective-permute-start.8 = (bf16[256,128]{1,0:T(8,128)(2,1)S(1)}, bf16[256,128]{1,0:T(8,128)(2,1)S(1)}, u32[]{:S(2)}, u32[]{:S(2)}) collective-permute-start(bf16[256,128]{1,0:T(8,128)(2,1)S(1)} %get-tuple-element.191), channel_id=1, source_target_pairs={{0,2},{1,3},{2,0},{3,1},{4,6},{5,7},{6,4},{7,5},{8,10},{9,11},{10,... | collective-permute-start | bytes 196616 | tf_op jit(solution)/shard_map/ppermute | solution.py:64
  116.9 33.1 %collective-permute-start.7 = (bf16[256,128]{1,0:T(8,128)(2,1)S(1)}, bf16[256,128]{1,0:T(8,128)(2,1)S(1)}, u32[]{:S(2)}, u32[]{:S(2)}) collective-permute-start(bf16[256,128]{1,0:T(8,128)(2,1)S(1)} %get-tuple-element.192), channel_id=1, source_target_pairs={{0,1},{1,0},{2,3},{3,2},{4,5},{5,4},{6,7},{7,6},{8,9},{9,8},{10,11... | collective-permute-start | bytes 196616 | tf_op jit(solution)/shard_map/ppermute | solution.py:64
  175.5 51.8 %collective-permute-start.17 = (bf16[512,2048]{1,0:T(8,128)(2,1)}, bf16[512,2048]{1,0:T(8,128)(2,1)S(1)}, u32[]{:S(2)}, u32[]{:S(2)}) collective-permute-start(bf16[512,2048]{1,0:T(8,128)(2,1)} %collective-permute-done.refs_1_.w2), channel_id=1, source_target_pairs={{0,1},{1,0},{2,3},{3,2},{4,5},{5,4},{6,7},{7,6},{8,9},{9,8},{10,11... | collective-permute-start | bytes 6291464 | tf_op jit(solution)/shard_map/ppermute | solution.py:64
  240.8 33.9 %collective-permute-start.24 = (bf16[2,256,512]{2,1,0:T(8,128)(2,1)}, bf16[2,256,512]{2,1,0:T(8,128)(2,1)}, u32[]{:S(2)}, u32[]{:S(2)}) collective-permute-start(bf16[2,256,512]{2,1,0:T(8,128)(2,1)} %get-tuple-element.104._after_one._after_two.c0), channel_id=1, source_target_pairs={{0,2},{1,3},{2,0},{3,1},{4,6},{5,7},{6,4},{7,5},{8,10},{9,11},{10,... | collective-permute-start | bytes 1572872 | tf_op jit(solution)/shard_map/ppermute | solution.py:64
  241.8 32.9 %collective-permute-start.25 = (bf16[2,256,512]{2,1,0:T(8,128)(2,1)}, bf16[2,256,512]{2,1,0:T(8,128)(2,1)}, u32[]{:S(2)}, u32[]{:S(2)}) collective-permute-start(bf16[2,256,512]{2,1,0:T(8,128)(2,1)} %get-tuple-element.111), channel_id=1, source_target_pairs={{0,3},{1,2},{2,1},{3,0},{4,7},{5,6},{6,5},{7,4},{8,11},{9,10},{10,... | collective-permute-start | bytes 1572872 | tf_op jit(solution)/shard_map/ppermute | solution.py:64
  242.2 32.5 %collective-permute-start.22 = (bf16[256,2048]{1,0:T(8,128)(2,1)}, bf16[256,2048]{1,0:T(8,128)(2,1)S(1)}, u32[]{:S(2)}, u32[]{:S(2)}) collective-permute-start(bf16[256,2048]{1,0:T(8,128)(2,1)} %get-tuple-element.109.x_mine), channel_id=1, source_target_pairs={{0,1},{1,0},{2,3},{3,2},{4,5},{5,4},{6,7},{7,6},{8,9},{9,8},{10,11... | collective-permute-start | bytes 3145736 | tf_op jit(solution)/shard_map/ppermute | solution.py:64
  242.9 31.7 %collective-permute-start.23 = (bf16[256,2048]{1,0:T(8,128)(2,1)S(1)}, bf16[256,2048]{1,0:T(8,128)(2,1)S(1)}, u32[]{:S(2)}, u32[]{:S(2)}) collective-permute-start(bf16[256,2048]{1,0:T(8,128)(2,1)S(1)} %copy-done.41), channel_id=1, source_target_pairs={{0,1},{1,0},{2,3},{3,2},{4,5},{5,4},{6,7},{7,6},{8,9},{9,8},{10,11... | collective-permute-start | bytes 3145736 | tf_op jit(solution)/shard_map/ppermute | solution.py:64
  273.7 30.8 %collective-permute-start.29 = (bf16[256,2048]{1,0:T(8,128)(2,1)}, bf16[256,2048]{1,0:T(8,128)(2,1)}, u32[]{:S(2)}, u32[]{:S(2)}) collective-permute-start(bf16[256,2048]{1,0:T(8,128)(2,1)} %cast_after.3.grad_mine_in), channel_id=1, source_target_pairs={{0,2},{1,3},{2,0},{3,1},{4,6},{5,7},{6,4},{7,5},{8,10},{9,11},{10,... | collective-permute-start | bytes 3145736 | tf_op jit(solution)/shard_map/ppermute | solution.py:64
  320.7 43.6 %collective-permute-start.21 = (bf16[256,2048]{1,0:T(8,128)(2,1)}, bf16[256,2048]{1,0:T(8,128)(2,1)}, u32[]{:S(2)}, u32[]{:S(2)}) collective-permute-start(bf16[256,2048]{1,0:T(8,128)(2,1)} %get-tuple-element.108), channel_id=1, source_target_pairs={{0,1},{1,0},{2,3},{3,2},{4,5},{5,4},{6,7},{7,6},{8,9},{9,8},{10,11... | collective-permute-start | bytes 3145736 | tf_op jit(solution)/shard_map/ppermute | solution.py:64
  321.1 31.9 %collective-permute-start.33 = (bf16[256,2048]{1,0:T(8,128)(2,1)}, bf16[256,2048]{1,0:T(8,128)(2,1)S(1)}, u32[]{:S(2)}, u32[]{:S(2)}) collective-permute-start(bf16[256,2048]{1,0:T(8,128)(2,1)} %get-tuple-element.119), channel_id=1, source_target_pairs={{0,1},{1,0},{2,3},{3,2},{4,5},{5,4},{6,7},{7,6},{8,9},{9,8},{10,11... | collective-permute-start | bytes 3145736 | tf_op jit(solution)/shard_map/ppermute | solution.py:64
  321.2 32.3 %collective-permute-start.34 = (bf16[256,2048]{1,0:T(8,128)(2,1)S(1)}, bf16[256,2048]{1,0:T(8,128)(2,1)S(1)}, u32[]{:S(2)}, u32[]{:S(2)}) collective-permute-start(bf16[256,2048]{1,0:T(8,128)(2,1)S(1)} %copy-done.17), channel_id=1, source_target_pairs={{0,2},{1,3},{2,0},{3,1},{4,6},{5,7},{6,4},{7,5},{8,10},{9,11},{10,... | collective-permute-start | bytes 3145736 | tf_op jit(solution)/shard_map/ppermute | solution.py:64
  325.1 44.2 %collective-permute-start.30 = (bf16[256,2048]{1,0:T(8,128)(2,1)}, bf16[256,2048]{1,0:T(8,128)(2,1)}, u32[]{:S(2)}, u32[]{:S(2)}) collective-permute-start(bf16[256,2048]{1,0:T(8,128)(2,1)} %add_after.2), channel_id=1, source_target_pairs={{0,2},{1,3},{2,0},{3,1},{4,6},{5,7},{6,4},{7,5},{8,10},{9,11},{10,... | collective-permute-start | bytes 3145736 | tf_op jit(solution)/shard_map/ppermute | solution.py:64
  405.5 46.4 %collective-permute-start.38 = (bf16[256,2048]{1,0:T(8,128)(2,1)}, bf16[256,2048]{1,0:T(8,128)(2,1)}, u32[]{:S(2)}, u32[]{:S(2)}) collective-permute-start(bf16[256,2048]{1,0:T(8,128)(2,1)} %get-tuple-element.125), channel_id=1, source_target_pairs={{0,1},{1,0},{2,3},{3,2},{4,5},{5,4},{6,7},{7,6},{8,9},{9,8},{10,11... | collective-permute-start | bytes 3145736 | tf_op jit(solution)/shard_map/ppermute | solution.py:64
  419.8 32.1 %collective-permute-start.42 = (bf16[256,2048]{1,0:T(8,128)(2,1)}, bf16[256,2048]{1,0:T(8,128)(2,1)}, u32[]{:S(2)}, u32[]{:S(2)}) collective-permute-start(bf16[256,2048]{1,0:T(8,128)(2,1)} %add_after.3), channel_id=1, source_target_pairs={{0,2},{1,3},{2,0},{3,1},{4,6},{5,7},{6,4},{7,5},{8,10},{9,11},{10,... | collective-permute-start | bytes 3145736 | tf_op jit(solution)/shard_map/ppermute | solution.py:64
  519.0 41.4 %collective-permute-start.61 = (bf16[2,2,4,128,512]{4,3,2,1,0:T(8,128)(2,1)}, bf16[2,2,4,128,512]{4,3,2,1,0:T(8,128)(2,1)}, u32[]{:S(2)}, u32[]{:S(2)}) collective-permute-start(bf16[2,2,4,128,512]{4,3,2,1,0:T(8,128)(2,1)} %get-tuple-element.161), channel_id=1, source_target_pairs={{0,1},{1,0},{2,3},{3,2},{4,5},{5,4},{6,7},{7,6},{8,9},{9,8},{10,11... | collective-permute-start | bytes 6291464 | tf_op jit(solution)/shard_map/ppermute | solution.py:64
  552.7 35.8 %collective-permute-start.64 = (bf16[2,4,128,512]{3,2,1,0:T(8,128)(2,1)S(1)}, bf16[2,4,128,512]{3,2,1,0:T(8,128)(2,1)}, u32[]{:S(2)}, u32[]{:S(2)}) collective-permute-start(bf16[2,4,128,512]{3,2,1,0:T(8,128)(2,1)S(1)} %copy-done.8), channel_id=1, source_target_pairs={{0,4},{4,0},{8,12},{12,8},{16,20},{20,16},{24,28},{28,24},{1,5},{5... | collective-permute-start | bytes 3145736 | tf_op jit(solution)/shard_map/ppermute | solution.py:64
  552.7 52.5 %collective-permute-start.69 = (bf16[2,2,4,112,512]{4,3,2,1,0:T(8,128)(2,1)}, bf16[2,2,4,112,512]{4,3,2,1,0:T(8,128)(2,1)}, u32[]{:S(2)}, u32[]{:S(2)}) collective-permute-start(bf16[2,2,4,112,512]{4,3,2,1,0:T(8,128)(2,1)} %get-tuple-element.163), channel_id=1, source_target_pairs={{0,1},{1,0},{2,3},{3,2},{4,5},{5,4},{6,7},{7,6},{8,9},{9,8},{10,11... | collective-permute-start | bytes 5505032 | tf_op jit(solution)/shard_map/ppermute | solution.py:64
  552.7 55.8 %collective-permute-start.72 = (bf16[2,2,4,112,512]{4,3,2,1,0:T(8,128)(2,1)}, bf16[2,2,4,112,512]{4,3,2,1,0:T(8,128)(2,1)S(1)}, u32[]{:S(2)}, u32[]{:S(2)}) collective-permute-start(bf16[2,2,4,112,512]{4,3,2,1,0:T(8,128)(2,1)} %get-tuple-element.165), channel_id=1, source_target_pairs={{0,1},{1,0},{2,3},{3,2},{4,5},{5,4},{6,7},{7,6},{8,9},{9,8},{10,11... | collective-permute-start | bytes 5505032 | tf_op jit(solution)/shard_map/ppermute | solution.py:64
  577.6 75.2 %collective-permute-start.60 = (bf16[4,4,256,128]{3,2,1,0:T(8,128)(2,1)S(1)}, bf16[4,4,256,128]{3,2,1,0:T(8,128)(2,1)S(1)}, u32[]{:S(2)}, u32[]{:S(2)}) collective-permute-start(bf16[4,4,256,128]{3,2,1,0:T(8,128)(2,1)S(1)} %pad_maximum_fusion.1), channel_id=1, source_target_pairs={{0,4},{4,0},{8,12},{12,8},{16,20},{20,16},{24,28},{28,24},{1,5},{5... | collective-permute-start | bytes 3145736 | tf_op jit(solution)/shard_map/ppermute | solution.py:64
  (119 other events, 1268.2 us)
Sparse Core Ops, SparseCore 0:
  11.5 135.0 all-gather.2

commit v3 on v2

--- a/solution.py
+++ b/solution.py
@@ -64,15 +64,20 @@
     return lax.ppermute(values, axis, [(i, i ^ bit) for i in range(size)])
 
 
-def lookup_kernel(ids_ref, table_ref, out_ref):
+def lookup_kernel(ids_ref, table_ref, _after, out_ref):
     rows = ids_ref.shape[0]
-    height = table_ref.shape[0]
-    places = lax.broadcasted_iota(jnp.int32, (rows, height), 1)
-    chosen = jnp.where(ids_ref[...] == places, 1.0, 0.0).astype(BF16)
-    out_ref[...] = matmul(chosen, table_ref[...]).astype(BF16)
-
-
-def lookup(ids, table):
+    height, width = table_ref.shape
+    half = height // 2
+    ids = ids_ref[...]
+    upper = ids >= half
+    places = jnp.where(upper, ids - half, ids)
+    chosen = places == lax.broadcasted_iota(jnp.int32, (rows, half), 1)
+    pairs = jnp.concatenate([table_ref[:half], table_ref[half:]], axis=1)
+    found = matmul(jnp.where(chosen, 1.0, 0.0).astype(BF16), pairs)
+    out_ref[...] = jnp.where(upper, found[:, width:], found[:, :width]).astype(BF16)
+
+
+def lookup(ids, table, after):
     count = ids.shape[0]
     height, width = table.shape
     rows = 512
@@ -82,6 +87,7 @@
         in_specs=[
             pl.BlockSpec((rows, 1), lambda i: (i, 0)),
             pl.BlockSpec((height, width), lambda i: (0, 0)),
+            pl.BlockSpec(memory_space=pl.ANY),
         ],
         out_specs=pl.BlockSpec((rows, width), lambda i: (i, 0)),
         out_shape=jax.ShapeDtypeStruct((count, width), BF16),
@@ -90,43 +96,53 @@
             flops=4 * count * height * width, bytes_accessed=4 * count * width, transcendentals=0
         ),
         name="lookup",
-    )(ids[:, None], table)
-
-
-def collect_kernel(ids_ref, rows_ref, base_ref, out_ref):
+    )(ids[:, None], table, after)
+
+
+def collect_kernel(ids_ref, ids_left, ids_right, left_ref, right_ref, base_ref, out_ref):
     @pl.when(pl.program_id(0) == 0)
     def _():
         out_ref[...] = jnp.zeros_like(out_ref) if base_ref is None else base_ref[...]
 
-    height = out_ref.shape[0]
-    places = lax.broadcasted_iota(jnp.int32, (height, ids_ref.shape[1]), 0)
-    chosen = jnp.where(ids_ref[...] == places, 1.0, 0.0).astype(BF16)
-    out_ref[...] += matmul(chosen, rows_ref[...])
-
-
-def collect(ids, values, height, base):
-    count, width = values.shape
-    rows = 512
+    height, width = out_ref.shape
+    half = height // 2
+    total = None
+    for i, (column, rows_ref) in enumerate(((ids_left, left_ref), (ids_right, right_ref))):
+        ids = ids_ref[i : i + 1, :]
+        ids = jnp.where(ids >= half, ids - half, ids)
+        places = lax.broadcasted_iota(jnp.int32, (half, ids.shape[1]), 0)
+        chosen = jnp.where(ids == places, 1.0, 0.0).astype(BF16)
+        rows = rows_ref[...].astype(F32)
+        upper = column[...] >= half
+        pairs = [jnp.where(upper, 0.0, rows), jnp.where(upper, rows, 0.0)]
+        part = matmul(chosen, jnp.concatenate(pairs, axis=1).astype(BF16))
+        total = part if total is None else total + part
+    out_ref[:half] += total[:, :width]
+    out_ref[half:] += total[:, width:]
+
+
+def collect(ids, columns, left, right, height, base):
+    count, width = left.shape
+    rows = 256
     whole = pl.BlockSpec((height, width), lambda i: (0, 0))
     kernel = collect_kernel
     if base is None:
-        kernel = lambda ids_ref, rows_ref, out_ref: collect_kernel(ids_ref, rows_ref, None, out_ref)
+        kernel = lambda *refs: collect_kernel(*refs[:5], None, refs[5])
     return pl.pallas_call(
         kernel,
         grid=(count // rows,),
-        in_specs=[
-            pl.BlockSpec((1, rows), lambda i: (0, i)),
-            pl.BlockSpec((rows, width), lambda i: (i, 0)),
-        ]
+        in_specs=[pl.BlockSpec((2, rows), lambda i: (0, i))]
+        + [pl.BlockSpec((rows, 1), lambda i: (i, 0))] * 2
+        + [pl.BlockSpec((rows, width), lambda i: (i, 0))] * 2
         + ([] if base is None else [whole]),
         out_specs=whole,
         out_shape=jax.ShapeDtypeStruct((height, width), F32),
         compiler_params=pltpu.CompilerParams(vmem_limit_bytes=48 << 20),
         cost_estimate=pl.CostEstimate(
-            flops=4 * count * height * width, bytes_accessed=4 * count * width, transcendentals=0
+            flops=8 * count * height * width, bytes_accessed=8 * count * width, transcendentals=0
         ),
         name="collect",
-    )(ids[None, :], values, *([] if base is None else [base]))
+    )(ids, *columns, left, right, *([] if base is None else [base]))
 
 
 QUERY_ROWS = 256
@@ -272,7 +288,7 @@
 
 def attend_back_kernel(
     place, part0, part1, part2, part3, context_t, log_total, table_q, table_kv, ids, ids_share, trig,
-    w_query, w_kv, embeds, gain, grad_hidden, _after_one, _after_two, _after_three, grad_entries,
+    w_query, w_kv, embeds, gain, grad_hidden, _a0, _a1, _a2, _a3, _a4, grads0, grads1, grads2, grads3,
     onehot, columns, keys, keys_t, values, grad_keys, grad_values, total, grad_context,
 ):
     tokens = ids.shape[1]
@@ -350,9 +366,12 @@
         scaled = (full[:entries] + full[entries:]) * gain[...].astype(F32)
         wide = embeds[...].astype(F32)
         places = lax.broadcasted_iota(jnp.int32, (entries, ids_share.shape[1]), 0)
-        own = jnp.where(places == ids_share[...], 1.0, 0.0).astype(BF16)
-        result = rms_back(wide, rms_parts(wide), scaled) + matmul(own, grad_hidden[...])
-        grad_entries[...] = result.astype(BF16)
+        chosen = jnp.where(places == ids_share[...], 1.0, 0.0).astype(BF16)
+        result = rms_back(wide, rms_parts(wide), scaled) + matmul(chosen, grad_hidden[...])
+        result = result.astype(BF16)
+        own = grads0.shape[0]
+        for k, out in enumerate((grads0, grads1, grads2, grads3)):
+            out[...] = result[k * own : (k + 1) * own]
 
 
 def attend_back(
@@ -384,9 +403,9 @@
             whole(1, width),
             whole(*grad_hidden.shape),
         ]
-        + [pl.BlockSpec(memory_space=pl.ANY)] * 3,
-        out_specs=whole(entries, width),
-        out_shape=jax.ShapeDtypeStruct((entries, width), BF16),
+        + [pl.BlockSpec(memory_space=pl.ANY)] * 5,
+        out_specs=[whole(entries // 4, width)] * 4,
+        out_shape=[jax.ShapeDtypeStruct((entries // 4, width), BF16)] * 4,
         scratch_shapes=[
             pltpu.VMEM((lanes, tokens), BF16),
             pltpu.VMEM((tokens, lanes), BF16),
@@ -417,18 +436,38 @@
     return jnp.where(places == ids[...], 1.0, 0.0).astype(BF16)
 
 
+def load_weights(sources, targets, sems):
+    copies = [
+        pltpu.make_async_copy(source, target, sems.at[i])
+        for i, (source, target) in enumerate(zip(sources, targets))
+    ]
+    for copy in copies:
+        copy.start()
+    return copies
+
+
 def hidden_kernel(
     embeds, ids_own, ids_peer, gain, c0, c1, c2, c3, w0, w1, w2, w3, _after_one, _after_two,
-    normed_own, normed_peer, hidden,
+    normed_own, normed_peer, hidden, held, sems,
 ):
+    heads = w0.shape[0]
+    copies = load_weights(
+        (w0, w1, w2, w3), [held.at[pl.ds(k * heads, heads)] for k in range(4)], sems
+    )
+    rows = jnp.concatenate([pick_rows(ids_own, embeds.shape[0]), pick_rows(ids_peer, embeds.shape[0])], axis=1)
+    total = matmul_left_t(rows, embeds[...])
+    for first, (left, right) in ((0, (c0, c1)), (2, (c2, c3))):
+        own = first // 2
+        sides = [jnp.concatenate([part[own], part[1 - own]], axis=0) for part in (left, right)]
+        copies[first].wait()
+        copies[first + 1].wait()
+        both = jnp.concatenate(sides, axis=1)
+        total = total + matmul(both, held[first * heads : (first + 2) * heads])
+    low = (total * rms_parts(total) * gain[...].astype(F32)).astype(BF16)
     share = normed_own.shape[0]
-    for own, ids, normed in ((False, ids_peer, normed_peer), (True, ids_own, normed_own)):
-        total = matmul_left_t(pick_rows(ids, embeds.shape[0]), embeds[...])
-        for k, (part, weight) in enumerate(((c0, w0), (c1, w1), (c2, w2), (c3, w3))):
-            total = total + matmul(part[int(own == (k >= 2))], weight[...])
-        normed[...] = (total * rms_parts(total) * gain[...].astype(F32)).astype(BF16)
-        if own:
-            hidden[...] = total
+    normed_own[...] = low[:share]
+    normed_peer[...] = low[share:]
+    hidden[...] = total[:share]
 
 
 def hidden_rows_of(embeds, ids_own, ids_peer, gain, parts, weights, after):
@@ -436,12 +475,16 @@
     vmem = pl.BlockSpec(memory_space=pltpu.VMEM)
     return pl.pallas_call(
         hidden_kernel,
-        in_specs=[vmem] * 12 + [ANY_SPEC] * 2,
+        in_specs=[vmem] * 8 + [ANY_SPEC] * 6,
         out_specs=[vmem] * 3,
         out_shape=[
             jax.ShapeDtypeStruct((rows, width), BF16),
             jax.ShapeDtypeStruct((rows, width), BF16),
             jax.ShapeDtypeStruct((rows, width), F32),
+        ],
+        scratch_shapes=[
+            pltpu.VMEM((4 * weights[0].shape[0], width), BF16),
+            pltpu.SemaphoreType.DMA((4,)),
         ],
         compiler_params=pltpu.CompilerParams(vmem_limit_bytes=VMEM_LIMIT),
         cost_estimate=pl.CostEstimate(
@@ -452,17 +495,20 @@
 
 
 def hidden_back_kernel(
-    cotangent, hidden, kept, from_core, from_chip, gain, w0, w1, w2, w3,
-    low, p0, p1, p2, p3,
+    cotangent, hidden, kept, core_a, core_b, from_chip, gain, w0, w1, w2, w3,
+    low, p0, p1, p2, p3, held, sems,
 ):
-    grads = kept[...].astype(F32) + from_core[...].astype(F32) + from_chip[...].astype(F32)
+    copies = load_weights((w2, w3, w1, w0), [held.at[k] for k in range(4)], sems)
+    from_core = jnp.concatenate([core_a[...], core_b[...]], axis=0)
+    grads = kept[...].astype(F32) + from_core.astype(F32) + from_chip[...].astype(F32)
     rows = hidden[...]
     scaled = grads * gain[...].astype(F32)
     total = cotangent[0] + rms_back(rows, rms_parts(rows), scaled)
     total = total.astype(BF16)
     low[...] = total
-    for part, weight in ((p2, w2), (p3, w3), (p1, w1), (p0, w0)):
-        part[...] = matmul_right_t(total, weight[...]).astype(BF16)
+    for k, part in enumerate((p2, p3, p1, p0)):
+        copies[k].wait()
+        part[...] = matmul_right_t(total, held[k]).astype(BF16)
 
 
 def hidden_back(micro, cotangent, hidden, kept, from_core, from_chip, gain, weights):
@@ -472,92 +518,105 @@
     return pl.pallas_call(
         hidden_back_kernel,
         grid=(1,),
-        in_specs=[pl.BlockSpec((1, rows, width), lambda i: (micro, 0, 0))]
-        + [whole(rows, width)] * 4
-        + [whole(1, width)]
-        + [whole(heads, width)] * 4,
+        in_specs=[
+            pl.BlockSpec((1, rows, width), lambda i: (micro, 0, 0)),
+            whole(rows, width),
+            whole(rows, width),
+            whole(rows // 2, width),
+            whole(rows // 2, width),
+            whole(rows, width),
+            whole(1, width),
+        ]
+        + [ANY_SPEC] * 4,
         out_specs=[whole(rows, width)] + [whole(rows, heads)] * 4,
         out_shape=[jax.ShapeDtypeStruct((rows, width), BF16)]
         + [jax.ShapeDtypeStruct((rows, heads), BF16)] * 4,
+        scratch_shapes=[
+            pltpu.VMEM((4, heads, width), BF16),
+            pltpu.SemaphoreType.DMA((4,)),
+        ],
         compiler_params=pltpu.CompilerParams(vmem_limit_bytes=VMEM_LIMIT),
         cost_estimate=pl.CostEstimate(
             flops=2 * 10**9, bytes_accessed=16 * 10**6, transcendentals=0
         ),
         name="hidden_back",
-    )(cotangent, hidden, kept, from_core, from_chip, gain, *weights)
+    )(cotangent, hidden, kept, *from_core, from_chip, gain, *weights)
 
 
 def mlp_kernel(
-    x_mine, x_other, grad_mine_in, grad_other_in, gate_hbm, up_hbm, down_hbm, _after_one, _after_two, _after_three,
-    out_mine, out_other, grad_mine, grad_other,
-    w_gate, w_up, w_down, sems,
+    ready, x_mine, x_other, mine_in, other_in, gate_hbm, up_hbm, down_hbm,
+    _after_one, _after_two, _after_three,
+    out_mine, out_other, grad_mine, grad_a, grad_b,
+    w_both, w_down, sems,
 ):
-    copies = [
-        pltpu.make_async_copy(source, target, sems.at[i])
-        for i, (source, target) in enumerate(
-            ((gate_hbm, w_gate), (up_hbm, w_up), (down_hbm, w_down))
-        )
-    ]
-    for copy in copies:
-        copy.start()
+    units = w_down.shape[0]
+    main = units // 256 * 256
+    rest = units - main
+    cuts = ((0, gate_hbm, 0, main), (main, up_hbm, 0, main), (2 * main, gate_hbm, main, rest),
+            (2 * main + rest, up_hbm, main, rest))
+    copies = load_weights(
+        [source.at[:, pl.ds(at, size)] for _, source, at, size in cuts if size] + [down_hbm],
+        [w_both.at[:, pl.ds(to, size)] for to, _, _, size in cuts if size] + [w_down],
+        sems,
+    )
     for first, (rows, cots, out, grad) in enumerate(
-        ((x_other, grad_other_in, out_other, grad_other), (x_mine, grad_mine_in, out_mine, grad_mine))
+        ((x_other, other_in, out_other, None), (x_mine, mine_in, out_mine, grad_mine))
     ):
         if first == 0:
             copies[0].wait()
-        gate = matmul(rows[...], w_gate[...])
+        gate = matmul(rows[...], w_both[:, :main])
         if first == 0:
-            copies[1].wait()
-        upward = matmul(rows[...], w_up[...])
+            for copy in copies[1:-1]:
+                copy.wait()
+        others = matmul(rows[...], w_both[:, main:])
+        gate = jnp.concatenate([gate, others[:, main : main + rest]], axis=1)
+        upward = jnp.concatenate([others[:, :main], others[:, main + rest :]], axis=1)
         if first == 0:
-            copies[2].wait()
-        grad_active = matmul_right_t(cots[...], w_down[...])
+            copies[-1].wait()
+        if ready:
+            grad_active = cots[...].astype(F32)
+        else:
+            grad_active = matmul_right_t(cots[...], w_down[...])
         sigmoid = 1.0 / (1.0 + jnp.exp(-gate))
         silu = gate * sigmoid
         activated = (silu * upward).astype(BF16)
         grad_gate = grad_active * upward * (sigmoid * (1.0 + gate * (1.0 - sigmoid)))
+        grad_gate = grad_gate.astype(BF16)
         grad_up = (grad_active * silu).astype(BF16)
         out[...] = matmul(activated, w_down[...]).astype(BF16)
-        total = matmul_right_t(grad_gate.astype(BF16), w_gate[...])
-        grad[...] = (total + matmul_right_t(grad_up, w_up[...])).astype(BF16)
-
-
-def mlp(x_mine, x_other, cot_mine, cot_other, w_gate, w_up, w_down, after):
-    rows, width = x_mine.shape
+        parts = [grad_gate[:, :main], grad_up[:, :main], grad_gate[:, main:], grad_up[:, main:]]
+        total = matmul_right_t(jnp.concatenate(parts, axis=1), w_both[...]).astype(BF16)
+        if grad is None:
+            half = grad_a.shape[0]
+            grad_a[...] = total[:half]
+            grad_b[...] = total[half:]
+        else:
+            grad[...] = total
+
+
+def mlp(mine, other, mine_in, other_in, w_gate, w_up, w_down, after):
+    rows, width = mine.shape
     units = w_gate.shape[1]
+    assert units % 256 in (0, 128)
+    ready = mine_in.shape[1] == units
     vmem = pl.BlockSpec(memory_space=pltpu.VMEM)
     return pl.pallas_call(
-        mlp_kernel,
+        lambda *refs: mlp_kernel(ready, *refs),
         in_specs=[vmem] * 4 + [ANY_SPEC] * 6,
-        out_specs=[vmem] * 4,
-        out_shape=[jax.ShapeDtypeStruct((rows, width), BF16)] * 4,
+        out_specs=[vmem] * 5,
+        out_shape=[jax.ShapeDtypeStruct((rows, width), BF16)] * 3
+        + [jax.ShapeDtypeStruct((rows // 2, width), BF16)] * 2,
         scratch_shapes=[
-            pltpu.VMEM((width, units), BF16),
-            pltpu.VMEM((width, units), BF16),
+            pltpu.VMEM((width, 2 * units), BF16),
             pltpu.VMEM((units, width), BF16),
-            pltpu.SemaphoreType.DMA((3,)),
+            pltpu.SemaphoreType.DMA((5,)),
         ],
         compiler_params=pltpu.CompilerParams(vmem_limit_bytes=VMEM_LIMIT),
         cost_estimate=pl.CostEstimate(
             flops=24 * rows * width * units, bytes_accessed=26 * 10**6, transcendentals=2 * rows * units
         ),
         name="mlp",
-    )(x_mine, x_other, cot_mine, cot_other, w_gate, w_up, w_down, *after)
-
-
-def add_kernel(left, right, _after, out):
-    out[...] = (left[...].astype(F32) + right[...].astype(F32)).astype(BF16)
-
-
-def add_after(left, right, after):
-    vmem = pl.BlockSpec(memory_space=pltpu.VMEM)
-    return pl.pallas_call(
-        add_kernel,
-        in_specs=[vmem, vmem, ANY_SPEC],
-        out_specs=vmem,
-        out_shape=jax.ShapeDtypeStruct(left.shape, BF16),
-        name="add_after",
-    )(left, right, after)
+    )(mine, other, mine_in, other_in, w_gate, w_up, w_down, *after)
 
 
 def cast_kernel(values, _after, out):
@@ -566,14 +625,54 @@
 
 def cast_after(micro, values, after):
     _, rows, width = values.shape
+    steps = 4
     return pl.pallas_call(
         cast_kernel,
-        grid=(1,),
-        in_specs=[pl.BlockSpec((1, rows, width), lambda i: (micro, 0, 0)), ANY_SPEC],
-        out_specs=pl.BlockSpec((rows, width), lambda i: (0, 0)),
+        grid=(steps,),
+        in_specs=[pl.BlockSpec((1, rows // steps, width), lambda i: (micro, i, 0)), ANY_SPEC],
+        out_specs=pl.BlockSpec((rows // steps, width), lambda i: (i, 0)),
         out_shape=jax.ShapeDtypeStruct((rows, width), BF16),
         name="cast_after",
     )(values, after)
+
+
+def tie_kernel(_values, _after, _out):
+    pass
+
+
+def tie(values, after):
+    return pl.pallas_call(
+        tie_kernel,
+        in_specs=[ANY_SPEC] * 2,
+        out_specs=ANY_SPEC,
+        out_shape=jax.ShapeDtypeStruct(values.shape, values.dtype),
+        input_output_aliases={0: 0},
+        name="tie",
+    )(values, after)
+
+
+def results_kernel(*refs):
+    out = refs[9]
+    for micro in range(2):
+        first, *rest = refs[4 * micro : 4 * micro + 4]
+        total = first[...]
+        for part in rest:
+            total = total + part[...].astype(F32)
+        out[micro] = total.astype(BF16)
+
+
+def add_results(first, second, after):
+    rows, width = first[0].shape
+    steps = 4
+    part = pl.BlockSpec((rows // steps, width), lambda i: (i, 0))
+    return pl.pallas_call(
+        results_kernel,
+        grid=(steps,),
+        in_specs=[part] * 8 + [ANY_SPEC],
+        out_specs=pl.BlockSpec((2, rows // steps, width), lambda i: (0, i, 0)),
+        out_shape=jax.ShapeDtypeStruct((2, rows, width), BF16),
+        name="results",
+    )(*first, *second, after)
 
 
 BLOCKS = 32
@@ -587,8 +686,11 @@
     return ref[...].reshape(blocks * rows, width)
 
 
-def entry_bias(valid, rows, slots):
-    shape = (rows, rows)
+ENTRY_ROWS = 256
+
+
+def entry_bias(valid, slots):
+    shape = (valid.shape[1], valid.shape[1])
     same = lax.broadcasted_iota(jnp.int32, shape, 0) // slots == lax.broadcasted_iota(
         jnp.int32, shape, 1
     ) // slots
@@ -605,10 +707,34 @@
     return 0.5 * (1.0 + lax.erf(values * SQRT_HALF))
 
 
+def lay_out_vectors(small, vectors, inner_bias):
+    blocks, rows, lanes = small.shape
+
+    def spread_rows(values, each, width):
+        shape = (lanes, width)
+        line = lax.broadcasted_iota(jnp.int32, shape, 0)
+        column = lax.broadcasted_iota(jnp.int32, shape, 1)
+        copies = jnp.where(column % each == line, 1.0, 0.0).astype(BF16)
+        wide = matmul(values, copies).reshape(blocks, values.shape[0] // blocks, width)
+        block = lax.broadcasted_iota(jnp.int32, wide.shape, 0)
+        column = lax.broadcasted_iota(jnp.int32, wide.shape, 2)
+        return jnp.sum(jnp.where(column // each == block, wide, 0.0), axis=0)
+
+    count, width = vectors.shape
+    layers, inner_width = inner_bias.shape
+    values = small[...]
+    vectors[...] = spread_rows(values.reshape(blocks * rows, lanes), UNIT, width)[:count]
+    line = lax.broadcasted_iota(jnp.int32, values.shape, 1)
+    for layer in range(layers):
+        chosen = jnp.where(line == count + layer, values.astype(F32), 0.0)
+        chosen = jnp.sum(chosen, axis=1).astype(BF16)
+        inner_bias[layer : layer + 1, :] = spread_rows(chosen, 4 * UNIT, inner_width)
+
+
 def hyper_kernel(
-    slots, place, _after, part0, part1, part2, part3, valid, vectors, inner_bias, outer, w_q, w_k, w_v, w_o, in0, in1, in2, in3,
+    slots, place, _a0, _a1, _a2, _a3, _a4, _a5, _a6, _a7, _a8, _a9, _a10, _a11, part0, part1, part2, part3, valid, small, outer, w_q, w_k, w_v, w_o, in0, in1, in2, in3,
     pr0, pr1, pr2, pr3,
-    below, mixed, context, middle, inner, pooled, pooled_norm, embeds,
+    vectors, inner_bias, below, mixed, context, middle, inner, pooled, pooled_norm, embeds,
     state, joined,
 ):
     layer = pl.program_id(0)
@@ -621,6 +747,7 @@
         for k, part in enumerate((part0, part1, part2, part3)):
             at = pl.multiple_of((place[0] ^ k) * columns, columns)
             state[:, pl.ds(at, columns)] = part[...].astype(F32)
+        lay_out_vectors(small, vectors, inner_bias)
 
     def vector(index):
         return vectors[pl.ds(index * layers + layer, 1), :]
@@ -635,11 +762,13 @@
     mixed[0, :, :width] = queries
     mixed[0, :, width : 2 * width] = keys
     mixed[0, :, 2 * width :] = values
-    bias = entry_bias(valid[...], rows, slots)
-    for head in range(width // HEAD_DIM):
-        at = slice(head * HEAD_DIM, (head + 1) * HEAD_DIM)
-        soft = entry_soft(queries[:, at], keys[:, at], bias)
-        joined[:, at] = matmul(soft.astype(BF16), values[:, at])
+    for first in range(0, rows, ENTRY_ROWS):
+        lines = slice(first, first + ENTRY_ROWS)
+        bias = entry_bias(valid[:, lines], slots)
+        for head in range(width // HEAD_DIM):
+            at = slice(head * HEAD_DIM, (head + 1) * HEAD_DIM)
+            soft = entry_soft(queries[lines, at], keys[lines, at], bias)
+            joined[lines, at] = matmul(soft.astype(BF16), values[lines, at])
     context_low = joined[...].astype(BF16)
     context[0] = context_low
     centre = hidden + matmul(context_low, square(w_o)) + vector(4)
@@ -692,25 +821,28 @@
     return pl.BlockSpec(shape, lambda i: (0,) * len(shape))
 
 
-def hyper_forward(where, after, parts, valid, vectors, inner_bias, packed, slots):
+def hyper_forward(where, after, parts, valid, packed, slots, layers):
     rows, width = parts[0].shape[0], len(parts) * parts[0].shape[1]
-    layers, inner_width = inner_bias.shape
+    inner_width = 4 * width
+    count = VECTORS * layers + 2
+    last_rows = packed.shape[1] // (2 * UNIT) - 1
     entries = rows // slots
     by_layer = lambda *shape: pl.BlockSpec((1,) + shape, lambda i: (i,) + (0,) * len(shape))
     return pl.pallas_call(
         lambda *refs: hyper_kernel(slots, *refs),
         grid=(layers,),
         in_specs=[pl.BlockSpec(memory_space=pltpu.SMEM)]
-        + [pl.BlockSpec(memory_space=pl.ANY)]
+        + [pl.BlockSpec(memory_space=pl.ANY)] * 12
         + [whole_spec(*part.shape) for part in parts]
         + [
             whole_spec(1, rows),
-            whole_spec(*vectors.shape),
-            whole_spec(layers, inner_width),
+            pl.BlockSpec((BLOCKS, 2 * UNIT, 128), lambda i: (0, last_rows, 0)),
         ]
         + layer_specs(width, lambda i: i)
         + proj_specs(width, layers),
         out_specs=[
+            whole_spec(count, width),
+            whole_spec(layers, inner_width),
             by_layer(rows, width),
             by_layer(rows, 3 * width),
             by_layer(rows, width),
@@ -721,6 +853,8 @@
             whole_spec(entries, 4 * width),
         ],
         out_shape=[
+            jax.ShapeDtypeStruct((count, width), F32),
+            jax.ShapeDtypeStruct((layers, inner_width), F32),
             jax.ShapeDtypeStruct((layers, rows, width), F32),
             jax.ShapeDtypeStruct((layers, rows, 3 * width), BF16),
             jax.ShapeDtypeStruct((layers, rows, width), BF16),
@@ -736,7 +870,7 @@
             flops=8 * 10**9, bytes_accessed=25 * 10**6, transcendentals=4 * 10**6
         ),
         name="hyper",
-    )(where, after, *parts, valid, vectors, inner_bias, *([packed] * (LAYER_UNITS - 3 + 4)))
+    )(where, *after, *parts, valid, *([packed] * (1 + LAYER_UNITS - 3 + 4)))
 
 
 def hyper_back_kernel(
@@ -745,14 +879,14 @@
 ):
     place, refs = refs[0], refs[1:]
     if last:
-        grad_embeds, pooled, pooled_norm, pr0, pr1, pr2, pr3 = refs[:7]
-        refs = refs[7:]
+        arrivals, (pooled, pooled_norm, pr0, pr1, pr2, pr3) = refs[:8], refs[8:14]
+        refs = refs[14:]
     else:
         grad_start = refs[0]
         refs = refs[1:]
-    valid, vectors, below, mixed, context, middle, inner = refs[1:8]
-    outer, w_q, w_k, w_v, w_o, in0, in1, in2, in3 = refs[8:17]
-    refs = refs[17:]
+    valid, vectors, below, mixed, context, middle, inner = refs[2:9]
+    outer, w_q, w_k, w_v, w_o, in0, in1, in2, in3 = refs[9:18]
+    refs = refs[18:]
     if layer == 0:
         small_above, inner_above = refs[:2]
         refs = refs[2:]
@@ -792,6 +926,13 @@
     if last:
         normed, inverse = norm_parts(pooled[...])
         grad_norm = jnp.zeros(normed.shape, F32)
+        sums = []
+        for group in (arrivals[:4], arrivals[4:]):
+            total = group[0][...].astype(F32)
+            for part in group[1:]:
+                total = total + part[...].astype(F32)
+            sums.append(total)
+        grad_embeds = jnp.concatenate(sums, axis=0).astype(BF16)
         for j, piece in enumerate((pr0, pr1, pr2, pr3)):
             part = grad_embeds[:, j * width : (j + 1) * width]
             put(LAYER_UNITS + j, matmul_left_t(pooled_norm[...], part))
@@ -832,20 +973,23 @@
     low = grad_rows.astype(BF16)
     put(7, matmul_left_t(context[0], low))
     grad_context = matmul_right_t(low, square(w_o)).astype(BF16)
-    bias = entry_bias(valid[...], rows, slots)
-    for head in range(width // HEAD_DIM):
-        at, key_at, value_at = (
-            slice(i * width + head * HEAD_DIM, i * width + (head + 1) * HEAD_DIM) for i in range(3)
-        )
-        queries, keys, values = mixed[0, :, at], mixed[0, :, key_at], mixed[0, :, value_at]
-        soft = entry_soft(queries, keys, bias)
-        grad_head = grad_context[:, at]
-        grad_soft = matmul_right_t(grad_head, values)
-        offset = jnp.sum(soft * grad_soft, axis=1, keepdims=True)
-        grad_scores = (soft * (grad_soft - offset) * HEAD_DIM ** (-0.5)).astype(BF16)
-        grad_mixed[:, at] = matmul(grad_scores, keys)
-        grad_mixed[:, key_at] = matmul_left_t(grad_scores, queries)
-        grad_mixed[:, value_at] = matmul_left_t(soft.astype(BF16), grad_head)
+    for first in range(0, rows, ENTRY_ROWS):
+        lines = slice(first, first + ENTRY_ROWS)
+        bias = entry_bias(valid[:, lines], slots)
+        for head in range(width // HEAD_DIM):
+            at, key_at, value_at = (
+                slice(i * width + head * HEAD_DIM, i * width + (head + 1) * HEAD_DIM)
+                for i in range(3)
+            )
+            queries, keys, values = (mixed[0, lines, part] for part in (at, key_at, value_at))
+            soft = entry_soft(queries, keys, bias)
+            grad_head = grad_context[lines, at]
+            grad_soft = matmul_right_t(grad_head, values)
+            offset = jnp.sum(soft * grad_soft, axis=1, keepdims=True)
+            grad_scores = (soft * (grad_soft - offset) * HEAD_DIM ** (-0.5)).astype(BF16)
+            grad_mixed[lines, at] = matmul(grad_scores, keys)
+            grad_mixed[lines, key_at] = matmul_left_t(grad_scores, queries)
+            grad_mixed[lines, value_at] = matmul_left_t(soft.astype(BF16), grad_head)
     normed_one, inverse_one = norm_parts(below[0])
     normed_in = (normed_one * vector(0) + vector(1)).astype(BF16)
     grad_in = jnp.zeros(grad_rows.shape, F32)
@@ -893,15 +1037,15 @@
     at_layer = lambda *shape: pl.BlockSpec((1,) + shape, lambda i: (layer,) + (0,) * len(shape))
     inputs, specs = [place], [pl.BlockSpec(memory_space=pltpu.SMEM)]
     if last:
-        grad_embeds, pooled, pooled_norm = source
-        inputs += [grad_embeds, pooled, pooled_norm] + [packed] * 4
-        specs += [whole_spec(*grad_embeds.shape), whole_spec(*pooled.shape)]
+        arrivals, pooled, pooled_norm = source
+        inputs += [*arrivals, pooled, pooled_norm] + [packed] * 4
+        specs += [whole_spec(*part.shape) for part in arrivals] + [whole_spec(*pooled.shape)]
         specs += [whole_spec(*pooled_norm.shape)] + proj_specs(width, layers)
     else:
         inputs += [source]
         specs += [whole_spec(rows, width)]
-    inputs += [after, valid, vectors, below, mixed, context, middle, inner]
-    specs += [pl.BlockSpec(memory_space=pl.ANY)]
+    inputs += [*after, valid, vectors, below, mixed, context, middle, inner]
+    specs += [pl.BlockSpec(memory_space=pl.ANY)] * 2
     specs += [whole_spec(1, rows), whole_spec(*vectors.shape), at_layer(rows, width)]
     specs += [at_layer(rows, 3 * width), at_layer(rows, width), at_layer(rows, width)]
     specs += [at_layer(rows, inner_width)]
@@ -1001,20 +1145,22 @@
 
 
 def canonical(gathered, own, layers):
+    if own == UNIT:
+        return gathered
     devices, _, width = gathered.shape
     count = VECTORS * layers + 2
-    small = gathered[:, -2 * UNIT :]
-    vectors = small[:, :count, :own].transpose(1, 0, 2).reshape(count, devices * own)
-    inner_bias = small[:, count : count + layers, : 4 * own].transpose(1, 0, 2)
-    inner_bias = inner_bias.reshape(layers, devices * 4 * own)
-    if own != UNIT:
-        pieces, at = [], 0
-        for rows in piece_rows(layers, own) * layers + [own] * 4:
-            part = gathered[:, at : at + rows].reshape(BLOCKS, -1, width)
-            pieces.append(part)
-            at += rows
-        gathered = jnp.concatenate(pieces, axis=1)
-    return gathered, vectors.astype(F32), inner_bias.astype(F32)
+    pieces, at = [], 0
+    for rows in piece_rows(layers, own) * layers + [own] * 4:
+        pieces.append(gathered[:, at : at + rows].reshape(BLOCKS, -1, width))
+        at += rows
+    small = []
+    for first, rows, each in ((at, count, own), (at + count, layers, 4 * own)):
+        part = gathered[:, first : first + rows, :each].reshape(BLOCKS, -1, rows, each)
+        part = part.transpose(0, 2, 1, 3).reshape(BLOCKS, rows, -1)
+        small.append(jnp.pad(part, ((0, 0), (0, 0), (0, width - part.shape[2]))))
+    small = jnp.concatenate(small, axis=1)
+    pieces.append(jnp.pad(small, ((0, 0), (0, 2 * UNIT - small.shape[1]), (0, 0))))
+    return jnp.concatenate(pieces, axis=1)
 
 
 def to_devices(packed, devices, rows_list, vector_rows):
@@ -1040,22 +1186,24 @@
     return jnp.concatenate(pieces, axis=1)
 
 
-def unpack_kernel(layers, above, below, g_qkv, g_ao, g_in, g_out, g_proj, *vectors):
-    width = above.shape[1]
+def unpack_kernel(layers, above_kept, above_got, below_kept, below_got, g_qkv, g_ao, g_in, g_out, g_proj, *vectors):
+    width = above_kept.shape[2]
+    above = above_kept[0].astype(F32) + above_got[...].astype(F32)
+    below = below_kept[0].astype(F32) + below_got[...].astype(F32)
     for layer, ref in ((0, below), (1, above)):
-        g_out[layer] = ref[: 4 * UNIT].astype(F32)
+        g_out[layer] = ref[: 4 * UNIT]
         for j in range(3):
             at = (4 + j) * UNIT
-            g_qkv[layer, :, j * width : (j + 1) * width] = ref[at : at + UNIT].astype(F32)
-        g_ao[layer] = ref[7 * UNIT : 8 * UNIT].astype(F32)
+            g_qkv[layer, :, j * width : (j + 1) * width] = ref[at : at + UNIT]
+        g_ao[layer] = ref[7 * UNIT : 8 * UNIT]
         for j in range(4):
             at = (8 + j) * UNIT
-            g_in[layer, :, j * width : (j + 1) * width] = ref[at : at + UNIT].astype(F32)
+            g_in[layer, :, j * width : (j + 1) * width] = ref[at : at + UNIT]
     base = LAYER_UNITS * UNIT
     for j in range(4):
         at = base + j * UNIT
-        g_proj[:, j * width : (j + 1) * width] = above[at : at + UNIT].astype(F32)
-    small = below[base : base + 2 * UNIT, :128].astype(F32)
+        g_proj[:, j * width : (j + 1) * width] = above[at : at + UNIT]
+    small = below[base : base + 2 * UNIT, :128]
     for j in range(VECTORS):
         for i in range(layers):
             vectors[j][i : i + 1, :] = small[i * VECTORS + j : i * VECTORS + j + 1, :UNIT]
@@ -1066,7 +1214,7 @@
 
 
 def unpack_grads(above, below, own, layers):
-    width = above.shape[1]
+    width = above[0].shape[-1]
     count = VECTORS * layers
     if own == UNIT:
         shapes = [
@@ -1081,7 +1229,7 @@
             lambda *refs: unpack_kernel(layers, *refs),
             out_shape=[jax.ShapeDtypeStruct(shape, F32) for shape in shapes],
             name="unpack",
-        )(above, below)
+        )(*above, *below)
         return outs[:5], outs[5:13], outs[13][0], outs[14][0], outs[15]
     parts = []
     for ref in (below, above):
@@ -1111,14 +1259,73 @@
     return swap(values, "tensor", bit)
 
 
-def scatter_start(mine, other, first):
-    held = mine.astype(F32) + pair_swap(other, 1).astype(F32)
-    return held, held[1].astype(BF16)
-
-
-def scatter_rest(held, sent, first, second):
-    held = held[0] + swap(sent, *first).astype(F32)
-    return held[0] + swap(held[1].astype(BF16), *second).astype(F32)
+def halve_kernel(mine_a, got_a, mine_b, got_b, _after_one, _after_two, keep_a, send_a, keep_b, send_b):
+    for mine, got, keep, send in ((mine_a, got_a, keep_a, send_a), (mine_b, got_b, keep_b, send_b)):
+        for i, out in enumerate((keep, send)):
+            out[...] = (mine[i].astype(F32) + got[i].astype(F32)).astype(BF16)
+
+
+def halve_after(mine_a, got_a, mine_b, got_b, *after):
+    width = mine_a.shape[-1]
+    count = mine_a[0].size // (mine_a.shape[-2] * width)
+    together = 2
+    inputs, specs, outs, out_specs = [], [], [], []
+    for mine, got in ((mine_a, got_a), (mine_b, got_b)):
+        rows = mine.shape[-2]
+        inputs += [part.reshape(2, count, rows, width) for part in (mine, got)]
+        specs += [pl.BlockSpec((2, together, rows, width), lambda i: (0, i, 0, 0))] * 2
+        outs += [jax.ShapeDtypeStruct((count, rows, width), BF16)] * 2
+        out_specs += [pl.BlockSpec((together, rows, width), lambda i: (i, 0, 0))] * 2
+    halves = pl.pallas_call(
+        halve_kernel,
+        grid=(count // together,),
+        in_specs=specs + [pl.BlockSpec(memory_space=pl.ANY)] * 2,
+        out_specs=out_specs,
+        out_shape=outs,
+        name="halve_after",
+    )(*inputs, after[0], after[-1])
+    shapes = [part.shape[1:] for part in (mine_a, mine_a, mine_b, mine_b)]
+    return [half.reshape(shape) for half, shape in zip(halves, shapes)]
+
+
+def join_kernel(kept_a, got_a, kept_b, got_b, _after_one, _after_two, rest, last):
+    rows = kept_a.shape[1]
+    for at, kept, got in ((slice(0, rows), kept_a, got_a), (slice(rows, None), kept_b, got_b)):
+        total = (kept[...].astype(F32) + got[...].astype(F32)).astype(BF16)
+        rest[:, at, :] = total[:-1]
+        last[at, :] = total[-1]
+
+
+def join_after(kept_a, got_a, kept_b, got_b, *after):
+    line, rows_a, width = kept_a.shape
+    rows = rows_a + kept_b.shape[1]
+    vmem = pl.BlockSpec(memory_space=pltpu.VMEM)
+    return pl.pallas_call(
+        join_kernel,
+        in_specs=[vmem] * 4 + [pl.BlockSpec(memory_space=pl.ANY)] * 2,
+        out_specs=[vmem] * 2,
+        out_shape=[
+            jax.ShapeDtypeStruct((line - 1, rows, width), BF16),
+            jax.ShapeDtypeStruct((rows, width), BF16),
+        ],
+        name="join_after",
+    )(kept_a, got_a, kept_b, got_b, after[0], after[-1])
+
+
+def stack_kernel(p0, p1, p2, p3, _after_one, _after_two, out):
+    for k, part in enumerate((p0, p1, p2, p3)):
+        out[k] = part[...]
+
+
+def stack_after(parts, *after):
+    vmem = pl.BlockSpec(memory_space=pltpu.VMEM)
+    return pl.pallas_call(
+        stack_kernel,
+        in_specs=[vmem] * 4 + [pl.BlockSpec(memory_space=pl.ANY)] * 2,
+        out_specs=vmem,
+        out_shape=jax.ShapeDtypeStruct((4,) + parts[0].shape, parts[0].dtype),
+        name="stack_after",
+    )(*parts, *after)
 
 
 def next_on_line(values):
@@ -1126,39 +1333,29 @@
     return lax.ppermute(values, "dp", [(i, (i + 2) % size) for i in range(size)])
 
 
-def scatter_line(held):
-    total = held[3]
-    for ahead in (2, 1, 0):
-        total = held[ahead] + next_on_line(total.astype(BF16)).astype(F32)
-    return total
-
-
-def gather_line(values):
+def scatter_line(rest, last):
+    totals = [last]
+    for ahead in (2, 1):
+        got = next_on_line(totals[-1])
+        totals.append((rest[ahead].astype(F32) + got.astype(F32)).astype(BF16))
+    return totals[1], totals[2], next_on_line(totals[2])
+
+
+def gather_line(values, *after):
     parts = [values]
-    for _ in range(lax.axis_size("dp") // 2 - 1):
-        parts.append(next_on_line(parts[-1]))
-    return jnp.stack(parts)
+    for step in range(lax.axis_size("dp") // 2 - 1):
+        sent = parts[-1] if step >= len(after) else tie(parts[-1], after[step])
+        parts.append(next_on_line(sent))
+    return parts
 
 
 def sum_grads(packed, rows_list, vector_rows):
-    dp_size = lax.axis_size("dp")
-    if dp_size == 8:
-        x, y = ("dp", 1), ("tensor", 2)
-        held_a, sent_a = scatter_start(packed[0], packed[1], y)
-        held_b, sent_b = scatter_start(packed[2], packed[3], x)
-
-        def rest():
-            halves = [scatter_rest(held_a, sent_a, y, x), scatter_rest(held_b, sent_b, x, y)]
-            return scatter_line(jnp.concatenate(halves, axis=1))
-
-        return sent_b, rest
     packed_a = jnp.stack(packed[:2]).transpose(3, 2, 1, 0, 4, 5)
     packed_b = jnp.stack(packed[2:]).transpose(3, 1, 2, 0, 4, 5)
     packed = jnp.concatenate([packed_a, packed_b], axis=4)
     packed = packed.reshape((BLOCKS,) + packed.shape[4:])
-    packed = to_devices(packed, 4 * dp_size, rows_list, vector_rows)
-    summed = lax.psum_scatter(packed, BOTH, scatter_dimension=0, tiled=True)[0]
-    return packed, lambda: summed
+    packed = to_devices(packed, 4 * lax.axis_size("dp"), rows_list, vector_rows)
+    return lax.psum_scatter(packed, BOTH, scatter_dimension=0, tiled=True)[0]
 
 
 def dp_bits():
@@ -1182,11 +1379,11 @@
 
 def reduce_relative(keep, send):
     bits = dp_bits()
-    keep = keep + swap(send, "dp", bits[0])
+    first = keep = keep + swap(send, "dp", bits[0])
     for bit in bits[1:]:
         half = keep.shape[0] // 2
         keep = keep[:half] + swap(keep[half:], "dp", bit)
-    return keep[0]
+    return keep[0], first
 
 
 def exchange_relative(first, second, third):
@@ -1242,32 +1439,20 @@
     ids_back = jnp.zeros_like(ids_rel).at[dp_index ^ places].set(ids_rel)
     if dp_size == 8:
         behind = (dp_index + dp_size - 2 * jnp.arange(dp_size // 2)) % dp_size
-        ids_back = jnp.take(ids_back, jnp.concatenate([behind, behind ^ 1]), axis=0)
-    ids_back = ids_back.reshape(2, -1)
+        ids_back = jnp.take(ids_back, jnp.stack([behind, behind ^ 1], axis=1).reshape(-1), axis=0)
+    ids_back = ids_back.reshape(4, -1)
+    ids_columns = [ids[:, None] for ids in ids_back]
     ids_rel = ids_rel.reshape(2, -1)
     own_rows = micro_count * own_entries * slot_count
-    looked = [
-        lookup(ids_rel[i], piece_table).reshape(dp_size // 2, tensor_size, own_rows, table_cols)
-        for i in (1, 0)
-    ]
-    looked = reduce_relative(looked[1], looked[0])
+    looked = []
+    for i in (1, 0):
+        rows = lookup(ids_rel[i], piece_table, looked[0] if looked else ids_rel)
+        looked.append(rows.reshape(dp_size // 2, tensor_size, own_rows, table_cols))
+    near_looked = looked[1]
+    looked, _ = reduce_relative(looked[1], looked[0])
     pieces = [looked[0], *exchange_relative(*looked[1:])]
 
-    packed, vectors, inner_bias = canonical(gathered, own, layer_count)
-    counts_own = lax.dynamic_slice_in_dim(piece_counts, tensor_index * own_entries, own_entries, 1)
-    valid = jnp.arange(slot_count)[None, :] < counts_own.reshape(-1)[:, None]
-    valid = valid.astype(F32).reshape(1, own_rows)
-    w_out = [w_output, pair_swap(w_output, 1), pair_swap(w_output, 2)]
-    *kept_hyper, pooled, pooled_norm, embeds = hyper_forward(
-        where, w_out[2], pieces, valid, vectors, inner_bias, packed, slot_count
-    )
-
-    w_out.append(pair_swap(w_out[2], 1))
-    embeds = embeds.reshape(micro_count, own_entries, lm_width)
-    embeds = [embeds, pair_swap(embeds, 1), pair_swap(embeds, 2)]
-    embeds.append(pair_swap(embeds[2], 1))
     text_rel = text_ids ^ (tensor_index * own_entries)
-
     micros = range(micro_count)
     ids_row, ids_own, ids_peer = [], [], []
     for micro in micros:
@@ -1275,22 +1460,40 @@
         ids_row.append(row)
         ids_own.append(lax.dynamic_slice_in_dim(row, tensor_index * share, share, 1))
         ids_peer.append(lax.dynamic_slice_in_dim(row, (tensor_index ^ 2) * share, share, 1))
-
-    def cots_of(micro, after):
-        own = cast_after(micro, cotangent, after)
-        peer = pair_swap(own, 2)
-        return (own, pair_swap(own, 1)), (peer, pair_swap(peer, 1))
-
+    ids_small = jnp.stack(ids_own + ids_peer)
+
+    packed = canonical(gathered, own, layer_count)
+    counts_own = lax.dynamic_slice_in_dim(piece_counts, tensor_index * own_entries, own_entries, 1)
+    valid = jnp.arange(slot_count)[None, :] < counts_own.reshape(-1)[:, None]
+    valid = valid.astype(F32).reshape(1, own_rows)
+    w_out = [w_output, pair_swap(w_output, 1), pair_swap(w_output, 2)]
+    cots = [cast_after(micro, cotangent, near_looked) for micro in range(micro_count)]
+    grads_near = [
+        [matmul_right_t(part, w_down).astype(BF16) for part in (cot, pair_swap(cot, 1))]
+        for cot in cots
+    ]
+    vectors, _, *kept_hyper, pooled, pooled_norm, embeds = hyper_forward(
+        where, (w_out[2], *grads_near[0], *grads_near[1], trig, ids_small, *ids_columns, ids_back), pieces, valid, packed, slot_count, layer_count
+    )
+
+    w_out.append(pair_swap(w_out[2], 1))
+    embeds = embeds.reshape(micro_count, own_entries, lm_width)
+    embeds = [embeds] + [pair_swap(embeds, k) for k in (1, 2, 3)]
+
+    def peer_cot(micro, after):
+        cot = pair_swap(tie(cots[micro], after), 2)
+        return cot, pair_swap(cot, 1)
+
+    cots_peer = [peer_cot(0, embeds[3])]
     kept_attn, contexts = [], []
     after = (embeds[0], embeds[0])
-    cots_near, cots_peer = cots_of(0, embeds[3])
     for micro in micros:
         near, far, *kept = attend(
             where, micro, embeds, gain_first, w_query, w_kv, ids_row[micro], trig, after
         )
         kept_attn.append(kept)
         contexts.append([near, *exchange_relative(far, near, far)])
-        after = (near, cots_peer[0])
+        after = (near, cots_peer[0][0])
 
     def after_attention(micro, after):
         own, peer, rows = hidden_rows_of(
@@ -1299,86 +1502,129 @@
         )
         return (own, pair_swap(own, 1)), (peer, pair_swap(peer, 1)), rows
 
-    def feed_forward(normed, cots, *after):
+    def feed_forward(normed, grads_in, *after):
         after = (after + after[:1] * 2)[:3]
-        return mlp(*normed, *cots, w_gate, w_up, w_down, after)
+        return mlp(*normed, *grads_in, w_gate, w_up, w_down, after)
 
     def travel(part):
-        away = (part[2].astype(F32) + pair_swap(part[3], 1).astype(F32)).astype(BF16)
+        from_core = jnp.concatenate([pair_swap(half, 1) for half in part[3:]])
+        away = (part[2].astype(F32) + from_core.astype(F32)).astype(BF16)
         return away, pair_swap(away, 2)
 
     def back_of(micro, rows, near, arrived):
         low, *parts = hidden_back(
-            micro, cotangent, rows, near[2], pair_swap(near[3], 1), arrived, gain_second, w_out
+            micro, cotangent, rows, near[2], [pair_swap(half, 1) for half in near[3:]], arrived,
+            gain_second, w_out,
         )
         return low, [parts[0], *exchange_relative(*parts[1:])]
 
-    def result_of(rows, near, peer, after):
-        away = add_after(peer[0], pair_swap(peer[1], 1), after)
-        total = rows + near[0].astype(F32) + pair_swap(near[1], 1).astype(F32)
-        return (total + pair_swap(away, 2).astype(F32)).astype(BF16)
+    def send_result(peer, after):
+        total = (peer[0].astype(F32) + pair_swap(peer[1], 1).astype(F32)).astype(BF16)
+        return pair_swap(tie(total, after), 2)
 
     near_in, peer_in, rows_a = after_attention(0, (contexts[1][0], contexts[1][0]))
-    near_a = feed_forward(near_in, cots_near, rows_a)
-    cots_near_b, cots_peer_b = cots_of(1, near_a[2])
-    peer_a = feed_forward(peer_in, cots_peer, near_a[2], contexts[1][2], contexts[1][3])
+    near_a = feed_forward(near_in, grads_near[0], rows_a)
+    cots_peer.append(peer_cot(1, near_a[2]))
+    peer_a = feed_forward(peer_in, cots_peer[0], near_a[2], contexts[1][2], contexts[1][3])
     away_a, arrived_a = travel(peer_a)
-    near_in, peer_in, rows_b = after_attention(1, (away_a, cots_peer_b[0]))
-    out_a = result_of(rows_a, near_a, peer_a, rows_b)
-    peer_b = feed_forward(peer_in, cots_peer_b, rows_b)
+    near_in, peer_in, rows_b = after_attention(1, (away_a, cots_peer[1][0]))
+    peer_b = feed_forward(peer_in, cots_peer[1], rows_b)
     away_b, arrived_b = travel(peer_b)
     low_a, parts_a = back_of(0, rows_a, near_a, arrived_a)
-    near_b = feed_forward(near_in, cots_near_b, low_a, out_a, away_b)
+    near_b = feed_forward(near_in, grads_near[1], low_a, away_b)
+    result_a = send_result(peer_a, near_b[2])
     low_b, parts_b = back_of(1, rows_b, near_b, arrived_b)
-    out_b = result_of(rows_b, near_b, peer_b, low_b)
 
     place = jnp.stack([tensor_index % 2, tensor_index // 2, dp_index % 2, dp_index // 2])
     place = place.astype(jnp.int32)
     grad_embeds = []
-    after = (low_b, low_b, low_b)
+    after = (low_b,) * 5
+    near_swapped = [pair_swap(near[1], 1) for near in (near_a, near_b)]
     for micro, parts, low in ((0, parts_a, low_a), (1, parts_b, low_b)):
         grads = attend_back(
             where, parts, kept_attn[micro], ids_row[micro], ids_own[micro], trig,
             w_query, w_kv, gain_first, low, after,
         )
-        after = (grads, out_b, out_b)
-        grads = grads.reshape(2, 2, own_entries, lm_width)
-        arrived = pair_swap(grads[:, 1], 1).astype(F32) + grads[:, 0].astype(F32)
-        arrived = arrived[0] + pair_swap(arrived[1].astype(BF16), 2).astype(F32)
-        grad_embeds.append(arrived.astype(BF16))
+        after = (grads[0], result_a, parts_b[2], *near_swapped)
+        if micro == 0:
+            result_b = send_result(peer_b, grads[0])
+        grad_embeds += [grads[0], *exchange_relative(*grads[1:])]
 
     if dp_size != 8:
         place = place * 0
-    source = (jnp.concatenate(grad_embeds, axis=0), pooled, pooled_norm)
-    above, after = (), pooled
-    rest = [None] * layer_count
+    source = (grad_embeds, pooled, pooled_norm)
+    packs, above, after = [None] * layer_count, (), (result_b, result_b)
+    near_side, near_chip = ("dp", 1), ("tensor", 2)
     for layer in range(layer_count - 1, -1, -1):
         *parts, source, small, inner_small = hyper_backward(
             place, layer, source, valid, vectors, kept_hyper, packed, slot_count, above,
             table_cols, after,
         )
         above = (small, inner_small)
-        rows_list = piece_rows(layer_count, UNIT) + ([UNIT] * 4 if layer == layer_count - 1 else [])
-        after, rest[layer] = sum_grads(parts, rows_list, 2 * UNIT if layer == 0 else 0)
-    reduced = [part() for part in rest]
-
-    if dp_size != 8:
-        source = jnp.take(source, tensor_index ^ jnp.arange(tensor_size), axis=0)
-    arrived = jnp.stack([source[0], *exchange_relative(*source[1:])])
+        packs[layer] = parts
+        if dp_size == 8 and layer == layer_count - 1:
+            upper = halve_after(
+                parts[0], pair_swap(parts[1], 1), parts[2], pair_swap(parts[3], 1), small
+            )
+            after = (upper[1], upper[3])
     if dp_size == 8:
-        arrived = gather_line(arrived)
-        halves = [arrived, swap(arrived, "dp", 1)]
+        parts = packs[0]
+        from_chip = pair_swap(source[2:], 2)
+        results = add_results(
+            (rows_a, near_a[0], near_swapped[0], result_a),
+            (rows_b, near_b[0], near_swapped[1], result_b),
+            parts[0],
+        )
+        upper = halve_after(
+            upper[0], swap(upper[1], *near_chip), upper[2], swap(upper[3], *near_side), results
+        )
+        upper_got = swap(upper[3], *near_chip)
+        other_a, other_b = tie(parts[1], upper[1]), tie(parts[3], upper[1])
+        from_chip = pair_swap(source[2:], 2)
+        lower = halve_after(
+            parts[0], pair_swap(other_a, 1), parts[2], pair_swap(other_b, 1), upper[1]
+        )
+        near_piece, forward = tie(source[1], lower[1]), tie(from_chip[1], lower[1])
+        pieces = [source[0], pair_swap(near_piece, 1), from_chip[0], pair_swap(forward, 1)]
+        pieces = stack_after(pieces, upper_got, lower[1])
+        upper_rest, last = join_after(
+            upper[0], swap(upper[1], *near_side), upper[2], upper_got, pieces
+        )
+        sent = [tie(lower[1], last), tie(lower[3], last)]
+        pieces = gather_line(jnp.stack([pieces, swap(pieces, "dp", 1)]), last)
+        pieces = [part.reshape(-1, table_cols) for part in pieces]
+        step_one, step_two, upper_got = scatter_line(upper_rest, last)
+        table_grad = collect(ids_back[:2], ids_columns[:2], pieces[0], pieces[1], table_rows, None)
+        lower = halve_after(
+            lower[0], swap(sent[0], *near_chip), lower[2], swap(sent[1], *near_side), last
+        )
+        lower_rest, last = join_after(
+            lower[0], swap(lower[1], *near_side), lower[2], swap(lower[3], *near_chip), table_grad, step_two
+        )
+        *_, lower_got = scatter_line(lower_rest, last)
+        reduced = [(lower_rest, lower_got), (upper_rest, upper_got)]
     else:
-        halves = jnp.split(lax.all_gather(arrived, "dp", axis=0), 2)
-    table_grad = None
-    for ids, rows in zip(ids_back, halves):
-        table_grad = collect(ids, rows.reshape(-1, table_cols), table_rows, table_grad)
+        pieces = jnp.take(source, tensor_index ^ jnp.arange(tensor_size), axis=0)
+        pieces = jnp.stack([pieces[0], *exchange_relative(*pieces[1:])])
+        pieces = lax.all_gather(pieces, "dp", axis=0).reshape(4, -1, table_cols)
+        rows_list = piece_rows(layer_count, UNIT)
+        reduced = [
+            sum_grads(packs[0], rows_list, 2 * UNIT),
+            sum_grads(packs[1], rows_list + [UNIT] * 4, 0),
+        ]
+        table_grad = collect(ids_back[:2], ids_columns[:2], pieces[0], pieces[1], table_rows, None)
+        results = add_results(
+            (rows_a, near_a[0], near_swapped[0], result_a),
+            (rows_b, near_b[0], near_swapped[1], result_b),
+            table_grad,
+        )
+    table_grad = collect(ids_back[2:], ids_columns[2:], pieces[2], pieces[3], table_rows, table_grad)
 
     mats, vecs, out_final_gain, out_final_bias, out_inner_bias = unpack_grads(
         reduced[1], reduced[0], own, layer_count
     )
     return (
-        jnp.stack([out_a, out_b]),
+        results,
         table_grad,
         vecs[0],
         vecs[1],

time: 692 us -> 662 us (0.957)
  waiting for transfers between devices: 186 us -> 132 us
  local copies, waits for them, and re-layouts: 33 us -> 55.1 us
  matrix products: 0 us -> 20.9 us
  other arithmetic: 36.4 us -> 21.1 us
    ppermute x69 -> x75, waiting for transfers between devices: 123 us -> 82.9 us  [swap(): return lax.ppermute(values, axis, [(i, i ^ bit) for i in range(size)])]
    all_gather x1, waiting for transfers between devices: 29.3 us -> 6.26 us  [local(): gathered = lax.all_gather(pack_shards(shard_params), BOTH, axis=0)]
    dot_general x0 -> x4, matrix products: none -> 20.9 us  [matmul_right_t(): lax.dot_general(left, right, (((1,), (1,)), ((), ())), preferred_element_...]
    add x17 -> x1, other arithmetic: 17 us -> 1.52 us  [reduce_relative(): first = keep = keep + swap(send, 'dp', bits[0])]
    unnamed x130 -> x199, local copies, waits for them, and re-layouts: 15.8 us -> 28.6 us
    pallas_call x12 -> x29, Pallas kernels: 162 us -> 174 us  [the longest x4 95.4 us: mlp(): pl.pallas_call(lambda *refs: mlp_kernel(ready, *refs), in_specs=[vmem] *...]
    another operation x5 -> x9, local copies, waits for them, and re-layouts: 0.6 us -> 9.62 us  [local(): ids_columns = [ids[:, None] for ids in ids_back]]
    ppermute x9, waiting for transfers between devices: 33.5 us -> 42.4 us  [next_on_line(): lax.ppermute(values, 'dp', [(i, (i + 2) % size) for i in range(size)])]
  transfers between devices with their start and end apart: 79 -> 85, of which waited for: 33 -> 28; matrix products, arithmetic and copies ran while one was open for 8% -> 11% of each run, Pallas kernels for 44% -> 46%
where the time goes in v3:
time: 662 us; the launch traced here: 653 us
  Pallas kernels  354 us (53%)
  waiting for transfers between devices  132 us (20%)
  local copies, waits for them, and re-layouts  55.1 us (8%)
  starting transfers between devices  54.7 us (8%)
  other arithmetic  21.1 us (3%)
  matrix products  20.9 us (3%)
  between operations  15.6 us (2%)
    pallas_call x4, Pallas kernels, mlp(): pl.pallas_call(lambda *refs: mlp_kernel(ready, *refs), in_specs=[vmem] *...  95.4 us
    ppermute x75, waiting for transfers between devices, swap(): return lax.ppermute(values, axis, [(i, i ^ bit) for i in range(size)])  82.9 us
    ppermute x75, starting transfers between devices, swap(): return lax.ppermute(values, axis, [(i, i ^ bit) for i in range(size)])  52.1 us
    pallas_call x2, Pallas kernels, attend_back(): pl.pallas_call(attend_back_kernel, grid=(pairs,), in_specs=[pl.BlockSpec(...  51.6 us
    ppermute x9, waiting for transfers between devices, next_on_line(): lax.ppermute(values, 'dp', [(i, (i + 2) % size) for i in range(size)])  42.4 us
    pallas_call x2, Pallas kernels, attend(): pl.pallas_call(attend_kernel, grid=(pairs,), in_specs=[pl.BlockSpec(memor...  41.6 us
    pallas_call x2, Pallas kernels, hyper_backward(): pl.pallas_call(lambda *refs: hyper_back_kernel(slots, layer, layers, last...  35.6 us
    unnamed x199, local copies, waits for them, and re-layouts  28.6 us
  transfers between devices with their start and end apart: 85, of which 28 were waited for; matrix products, arithmetic and copies ran while one was open for 11% of the time, Pallas kernels for 46%

profile of v3, /device:TPU:0, one launch (start us, length us, event | category | flops | bytes accessed | tf_op | source)
XLA Modules:
  0.0 653.2 jit_solution(2248086196776201278)
XLA Ops:
  37.5 6.8 %lookup.2 = bf16[4096,128]{1,0:T(8,128)(2,1)} custom-call(s32[4096,1]{1,0:T(8,128)S(1)} %copy-done.8, bf16[4096,128]{1,0:T(8,128)(2,1)S(1)} %copy-done.11, s32[2,4096]{1,0:T(2,128)S(1)} %reshape.292._after), custom_call_target="tpu_custom_call" | custom-call | flops 8589934592 | bytes 2097152 | tf_op jit(solution)/shard_map/lookup/pallas_call | solution.py:84
  64.8 18.1 %collective-permute-done.6 = bf16[4,4,256,128]{3,2,1,0:T(8,128)(2,1)} collective-permute-done((bf16[4,4,256,128]{3,2,1,0:T(8,128)(2,1)}, bf16[4,4,256,128]{3,2,1,0:T(8,128)(2,1)}, u32[]{:S(2)}, u32[]{:S(2)}) %collective-permute-start.6) | collective-permute-done | bytes 1048608 | tf_op jit(solution)/shard_map/ppermute | solution.py:64
  116.7 22.9 %collective-permute-done.8 = bf16[1,4,256,128]{3,2,1,0:T(8,128)(2,1)S(1)} collective-permute-done((bf16[1,4,256,128]{3,2,1,0:T(8,128)(2,1)S(1)}, bf16[1,4,256,128]{3,2,1,0:T(8,128)(2,1)S(1)}, u32[]{:S(2)}, u32[]{:S(2)}) %collective-permute-start.8) | collective-permute-done | bytes 262176 | tf_op jit(solution)/shard_map/ppermute | solution.py:64
  146.1 6.3 all-gather.3.cloned.1.call-done
  152.4 17.1 %hyper.1 = (f32[18,512]{1,0:T(8,128)}, f32[2,2048]{1,0:T(2,128)}, f32[2,256,512]{2,1,0:T(8,128)}, bf16[2,256,1536]{2,1,0:T(8,128)(2,1)}, bf16[2,256,512]{2,1,0:T...) custom-call(s32[1]{0:T(128)} %bitcast.refs_0_.place, ...), custom_call_target="tpu_custom_call" | custom-call | flops 8000000000 | bytes 25000000 | tf_op jit(solution)/shard_map/hyper/pallas_call | solution.py:831
  181.3 20.9 %attend.2 = (bf16[2,256,512]{2,1,0:T(8,128)(2,1)}, bf16[2,256,512]{2,1,0:T(8,128)(2,1)}, bf16[512,1024]{1,0:T(8,128)(2,1)}, f32[4,2,1024]{2,1,0:T(2,128)}, bf16[...) custom-call(s32[1]{0:T(128)} %bitcast.refs_0_.place, ...), custom_call_target="tpu_custom_call" | custom-call | flops 12000000000 | bytes 8000000 | tf_op jit(solution)/shard_map/attend/pallas_call | solution.py:244
  205.7 20.7 %attend.3 = (bf16[2,256,512]{2,1,0:T(8,128)(2,1)}, bf16[2,256,512]{2,1,0:T(8,128)(2,1)}, bf16[512,1024]{1,0:T(8,128)(2,1)}, f32[4,2,1024]{2,1,0:T(2,128)}, bf16[...) custom-call(s32[1]{0:T(128)} %bitcast.refs_0_.place, ...), custom_call_target="tpu_custom_call" | custom-call | flops 12000000000 | bytes 8000000 | tf_op jit(solution)/shard_map/attend/pallas_call | solution.py:244
  229.1 11.7 %hidden.2 = (bf16[256,2048]{1,0:T(8,128)(2,1)}, bf16[256,2048]{1,0:T(8,128)(2,1)}, f32[256,2048]{1,0:T(8,128)}) custom-call(bf16[64,2048]{1,0:T(8,128)(2,1)} %get-tuple-element.134.embeds, s32[1,256]{1,0:T(1,128)} %copy-done.66, s32[1,256]{1,0:T(1,128)} %copy-done.68, bf16[1,2048]{1,0:T(2,128)(2,1)} %broadcast_in_dim.58.gain, ...), custom_call_target="tpu_custom_call" | custom-call | flops 6000000000 | bytes 18000000 | tf_op jit(solution)/shard_map/hidden/pallas_call | solution.py:476
  244.7 21.9 %mlp.4 = (bf16[256,2048]{1,0:T(8,128)(2,1)}, bf16[256,2048]{1,0:T(8,128)(2,1)}, bf16[256,2048]{1,0:T(8,128)(2,1)}, bf16[128,2048]{1,0:T(8,128)(2,1)}, bf16[128,2048]{1,0:T(8,128)(2,1)}) custom-call(bf16[256,2048]{1,0:T(8,128)(2,1)} %get-tuple-element.139.refs_0_, bf16[256,2048]{1,0:T(8,128)(2,1)} %copy-done.78, ...), custom_call_target="tpu_custom_call" | custom-call | flops 17716740096 | bytes 26000000 | tf_op jit(solution)/shard_map/mlp/pallas_call | solution.py:603
  269.2 25.8 %mlp.5 = (bf16[256,2048]{1,0:T(8,128)(2,1)}, bf16[256,2048]{1,0:T(8,128)(2,1)}, bf16[256,2048]{1,0:T(8,128)(2,1)}, bf16[128,2048]{1,0:T(8,128)(2,1)}, bf16[128,2048]{1,0:T(8,128)(2,1)}) custom-call(bf16[256,2048]{1,0:T(8,128)(2,1)} %get-tuple-element.142.refs_0_, bf16[256,2048]{1,0:T(8,128)(2,1)} %copy-done.74, bf16[256,2048]{1,0:T(8,128)(2,1)} %copy-done.71, ...), custom_call_target="tpu_custom_call" | custom-call | flops 17716740096 | bytes 26000000 | tf_op jit(solution)/shard_map/mlp/pallas_call | solution.py:603
  301.7 12.0 %hidden.3 = (bf16[256,2048]{1,0:T(8,128)(2,1)}, bf16[256,2048]{1,0:T(8,128)(2,1)}, f32[256,2048]{1,0:T(8,128)}) custom-call(bf16[64,2048]{1,0:T(8,128)(2,1)} %get-tuple-element.147.embeds, s32[1,256]{1,0:T(1,128)} %copy-done.65, s32[1,256]{1,0:T(1,128)} %copy-done.67, bf16[1,2048]{1,0:T(2,128)(2,1)} %broadcast_in_dim.58.gain, ...), custom_call_target="tpu_custom_call" | custom-call | flops 6000000000 | bytes 18000000 | tf_op jit(solution)/shard_map/hidden/pallas_call | solution.py:476
  321.3 25.6 %mlp.6 = (bf16[256,2048]{1,0:T(8,128)(2,1)}, bf16[256,2048]{1,0:T(8,128)(2,1)}, bf16[256,2048]{1,0:T(8,128)(2,1)}, bf16[128,2048]{1,0:T(8,128)(2,1)}, bf16[128,2048]{1,0:T(8,128)(2,1)}) custom-call(bf16[256,2048]{1,0:T(8,128)(2,1)} %get-tuple-element.155.refs_0_, bf16[256,2048]{1,0:T(8,128)(2,1)} %copy-done.76, bf16[256,2048]{1,0:T(8,128)(2,1)} %copy-done.73, ...), custom_call_target="tpu_custom_call" | custom-call | flops 17716740096 | bytes 26000000 | tf_op jit(solution)/shard_map/mlp/pallas_call | solution.py:603
  349.4 8.5 %hidden_back.2 = (bf16[256,2048]{1,0:T(8,128)(2,1)}, bf16[256,512]{1,0:T(8,128)(2,1)}, bf16[256,512]{1,0:T(8,128)(2,1)}, bf16[256,512]{1,0:T(8,128)(2,1)}, bf16[256,512]{1,0:T(8,128)(2,1)}) custom-call(f32[2,256,2048]{2,1,0:T(8,128)} %cotangent.3, f32[256,2048]{1,0:T(8,128)} %get-tuple-element.138.refs_7_.refs_8_.refs_9_.hidden.refs_0_, ...), custom_call_target="tpu_custom_call" | custom-call | flops 2000000000 | bytes 16000000 | tf_op jit(solution)/shard_map/hidden_back/pallas_call | solution.py:518
  362.4 22.2 %mlp.7 = (bf16[256,2048]{1,0:T(8,128)(2,1)}, bf16[256,2048]{1,0:T(8,128)(2,1)}, bf16[256,2048]{1,0:T(8,128)(2,1)}, bf16[128,2048]{1,0:T(8,128)(2,1)}, bf16[128,2048]{1,0:T(8,128)(2,1)}) custom-call(bf16[256,2048]{1,0:T(8,128)(2,1)} %get-tuple-element.151.refs_0_, bf16[256,2048]{1,0:T(8,128)(2,1)} %collective-permute-done.32.refs_1_, ...), custom_call_target="tpu_custom_call" | custom-call | flops 17716740096 | bytes 26000000 | tf_op jit(solution)/shard_map/mlp/pallas_call | solution.py:603
  392.1 8.6 %hidden_back.3 = (bf16[256,2048]{1,0:T(8,128)(2,1)}, bf16[256,512]{1,0:T(8,128)(2,1)}, bf16[256,512]{1,0:T(8,128)(2,1)}, bf16[256,512]{1,0:T(8,128)(2,1)}, bf16[256,512]{1,0:T(8,128)(2,1)}) custom-call(f32[2,256,2048]{2,1,0:T(8,128)} %cotangent.3, f32[256,2048]{1,0:T(8,128)} %get-tuple-element.156.refs_7_.refs_8_.refs_9_.hidden.refs_4_, ...), custom_call_target="tpu_custom_call" | custom-call | flops 2000000000 | bytes 16000000 | tf_op jit(solution)/shard_map/hidden_back/pallas_call | solution.py:518
  403.1 26.0 %attend_back.2 = (bf16[16,2048]{1,0:T(8,128)(2,1)}, bf16[16,2048]{1,0:T(8,128)(2,1)}, bf16[16,2048]{1,0:T(8,128)(2,1)}, bf16[16,2048]{1,0:T(8,128)(2,1)}) custom-call(s32[1]{0:T(128)} %bitcast.refs_0_.place, bf16[256,512]{1,0:T(8,128)(2,1)} %get-tuple-element.165.part0, bf16[256,512]{1,0:T(8,128)(2,1)} %copy-done.86, bf16[256,512]{1,0:T(8,128)(2,1)} %copy-done.87, ...), custom_call_target="tpu_custom_call" | custom-call | flops 24999999488 | bytes 8000000 | tf_op jit(solution)/shard_map/attend_back/pallas_call | solution.py:387
  434.9 25.6 %attend_back.3 = (bf16[16,2048]{1,0:T(8,128)(2,1)}, bf16[16,2048]{1,0:T(8,128)(2,1)}, bf16[16,2048]{1,0:T(8,128)(2,1)}, bf16[16,2048]{1,0:T(8,128)(2,1)}) custom-call(s32[1]{0:T(128)} %bitcast.refs_0_.place, bf16[256,512]{1,0:T(8,128)(2,1)} %get-tuple-element.180.part0, bf16[256,512]{1,0:T(8,128)(2,1)} %collective-permute-done.53.part1, ...), custom_call_target="tpu_custom_call" | custom-call | flops 24999999488 | bytes 8000000 | tf_op jit(solution)/shard_map/attend_back/pallas_call | solution.py:387
  468.1 18.9 %hyper_back.2 = (bf16[2,2,4,128,512]{4,3,2,1,0:T(8,128)(2,1)}, bf16[2,2,4,128,512]{4,3,2,1,0:T(8,128)(2,1)}, bf16[2,2,4,128,512]{4,3,2,1,0:T(8,128)(2,1)}, bf16[...) custom-call(s32[4]{0:T(128)} %pad_add_fusion.5.refs_0_, ...), custom_call_target="tpu_custom_call" | custom-call | flops 8000000000 | bytes 25000000 | tf_op jit(solution)/shard_map/hyper_back/pallas_call | solution.py:1072
  504.0 16.7 %hyper_back.3 = (bf16[2,2,4,112,512]{4,3,2,1,0:T(8,128)(2,1)}, bf16[2,2,4,112,512]{4,3,2,1,0:T(8,128)(2,1)}, bf16[2,2,4,112,512]{4,3,2,1,0:T(8,128)(2,1)}, bf16[...) custom-call(s32[4]{0:T(128)} %pad_add_fusion.5.refs_0_, ...), custom_call_target="tpu_custom_call" | custom-call | flops 8000000000 | bytes 25000000 | tf_op jit(solution)/shard_map/hyper_back/pallas_call | solution.py:1072
  569.0 15.3 %collective-permute-done.75 = bf16[256,512]{1,0:T(8,128)(2,1)S(1)} collective-permute-done((bf16[256,512]{1,0:T(8,128)(2,1)}, bf16[256,512]{1,0:T(8,128)(2,1)S(1)}, u32[]{:S(2)}, u32[]{:S(2)}) %collective-permute-start.75) | collective-permute-done | bytes 262176 | tf_op jit(solution)/shard_map/ppermute | solution.py:1333
  591.2 7.6 %collect.2.base_ref._after_one = f32[4096,128]{1,0:T(8,128)S(1)} custom-call(s32[2,2048]{1,0:T(2,128)S(1)} %slice.98.refs_0_, s32[2048,1]{1,0:T(8,128)S(1)} %copy-done.6, s32[2048,1]{1,0:T(8,128)S(1)} %copy-done.7, bf16[2048,128]{1,0:T(8,128)(2,1)S(1)} %bitcast.121, bf16[2048,128]{1,0:T(8,128)(2,1)} %bitcast.46.refs_4_), custom_call_target="tpu_custom_call" | custom-call | flops 8589934592 | bytes 2097152 | tf_op jit(solution)/shard_map/collect/pallas_call | solution.py:131
  605.3 9.1 %collective-permute-done.81 = bf16[224,512]{1,0:T(8,128)(2,1)S(1)} collective-permute-done((bf16[224,512]{1,0:T(8,128)(2,1)}, bf16[224,512]{1,0:T(8,128)(2,1)S(1)}, u32[]{:S(2)}, u32[]{:S(2)}) %collective-permute-start.81) | collective-permute-done | bytes 229408 | tf_op jit(solution)/shard_map/ppermute | solution.py:1333
  616.6 13.9 %collective-permute-done.82 = bf16[224,512]{1,0:T(8,128)(2,1)} collective-permute-done((bf16[224,512]{1,0:T(8,128)(2,1)S(1)}, bf16[224,512]{1,0:T(8,128)(2,1)}, u32[]{:S(2)}, u32[]{:S(2)}) %collective-permute-start.82) | collective-permute-done | bytes 229408 | tf_op jit(solution)/shard_map/ppermute | solution.py:1333
  633.3 9.0 %collect.3 = f32[4096,128]{1,0:T(8,128)} custom-call(s32[2,2048]{1,0:T(2,128)S(1)} %slice.91.ids_ref, s32[2048,1]{1,0:T(8,128)S(1)} %copy-done.4, s32[2048,1]{1,0:T(8,128)S(1)} %copy-done.5, bf16[2048,128]{1,0:T(8,128)(2,1)S(1)} %bitcast.122, bf16[2048,128]{1,0:T(8,128)(2,1)} %bitcast.44.right_ref, f32[4096,128]{1,0:T(8,128)S(1)} %copy-done.10), custom_call_target="tpu_custom_call" | custom-call | flops 8589934592 | bytes 2097152 | tf_op jit(solution)/shard_map/collect/pallas_call | solution.py:131
  (479 shorter events, 246.6 us)
Async XLA Ops:
  7.3 145.1 %all-gather.3.cloned.1.call-start = ((), (), s32[]{:S(2)}) async-start(), calls=%async_computation | async-start | bytes 16220160 | tf_op jit(solution)/shard_map/all_gather | solution.py:1431
  9.4 136.8 %collective-permute-start = (bf16[512,2048]{1,0:T(8,128)(2,1)}, bf16[512,2048]{1,0:T(8,128)(2,1)}, u32[]{:S(2)}, u32[]{:S(2)}) collective-permute-start(bf16[512,2048]{1,0:T(8,128)(2,1)} %w0.7), channel_id=1, source_target_pairs={{0,2},{1,3},{2,0},{3,1},{4,6},{5,7},{6,4},{7,5},{8,10},{9,11},{10,... | collective-permute-start | bytes 6291464 | tf_op jit(solution)/shard_map/ppermute | solution.py:64
  12.4 214.1 %collective-permute-start.18 = (bf16[512,2048]{1,0:T(8,128)(2,1)}, bf16[512,2048]{1,0:T(8,128)(2,1)}, u32[]{:S(2)}, u32[]{:S(2)}) collective-permute-start(bf16[512,2048]{1,0:T(8,128)(2,1)} %w0.7), channel_id=1, source_target_pairs={{0,1},{1,0},{2,3},{3,2},{4,5},{5,4},{6,7},{7,6},{8,9},{9,8},{10,11... | collective-permute-start | bytes 6291464 | tf_op jit(solution)/shard_map/ppermute | solution.py:64
  44.3 38.6 %collective-permute-start.6 = (bf16[4,4,256,128]{3,2,1,0:T(8,128)(2,1)}, bf16[4,4,256,128]{3,2,1,0:T(8,128)(2,1)}, u32[]{:S(2)}, u32[]{:S(2)}) collective-permute-start(bf16[4,4,256,128]{3,2,1,0:T(8,128)(2,1)} %bitcast.3._after), channel_id=1, source_target_pairs={{0,4},{4,0},{8,12},{12,8},{16,20},{20,16},{24,28},{28,24},{1,5},{5... | collective-permute-start | bytes 3145736 | tf_op jit(solution)/shard_map/ppermute | solution.py:64
  59.1 51.7 %collective-permute-start.4 = (bf16[256,2048]{1,0:T(8,128)(2,1)}, bf16[256,2048]{1,0:T(8,128)(2,1)}, u32[]{:S(2)}, u32[]{:S(2)}) collective-permute-start(bf16[256,2048]{1,0:T(8,128)(2,1)} %cast_after.2._values), channel_id=1, source_target_pairs={{0,1},{1,0},{2,3},{3,2},{4,5},{5,4},{6,7},{7,6},{8,9},{9,8},{10,11... | collective-permute-start | bytes 3145736 | tf_op jit(solution)/shard_map/ppermute | solution.py:64
  92.2 48.2 %collective-permute-start.5 = (bf16[256,2048]{1,0:T(8,128)(2,1)S(1)}, bf16[256,2048]{1,0:T(8,128)(2,1)}, u32[]{:S(2)}, u32[]{:S(2)}) collective-permute-start(bf16[256,2048]{1,0:T(8,128)(2,1)S(1)} %copy-done.19), channel_id=1, source_target_pairs={{0,1},{1,0},{2,3},{3,2},{4,5},{5,4},{6,7},{7,6},{8,9},{9,8},{10,11... | collective-permute-start | bytes 3145736 | tf_op jit(solution)/shard_map/ppermute | solution.py:64
  172.6 53.9 %collective-permute-start.19 = (bf16[512,2048]{1,0:T(8,128)(2,1)}, bf16[512,2048]{1,0:T(8,128)(2,1)S(1)}, u32[]{:S(2)}, u32[]{:S(2)}) collective-permute-start(bf16[512,2048]{1,0:T(8,128)(2,1)} %collective-permute-done.refs_1_.w2), channel_id=1, source_target_pairs={{0,1},{1,0},{2,3},{3,2},{4,5},{5,4},{6,7},{7,6},{8,9},{9,8},{10,11... | collective-permute-start | bytes 6291464 | tf_op jit(solution)/shard_map/ppermute | solution.py:64
  266.6 33.8 %collective-permute-start.31 = (bf16[256,2048]{1,0:T(8,128)(2,1)}, bf16[256,2048]{1,0:T(8,128)(2,1)S(1)}, u32[]{:S(2)}, u32[]{:S(2)}) collective-permute-start(bf16[256,2048]{1,0:T(8,128)(2,1)} %tie.12), channel_id=1, source_target_pairs={{0,2},{1,3},{2,0},{3,1},{4,6},{5,7},{6,4},{7,5},{8,10},{9,11},{10,... | collective-permute-start | bytes 3145736 | tf_op jit(solution)/shard_map/ppermute | solution.py:64
  314.2 32.9 %collective-permute-start.33 = (bf16[128,2048]{1,0:T(8,128)(2,1)S(1)}, bf16[128,2048]{1,0:T(8,128)(2,1)}, u32[]{:S(2)}, u32[]{:S(2)}) collective-permute-start(bf16[128,2048]{1,0:T(8,128)(2,1)S(1)} %copy-done.80), channel_id=1, source_target_pairs={{0,1},{1,0},{2,3},{3,2},{4,5},{5,4},{6,7},{7,6},{8,9},{9,8},{10,11... | collective-permute-start | bytes 1572872 | tf_op jit(solution)/shard_map/ppermute | solution.py:64
  314.3 33.1 %collective-permute-start.34 = (bf16[128,2048]{1,0:T(8,128)(2,1)S(1)}, bf16[128,2048]{1,0:T(8,128)(2,1)S(1)}, u32[]{:S(2)}, u32[]{:S(2)}) collective-permute-start(bf16[128,2048]{1,0:T(8,128)(2,1)S(1)} %copy-done.79), channel_id=1, source_target_pairs={{0,1},{1,0},{2,3},{3,2},{4,5},{5,4},{6,7},{7,6},{8,9},{9,8},{10,11... | collective-permute-start | bytes 1572872 | tf_op jit(solution)/shard_map/ppermute | solution.py:64
  314.7 33.7 %collective-permute-start.35 = (bf16[256,2048]{1,0:T(8,128)(2,1)S(1)}, bf16[256,2048]{1,0:T(8,128)(2,1)S(1)}, u32[]{:S(2)}, u32[]{:S(2)}) collective-permute-start(bf16[256,2048]{1,0:T(8,128)(2,1)S(1)} %copy-done.30), channel_id=1, source_target_pairs={{0,2},{1,3},{2,0},{3,1},{4,6},{5,7},{6,4},{7,5},{8,10},{9,11},{10,... | collective-permute-start | bytes 3145736 | tf_op jit(solution)/shard_map/ppermute | solution.py:64
  316.5 45.9 %collective-permute-start.32 = (bf16[256,2048]{1,0:T(8,128)(2,1)}, bf16[256,2048]{1,0:T(8,128)(2,1)}, u32[]{:S(2)}, u32[]{:S(2)}) collective-permute-start(bf16[256,2048]{1,0:T(8,128)(2,1)} %get-tuple-element.151.refs_0_), channel_id=1, source_target_pairs={{0,1},{1,0},{2,3},{3,2},{4,5},{5,4},{6,7},{7,6},{8,9},{9,8},{10,11... | collective-permute-start | bytes 3145736 | tf_op jit(solution)/shard_map/ppermute | solution.py:64
  348.2 52.5 %collective-permute-start.22 = (bf16[256,2048]{1,0:T(8,128)(2,1)}, bf16[256,2048]{1,0:T(8,128)(2,1)S(1)}, u32[]{:S(2)}, u32[]{:S(2)}) collective-permute-start(bf16[256,2048]{1,0:T(8,128)(2,1)} %get-tuple-element.141), channel_id=1, source_target_pairs={{0,1},{1,0},{2,3},{3,2},{4,5},{5,4},{6,7},{7,6},{8,9},{9,8},{10,11... | collective-permute-start | bytes 3145736 | tf_op jit(solution)/shard_map/ppermute | solution.py:64
  348.4 36.3 %collective-permute-start.27 = (bf16[256,2048]{1,0:T(8,128)(2,1)}, bf16[256,2048]{1,0:T(8,128)(2,1)S(1)}, u32[]{:S(2)}, u32[]{:S(2)}) collective-permute-start(bf16[256,2048]{1,0:T(8,128)(2,1)} %get-tuple-element.146), channel_id=1, source_target_pairs={{0,1},{1,0},{2,3},{3,2},{4,5},{5,4},{6,7},{7,6},{8,9},{9,8},{10,11... | collective-permute-start | bytes 3145736 | tf_op jit(solution)/shard_map/ppermute | solution.py:64
  360.9 30.2 %collective-permute-start.48 = (bf16[256,2048]{1,0:T(8,128)(2,1)}, bf16[256,2048]{1,0:T(8,128)(2,1)}, u32[]{:S(2)}, u32[]{:S(2)}) collective-permute-start(bf16[256,2048]{1,0:T(8,128)(2,1)} %add_convert_fusion.1.refs_8_), channel_id=1, source_target_pairs={{0,2},{1,3},{2,0},{3,1},{4,6},{5,7},{6,4},{7,5},{8,10},{9,11},{10,... | collective-permute-start | bytes 3145736 | tf_op jit(solution)/shard_map/ppermute | solution.py:64
  391.2 38.0 %collective-permute-start.40 = (bf16[256,2048]{1,0:T(8,128)(2,1)S(1)}, bf16[256,2048]{1,0:T(8,128)(2,1)S(1)}, u32[]{:S(2)}, u32[]{:S(2)}) collective-permute-start(bf16[256,2048]{1,0:T(8,128)(2,1)S(1)} %copy-done.15), channel_id=1, source_target_pairs={{0,2},{1,3},{2,0},{3,1},{4,6},{5,7},{6,4},{7,5},{8,10},{9,11},{10,... | collective-permute-start | bytes 3145736 | tf_op jit(solution)/shard_map/ppermute | solution.py:64
  400.7 29.5 %collective-permute-start.41 = (bf16[256,2048]{1,0:T(8,128)(2,1)}, bf16[256,2048]{1,0:T(8,128)(2,1)}, u32[]{:S(2)}, u32[]{:S(2)}) collective-permute-start(bf16[256,2048]{1,0:T(8,128)(2,1)} %get-tuple-element.162), channel_id=1, source_target_pairs={{0,1},{1,0},{2,3},{3,2},{4,5},{5,4},{6,7},{7,6},{8,9},{9,8},{10,11... | collective-permute-start | bytes 3145736 | tf_op jit(solution)/shard_map/ppermute | solution.py:64
  400.9 29.6 %collective-permute-start.53 = (bf16[256,512]{1,0:T(8,128)(2,1)}, bf16[256,512]{1,0:T(8,128)(2,1)}, u32[]{:S(2)}, u32[]{:S(2)}) collective-permute-start(bf16[256,512]{1,0:T(8,128)(2,1)} %get-tuple-element.181), channel_id=1, source_target_pairs={{0,1},{1,0},{2,3},{3,2},{4,5},{5,4},{6,7},{7,6},{8,9},{9,8},{10,11... | collective-permute-start | bytes 786440 | tf_op jit(solution)/shard_map/ppermute | solution.py:64
  401.3 30.2 %collective-permute-start.54 = (bf16[256,512]{1,0:T(8,128)(2,1)}, bf16[256,512]{1,0:T(8,128)(2,1)}, u32[]{:S(2)}, u32[]{:S(2)}) collective-permute-start(bf16[256,512]{1,0:T(8,128)(2,1)} %get-tuple-element.182), channel_id=1, source_target_pairs={{0,2},{1,3},{2,0},{3,1},{4,6},{5,7},{6,4},{7,5},{8,10},{9,11},{10,... | collective-permute-start | bytes 786440 | tf_op jit(solution)/shard_map/ppermute | solution.py:64
  402.4 31.8 %collective-permute-start.55 = (bf16[256,512]{1,0:T(8,128)(2,1)}, bf16[256,512]{1,0:T(8,128)(2,1)S(1)}, u32[]{:S(2)}, u32[]{:S(2)}) collective-permute-start(bf16[256,512]{1,0:T(8,128)(2,1)} %get-tuple-element.183), channel_id=1, source_target_pairs={{0,3},{1,2},{2,1},{3,0},{4,7},{5,6},{6,5},{7,4},{8,11},{9,10},{10,... | collective-permute-start | bytes 786440 | tf_op jit(solution)/shard_map/ppermute | solution.py:64
  429.2 37.9 %collective-permute-start.49 = (bf16[256,2048]{1,0:T(8,128)(2,1)}, bf16[256,2048]{1,0:T(8,128)(2,1)S(1)}, u32[]{:S(2)}, u32[]{:S(2)}) collective-permute-start(bf16[256,2048]{1,0:T(8,128)(2,1)} %tie.14), channel_id=1, source_target_pairs={{0,2},{1,3},{2,0},{3,1},{4,6},{5,7},{6,4},{7,5},{8,10},{9,11},{10,... | collective-permute-start | bytes 3145736 | tf_op jit(solution)/shard_map/ppermute | solution.py:64
  430.2 31.7 %collective-permute-start.50 = (bf16[16,2048]{1,0:T(8,128)(2,1)S(1)}, bf16[16,2048]{1,0:T(8,128)(2,1)S(1)}, u32[]{:S(2)}, u32[]{:S(2)}) collective-permute-start(bf16[16,2048]{1,0:T(8,128)(2,1)S(1)} %copy-done.94), channel_id=1, source_target_pairs={{0,1},{1,0},{2,3},{3,2},{4,5},{5,4},{6,7},{7,6},{8,9},{9,8},{10,11... | collective-permute-start | bytes 196616 | tf_op jit(solution)/shard_map/ppermute | solution.py:64
  430.5 32.0 %collective-permute-start.51 = (bf16[16,2048]{1,0:T(8,128)(2,1)S(1)}, bf16[16,2048]{1,0:T(8,128)(2,1)S(1)}, u32[]{:S(2)}, u32[]{:S(2)}) collective-permute-start(bf16[16,2048]{1,0:T(8,128)(2,1)S(1)} %copy-done.93), channel_id=1, source_target_pairs={{0,2},{1,3},{2,0},{3,1},{4,6},{5,7},{6,4},{7,5},{8,10},{9,11},{10,... | collective-permute-start | bytes 196616 | tf_op jit(solution)/shard_map/ppermute | solution.py:64
  431.5 32.4 %collective-permute-start.52 = (bf16[16,2048]{1,0:T(8,128)(2,1)S(1)}, bf16[16,2048]{1,0:T(8,128)(2,1)S(1)}, u32[]{:S(2)}, u32[]{:S(2)}) collective-permute-start(bf16[16,2048]{1,0:T(8,128)(2,1)S(1)} %copy-done.92), channel_id=1, source_target_pairs={{0,3},{1,2},{2,1},{3,0},{4,7},{5,6},{6,5},{7,4},{8,11},{9,10},{10,... | collective-permute-start | bytes 196616 | tf_op jit(solution)/shard_map/ppermute | solution.py:64
  (159 other events, 1480.5 us)
Sparse Core Ops, SparseCore 0:
  11.0 141.3 all-gather.2

commit v4 on v3

--- a/solution.py
+++ b/solution.py
@@ -205,24 +205,32 @@
         turned.append(spread(table_q[0, j], onehot[...], trig[...]).astype(BF16))
     odd = place[0] % 2
     rows_out = []
-    for block in range(tokens // QUERY_ROWS):
+
+    def score(block):
         start, stop = block * QUERY_ROWS, (block + 1) * QUERY_ROWS
+        return [matmul(keys[:stop], turned[j][:, start:stop]) for j in range(2)]
+
+    blocks = tokens // QUERY_ROWS
+    scores = score(0)
+    for block in range(blocks):
+        start, stop = block * QUERY_ROWS, (block + 1) * QUERY_ROWS
+        following = score(block + 1) if block + 1 < blocks else None
         done = []
         for j in range(2):
-            scores = matmul(keys[:stop], turned[j][:, start:stop])
-            last = jnp.where(ahead, scores[start:], -1e30)
+            last = jnp.where(ahead, scores[j][start:], -1e30)
             highest = jnp.max(last, axis=0, keepdims=True)
             if block:
-                highest = jnp.maximum(highest, jnp.max(scores[:start], axis=0, keepdims=True))
+                highest = jnp.maximum(highest, jnp.max(scores[j][:start], axis=0, keepdims=True))
             last = jnp.exp(last - highest)
             total = jnp.sum(last, axis=0, keepdims=True)
-            summed = matmul(values_t[:, start:stop], last.astype(BF16))
+            soft = last.astype(BF16)
             if block:
-                first = jnp.exp(scores[:start] - highest)
+                first = jnp.exp(scores[j][:start] - highest)
                 total = total + jnp.sum(first, axis=0, keepdims=True)
-                summed = summed + matmul(values_t[:, :start], first.astype(BF16))
-            done.append(summed / total)
+                soft = jnp.concatenate([first.astype(BF16), soft], axis=0)
+            done.append(matmul(values_t[:, :stop], soft) / total)
             log_total[0, j : j + 1, start:stop] = highest + jnp.log(total)
+        scores = following
         done = jnp.concatenate(done, axis=0)
         context_t[:, start:stop] = done.astype(BF16)
         rows_out.append(done.T.astype(BF16))
@@ -329,30 +337,69 @@
     grad_t = grad_context[...].astype(F32).T
     products = grad_t * context_t[...].astype(F32)
     grad_t = grad_t.astype(BF16)
+    heads = [slice(j * HEAD_DIM, (j + 1) * HEAD_DIM) for j in range(2)]
+    turned = [spread(table_q[0, j], onehot[...], trig[...]) for j in range(2)]
+    queries_t = [part.astype(BF16) for part in turned]
+    queries = [part.T.astype(BF16) for part in turned]
+    offset = [jnp.sum(products[head], axis=0, keepdims=True) for head in heads]
+    turned_back = [[], []]
+
+    def score(block, j):
+        start, stop = block * QUERY_ROWS, (block + 1) * QUERY_ROWS
+        return (
+            matmul(keys[:stop], queries_t[j][:, start:stop]),
+            matmul(values[:stop], grad_t[heads[j], start:stop]),
+        )
+
+    order = [(block, j) for block in range(tokens // QUERY_ROWS) for j in range(2)]
+    sums = [[None, None] for _ in range(tokens // QUERY_ROWS)]
+
+    def weigh(block, j, scores, grad_soft):
+        start, stop = block * QUERY_ROWS, (block + 1) * QUERY_ROWS
+        soft = jnp.exp(scores - log_total[0, j : j + 1, start:stop])
+        last = jnp.where(ahead, soft[start:], 0.0)
+        soft = jnp.concatenate([soft[:start], last], axis=0) if block else last
+        grad_scores = (soft * (grad_soft - offset[j][:, start:stop])).astype(BF16)
+        return soft.astype(BF16), grad_scores
+
+    def gather_up(block, j, soft, grad_scores):
+        start, stop = block * QUERY_ROWS, (block + 1) * QUERY_ROWS
+        for kind, part in enumerate(
+            (
+                matmul(soft, grad_context[start:stop, heads[j]]),
+                matmul(grad_scores, queries[j][start:stop]),
+            )
+        ):
+            for i in range(block + 1):
+                piece = part[i * QUERY_ROWS : (i + 1) * QUERY_ROWS]
+                held = sums[i][kind]
+                sums[i][kind] = piece if held is None else held + piece
+        grad_queries = matmul(keys_t[:, :stop], grad_scores) * HEAD_DIM ** (-0.5)
+        turned_back[j].append(
+            jnp.concatenate(
+                [grad_queries * cosine[:, start:stop], grad_queries * sine[:, start:stop]], axis=0
+            ).astype(BF16)
+        )
+
+    ready = score(*order[0])
+    waiting = None
+    for i, item in enumerate(order):
+        current = ready
+        ready = score(*order[i + 1]) if i + 1 < len(order) else None
+        if waiting is not None:
+            gather_up(*waiting)
+        waiting = (*item, *weigh(*item, *current))
+    gather_up(*waiting)
+    for i, (value_sum, key_sum) in enumerate(sums):
+        lines = slice(i * QUERY_ROWS, (i + 1) * QUERY_ROWS)
+        grad_values[lines] += value_sum
+        grad_keys[lines] += key_sum
+    both = jnp.concatenate([jnp.concatenate(parts, axis=1) for parts in turned_back], axis=0)
+    both = matmul(both, columns[...])
     per_head = []
     for j in range(2):
-        head = slice(j * HEAD_DIM, (j + 1) * HEAD_DIM)
-        turned = spread(table_q[0, j], onehot[...], trig[...])
-        queries_t = turned.astype(BF16)
-        queries = turned.T.astype(BF16)
-        offset = jnp.sum(products[head], axis=0, keepdims=True)
-        straight = jnp.zeros((HEAD_DIM, columns.shape[1]), F32)
-        crossed = jnp.zeros((HEAD_DIM, columns.shape[1]), F32)
-        for block in range(tokens // QUERY_ROWS):
-            start, stop = block * QUERY_ROWS, (block + 1) * QUERY_ROWS
-            scores = matmul(keys[:stop], queries_t[:, start:stop])
-            soft = jnp.exp(scores - log_total[0, j : j + 1, start:stop])
-            last = jnp.where(ahead, soft[start:], 0.0)
-            soft = jnp.concatenate([soft[:start], last], axis=0) if block else last
-            grad_soft = matmul(values[:stop], grad_t[head, start:stop])
-            grad_scores = (soft * (grad_soft - offset[:, start:stop])).astype(BF16)
-            grad_values[:stop] += matmul(soft.astype(BF16), grad_context[start:stop, head])
-            grad_keys[:stop] += matmul(grad_scores, queries[start:stop])
-            grad_queries = matmul(keys_t[:, :stop], grad_scores) * HEAD_DIM ** (-0.5)
-            parts = to_entries(
-                grad_queries, cosine[:, start:stop], sine[:, start:stop], columns[start:stop]
-            )
-            straight, crossed = straight + parts[0], crossed + parts[1]
+        at = 2 * HEAD_DIM * j
+        straight, crossed = both[at : at + HEAD_DIM], both[at + HEAD_DIM : at + 2 * HEAD_DIM]
         per_head.append(straight - turn_rows(crossed))
     total[...] += matmul_right_t(two_stacked(jnp.concatenate(per_head, axis=0)), w_query[...])
 
@@ -559,39 +606,38 @@
         [w_both.at[:, pl.ds(to, size)] for to, _, _, size in cuts if size] + [w_down],
         sems,
     )
-    for first, (rows, cots, out, grad) in enumerate(
-        ((x_other, other_in, out_other, None), (x_mine, mine_in, out_mine, grad_mine))
-    ):
-        if first == 0:
-            copies[0].wait()
-        gate = matmul(rows[...], w_both[:, :main])
-        if first == 0:
-            for copy in copies[1:-1]:
-                copy.wait()
-        others = matmul(rows[...], w_both[:, main:])
-        gate = jnp.concatenate([gate, others[:, main : main + rest]], axis=1)
-        upward = jnp.concatenate([others[:, :main], others[:, main + rest :]], axis=1)
-        if first == 0:
-            copies[-1].wait()
-        if ready:
-            grad_active = cots[...].astype(F32)
-        else:
-            grad_active = matmul_right_t(cots[...], w_down[...])
+    halves = ((x_other, other_in), (x_mine, mine_in))
+    copies[0].wait()
+    gates = [matmul(rows[...], w_both[:, :main]) for rows, _ in halves]
+    for copy in copies[1:-1]:
+        copy.wait()
+    others = [matmul(rows[...], w_both[:, main:]) for rows, _ in halves]
+    copies[-1].wait()
+    if ready:
+        grads_active = [cots[...].astype(F32) for _, cots in halves]
+    else:
+        grads_active = [matmul_right_t(cots[...], w_down[...]) for _, cots in halves]
+    middle = []
+    for gate, other, grad_active in zip(gates, others, grads_active):
+        gate = jnp.concatenate([gate, other[:, main : main + rest]], axis=1)
+        upward = jnp.concatenate([other[:, :main], other[:, main + rest :]], axis=1)
         sigmoid = 1.0 / (1.0 + jnp.exp(-gate))
         silu = gate * sigmoid
         activated = (silu * upward).astype(BF16)
         grad_gate = grad_active * upward * (sigmoid * (1.0 + gate * (1.0 - sigmoid)))
         grad_gate = grad_gate.astype(BF16)
         grad_up = (grad_active * silu).astype(BF16)
-        out[...] = matmul(activated, w_down[...]).astype(BF16)
         parts = [grad_gate[:, :main], grad_up[:, :main], grad_gate[:, main:], grad_up[:, main:]]
-        total = matmul_right_t(jnp.concatenate(parts, axis=1), w_both[...]).astype(BF16)
+        middle.append((activated, jnp.concatenate(parts, axis=1)))
+    for (activated, grads), out, grad in zip(middle, (out_other, out_mine), (None, grad_mine)):
+        total = matmul_right_t(grads, w_both[...]).astype(BF16)
         if grad is None:
             half = grad_a.shape[0]
             grad_a[...] = total[:half]
             grad_b[...] = total[half:]
         else:
             grad[...] = total
+        out[...] = matmul(activated, w_down[...]).astype(BF16)
 
 
 def mlp(mine, other, mine_in, other_in, w_gate, w_up, w_down, after):
@@ -686,9 +732,6 @@
     return ref[...].reshape(blocks * rows, width)
 
 
-ENTRY_ROWS = 256
-
-
 def entry_bias(valid, slots):
     shape = (valid.shape[1], valid.shape[1])
     same = lax.broadcasted_iota(jnp.int32, shape, 0) // slots == lax.broadcasted_iota(
@@ -697,8 +740,11 @@
     return jnp.where(jnp.logical_and(same, valid > 0.5), 0.0, -1e30)
 
 
-def entry_soft(queries, keys, bias):
-    scores = matmul_right_t(queries, keys) * HEAD_DIM ** (-0.5) + bias
+def entry_scores(queries, keys, bias):
+    return matmul_right_t(queries, keys) * HEAD_DIM ** (-0.5) + bias
+
+
+def entry_soft(scores):
     expon = jnp.exp(scores - jnp.max(scores, axis=1, keepdims=True))
     return expon / jnp.sum(expon, axis=1, keepdims=True)
 
@@ -762,13 +808,12 @@
     mixed[0, :, :width] = queries
     mixed[0, :, width : 2 * width] = keys
     mixed[0, :, 2 * width :] = values
-    for first in range(0, rows, ENTRY_ROWS):
-        lines = slice(first, first + ENTRY_ROWS)
-        bias = entry_bias(valid[:, lines], slots)
-        for head in range(width // HEAD_DIM):
-            at = slice(head * HEAD_DIM, (head + 1) * HEAD_DIM)
-            soft = entry_soft(queries[lines, at], keys[lines, at], bias)
-            joined[lines, at] = matmul(soft.astype(BF16), values[lines, at])
+    bias = entry_bias(valid[...], slots)
+    heads = [slice(i, i + HEAD_DIM) for i in range(0, width, HEAD_DIM)]
+    scores = [entry_scores(queries[:, at], keys[:, at], bias) for at in heads]
+    soft = [entry_soft(part).astype(BF16) for part in scores]
+    parts = [matmul(part, values[:, at]) for part, at in zip(soft, heads)]
+    joined[...] = jnp.concatenate(parts, axis=1)
     context_low = joined[...].astype(BF16)
     context[0] = context_low
     centre = hidden + matmul(context_low, square(w_o)) + vector(4)
@@ -973,23 +1018,29 @@
     low = grad_rows.astype(BF16)
     put(7, matmul_left_t(context[0], low))
     grad_context = matmul_right_t(low, square(w_o)).astype(BF16)
-    for first in range(0, rows, ENTRY_ROWS):
-        lines = slice(first, first + ENTRY_ROWS)
-        bias = entry_bias(valid[:, lines], slots)
-        for head in range(width // HEAD_DIM):
-            at, key_at, value_at = (
-                slice(i * width + head * HEAD_DIM, i * width + (head + 1) * HEAD_DIM)
-                for i in range(3)
-            )
-            queries, keys, values = (mixed[0, lines, part] for part in (at, key_at, value_at))
-            soft = entry_soft(queries, keys, bias)
-            grad_head = grad_context[lines, at]
-            grad_soft = matmul_right_t(grad_head, values)
-            offset = jnp.sum(soft * grad_soft, axis=1, keepdims=True)
-            grad_scores = (soft * (grad_soft - offset) * HEAD_DIM ** (-0.5)).astype(BF16)
-            grad_mixed[lines, at] = matmul(grad_scores, keys)
-            grad_mixed[lines, key_at] = matmul_left_t(grad_scores, queries)
-            grad_mixed[lines, value_at] = matmul_left_t(soft.astype(BF16), grad_head)
+    bias = entry_bias(valid[...], slots)
+    heads = [slice(i, i + HEAD_DIM) for i in range(0, width, HEAD_DIM)]
+    queries, keys, values = (
+        [mixed[0, :, i * width + at.start : i * width + at.stop] for at in heads] for i in range(3)
+    )
+    grads = [grad_context[:, at] for at in heads]
+    scores = [entry_scores(q, k, bias) for q, k in zip(queries, keys)]
+    grad_soft = [matmul_right_t(g, v) for g, v in zip(grads, values)]
+    soft = [entry_soft(part) for part in scores]
+    grad_scores = []
+    for part, grad in zip(soft, grad_soft):
+        offset = jnp.sum(part * grad, axis=1, keepdims=True)
+        grad_scores.append((part * (grad - offset) * HEAD_DIM ** (-0.5)).astype(BF16))
+    soft = [part.astype(BF16) for part in soft]
+    grad_mixed[:, :width] = jnp.concatenate(
+        [matmul(g, k) for g, k in zip(grad_scores, keys)], axis=1
+    )
+    grad_mixed[:, width : 2 * width] = jnp.concatenate(
+        [matmul_left_t(g, q) for g, q in zip(grad_scores, queries)], axis=1
+    )
+    grad_mixed[:, 2 * width :] = jnp.concatenate(
+        [matmul_left_t(p, g) for p, g in zip(soft, grads)], axis=1
+    )
     normed_one, inverse_one = norm_parts(below[0])
     normed_in = (normed_one * vector(0) + vector(1)).astype(BF16)
     grad_in = jnp.zeros(grad_rows.shape, F32)

time: 662 us -> 653 us (0.986)
  Pallas kernels: 354 us -> 329 us
  waiting for transfers between devices: 132 us -> 149 us
    ppermute x75, waiting for transfers between devices: 82.9 us -> 100 us  [swap(): return lax.ppermute(values, axis, [(i, i ^ bit) for i in range(size)])]
    pallas_call x2, Pallas kernels: 51.6 us -> 41.3 us  [attend_back(): pl.pallas_call(attend_back_kernel, grid=(pairs,), in_specs=[pl.BlockSpec(...]
    pallas_call x2, Pallas kernels: 41.6 us -> 33.8 us  [attend(): pl.pallas_call(attend_kernel, grid=(pairs,), in_specs=[pl.BlockSpec(memor...]
  transfers between devices with their start and end apart: 85 -> 85, of which waited for: 28 -> 30; matrix products, arithmetic and copies ran while one was open for 11% -> 11% of each run, Pallas kernels for 46% -> 43%
where the time goes in v4:
time: 653 us; the launch traced here: 644 us
  Pallas kernels  329 us (50%)
  waiting for transfers between devices  149 us (23%)
  local copies, waits for them, and re-layouts  55.7 us (9%)
  starting transfers between devices  52.9 us (8%)
  other arithmetic  21.1 us (3%)
  matrix products  20.9 us (3%)
  between operations  15.9 us (2%)
    ppermute x75, waiting for transfers between devices, swap(): return lax.ppermute(values, axis, [(i, i ^ bit) for i in range(size)])  100 us
    pallas_call x4, Pallas kernels, mlp(): pl.pallas_call(lambda *refs: mlp_kernel(ready, *refs), in_specs=[vmem] *...  94.1 us
    ppermute x75, starting transfers between devices, swap(): return lax.ppermute(values, axis, [(i, i ^ bit) for i in range(size)])  50.5 us
    ppermute x9, waiting for transfers between devices, next_on_line(): lax.ppermute(values, 'dp', [(i, (i + 2) % size) for i in range(size)])  42.5 us
    pallas_call x2, Pallas kernels, attend_back(): pl.pallas_call(attend_back_kernel, grid=(pairs,), in_specs=[pl.BlockSpec(...  41.3 us
    pallas_call x2, Pallas kernels, attend(): pl.pallas_call(attend_kernel, grid=(pairs,), in_specs=[pl.BlockSpec(memor...  33.8 us
    pallas_call x2, Pallas kernels, hyper_backward(): pl.pallas_call(lambda *refs: hyper_back_kernel(slots, layer, layers, last...  30.7 us
    unnamed x199, local copies, waits for them, and re-layouts  29.2 us
  transfers between devices with their start and end apart: 85, of which 30 were waited for; matrix products, arithmetic and copies ran while one was open for 11% of the time, Pallas kernels for 43%

profile of v4, /device:TPU:0, one launch (start us, length us, event | category | flops | bytes accessed | tf_op | source)
XLA Modules:
  0.0 644.2 jit_solution(863287826011026761)
XLA Ops:
  37.5 6.8 %lookup.2 = bf16[4096,128]{1,0:T(8,128)(2,1)} custom-call(s32[4096,1]{1,0:T(8,128)S(1)} %copy-done.8, bf16[4096,128]{1,0:T(8,128)(2,1)S(1)} %copy-done.11, s32[2,4096]{1,0:T(2,128)S(1)} %reshape.292._after), custom_call_target="tpu_custom_call" | custom-call | flops 8589934592 | bytes 2097152 | tf_op jit(solution)/shard_map/lookup/pallas_call | solution.py:84
  64.8 18.1 %collective-permute-done.6 = bf16[4,4,256,128]{3,2,1,0:T(8,128)(2,1)} collective-permute-done((bf16[4,4,256,128]{3,2,1,0:T(8,128)(2,1)}, bf16[4,4,256,128]{3,2,1,0:T(8,128)(2,1)}, u32[]{:S(2)}, u32[]{:S(2)}) %collective-permute-start.6) | collective-permute-done | bytes 1048608 | tf_op jit(solution)/shard_map/ppermute | solution.py:64
  116.7 22.9 %collective-permute-done.8 = bf16[1,4,256,128]{3,2,1,0:T(8,128)(2,1)S(1)} collective-permute-done((bf16[1,4,256,128]{3,2,1,0:T(8,128)(2,1)S(1)}, bf16[1,4,256,128]{3,2,1,0:T(8,128)(2,1)S(1)}, u32[]{:S(2)}, u32[]{:S(2)}) %collective-permute-start.8) | collective-permute-done | bytes 262176 | tf_op jit(solution)/shard_map/ppermute | solution.py:64
  152.4 15.3 %hyper.1 = (f32[18,512]{1,0:T(8,128)}, f32[2,2048]{1,0:T(2,128)}, f32[2,256,512]{2,1,0:T(8,128)}, bf16[2,256,1536]{2,1,0:T(8,128)(2,1)}, bf16[2,256,512]{2,1,0:T...) custom-call(s32[1]{0:T(128)} %bitcast.refs_0_.place, ...), custom_call_target="tpu_custom_call" | custom-call | flops 8000000000 | bytes 25000000 | tf_op jit(solution)/shard_map/hyper/pallas_call | solution.py:876
  179.4 12.6 %attend.2 = (bf16[2,256,512]{2,1,0:T(8,128)(2,1)}, bf16[2,256,512]{2,1,0:T(8,128)(2,1)}, bf16[512,1024]{1,0:T(8,128)(2,1)}, f32[4,2,1024]{2,1,0:T(2,128)}, bf16[...) custom-call(s32[1]{0:T(128)} %bitcast.refs_0_.place, ...), custom_call_target="tpu_custom_call" | custom-call | flops 12000000000 | bytes 8000000 | tf_op jit(solution)/shard_map/attend/pallas_call | solution.py:252
  192.8 10.0 %collective-permute-done.20._after_two.refs_2_ = bf16[256,2048]{1,0:T(8,128)(2,1)S(1)} collective-permute-done((bf16[256,2048]{1,0:T(8,128)(2,1)}, bf16[256,2048]{1,0:T(8,128)(2,1)S(1)}, u32[]{:S(2)}, u32[]{:S(2)}) %collective-permute-start.20) | collective-permute-done | bytes 1048608 | tf_op jit(solution)/shard_map/ppermute | solution.py:64
  204.3 21.2 %attend.3 = (bf16[2,256,512]{2,1,0:T(8,128)(2,1)}, bf16[2,256,512]{2,1,0:T(8,128)(2,1)}, bf16[512,1024]{1,0:T(8,128)(2,1)}, f32[4,2,1024]{2,1,0:T(2,128)}, bf16[...) custom-call(s32[1]{0:T(128)} %bitcast.refs_0_.place, ...), custom_call_target="tpu_custom_call" | custom-call | flops 12000000000 | bytes 8000000 | tf_op jit(solution)/shard_map/attend/pallas_call | solution.py:252
  227.4 11.7 %hidden.2 = (bf16[256,2048]{1,0:T(8,128)(2,1)}, bf16[256,2048]{1,0:T(8,128)(2,1)}, f32[256,2048]{1,0:T(8,128)}) custom-call(bf16[64,2048]{1,0:T(8,128)(2,1)} %get-tuple-element.134.embeds, s32[1,256]{1,0:T(1,128)} %copy-done.66, s32[1,256]{1,0:T(1,128)} %copy-done.68, bf16[1,2048]{1,0:T(2,128)(2,1)} %broadcast_in_dim.58.gain, ...), custom_call_target="tpu_custom_call" | custom-call | flops 6000000000 | bytes 18000000 | tf_op jit(solution)/shard_map/hidden/pallas_call | solution.py:523
  243.0 21.7 %mlp.4 = (bf16[256,2048]{1,0:T(8,128)(2,1)}, bf16[256,2048]{1,0:T(8,128)(2,1)}, bf16[256,2048]{1,0:T(8,128)(2,1)}, bf16[128,2048]{1,0:T(8,128)(2,1)}, bf16[128,2048]{1,0:T(8,128)(2,1)}) custom-call(bf16[256,2048]{1,0:T(8,128)(2,1)} %get-tuple-element.139.refs_0_, bf16[256,2048]{1,0:T(8,128)(2,1)} %copy-done.78, ...), custom_call_target="tpu_custom_call" | custom-call | flops 17716740096 | bytes 26000000 | tf_op jit(solution)/shard_map/mlp/pallas_call | solution.py:649
  267.8 25.2 %mlp.5 = (bf16[256,2048]{1,0:T(8,128)(2,1)}, bf16[256,2048]{1,0:T(8,128)(2,1)}, bf16[256,2048]{1,0:T(8,128)(2,1)}, bf16[128,2048]{1,0:T(8,128)(2,1)}, bf16[128,2048]{1,0:T(8,128)(2,1)}) custom-call(bf16[256,2048]{1,0:T(8,128)(2,1)} %get-tuple-element.142.refs_0_, bf16[256,2048]{1,0:T(8,128)(2,1)} %copy-done.74, bf16[256,2048]{1,0:T(8,128)(2,1)} %copy-done.71, ...), custom_call_target="tpu_custom_call" | custom-call | flops 17716740096 | bytes 26000000 | tf_op jit(solution)/shard_map/mlp/pallas_call | solution.py:649
  299.6 11.9 %hidden.3 = (bf16[256,2048]{1,0:T(8,128)(2,1)}, bf16[256,2048]{1,0:T(8,128)(2,1)}, f32[256,2048]{1,0:T(8,128)}) custom-call(bf16[64,2048]{1,0:T(8,128)(2,1)} %get-tuple-element.147.embeds, s32[1,256]{1,0:T(1,128)} %copy-done.65, s32[1,256]{1,0:T(1,128)} %copy-done.67, bf16[1,2048]{1,0:T(2,128)(2,1)} %broadcast_in_dim.58.gain, ...), custom_call_target="tpu_custom_call" | custom-call | flops 6000000000 | bytes 18000000 | tf_op jit(solution)/shard_map/hidden/pallas_call | solution.py:523
  319.2 25.1 %mlp.6 = (bf16[256,2048]{1,0:T(8,128)(2,1)}, bf16[256,2048]{1,0:T(8,128)(2,1)}, bf16[256,2048]{1,0:T(8,128)(2,1)}, bf16[128,2048]{1,0:T(8,128)(2,1)}, bf16[128,2048]{1,0:T(8,128)(2,1)}) custom-call(bf16[256,2048]{1,0:T(8,128)(2,1)} %get-tuple-element.155.refs_0_, bf16[256,2048]{1,0:T(8,128)(2,1)} %copy-done.76, bf16[256,2048]{1,0:T(8,128)(2,1)} %copy-done.73, ...), custom_call_target="tpu_custom_call" | custom-call | flops 17716740096 | bytes 26000000 | tf_op jit(solution)/shard_map/mlp/pallas_call | solution.py:649
  346.8 8.5 %hidden_back.2 = (bf16[256,2048]{1,0:T(8,128)(2,1)}, bf16[256,512]{1,0:T(8,128)(2,1)}, bf16[256,512]{1,0:T(8,128)(2,1)}, bf16[256,512]{1,0:T(8,128)(2,1)}, bf16[256,512]{1,0:T(8,128)(2,1)}) custom-call(f32[2,256,2048]{2,1,0:T(8,128)} %cotangent.3, f32[256,2048]{1,0:T(8,128)} %get-tuple-element.138.refs_7_.refs_8_.refs_9_.hidden.refs_0_, ...), custom_call_target="tpu_custom_call" | custom-call | flops 2000000000 | bytes 16000000 | tf_op jit(solution)/shard_map/hidden_back/pallas_call | solution.py:565
  359.5 22.1 %mlp.7 = (bf16[256,2048]{1,0:T(8,128)(2,1)}, bf16[256,2048]{1,0:T(8,128)(2,1)}, bf16[256,2048]{1,0:T(8,128)(2,1)}, bf16[128,2048]{1,0:T(8,128)(2,1)}, bf16[128,2048]{1,0:T(8,128)(2,1)}) custom-call(bf16[256,2048]{1,0:T(8,128)(2,1)} %get-tuple-element.151.refs_0_, bf16[256,2048]{1,0:T(8,128)(2,1)} %collective-permute-done.32.refs_1_, ...), custom_call_target="tpu_custom_call" | custom-call | flops 17716740096 | bytes 26000000 | tf_op jit(solution)/shard_map/mlp/pallas_call | solution.py:649
  389.0 8.7 %hidden_back.3 = (bf16[256,2048]{1,0:T(8,128)(2,1)}, bf16[256,512]{1,0:T(8,128)(2,1)}, bf16[256,512]{1,0:T(8,128)(2,1)}, bf16[256,512]{1,0:T(8,128)(2,1)}, bf16[256,512]{1,0:T(8,128)(2,1)}) custom-call(f32[2,256,2048]{2,1,0:T(8,128)} %cotangent.3, f32[256,2048]{1,0:T(8,128)} %get-tuple-element.156.refs_7_.refs_8_.refs_9_.hidden.refs_4_, ...), custom_call_target="tpu_custom_call" | custom-call | flops 2000000000 | bytes 16000000 | tf_op jit(solution)/shard_map/hidden_back/pallas_call | solution.py:565
  400.1 20.5 %attend_back.2 = (bf16[16,2048]{1,0:T(8,128)(2,1)}, bf16[16,2048]{1,0:T(8,128)(2,1)}, bf16[16,2048]{1,0:T(8,128)(2,1)}, bf16[16,2048]{1,0:T(8,128)(2,1)}) custom-call(s32[1]{0:T(128)} %bitcast.refs_0_.place, bf16[256,512]{1,0:T(8,128)(2,1)} %get-tuple-element.165.part0, bf16[256,512]{1,0:T(8,128)(2,1)} %copy-done.86, bf16[256,512]{1,0:T(8,128)(2,1)} %copy-done.87, ...), custom_call_target="tpu_custom_call" | custom-call | flops 24999999488 | bytes 8000000 | tf_op jit(solution)/shard_map/attend_back/pallas_call | solution.py:434
  431.8 20.7 %attend_back.3 = (bf16[16,2048]{1,0:T(8,128)(2,1)}, bf16[16,2048]{1,0:T(8,128)(2,1)}, bf16[16,2048]{1,0:T(8,128)(2,1)}, bf16[16,2048]{1,0:T(8,128)(2,1)}) custom-call(s32[1]{0:T(128)} %bitcast.refs_0_.place, bf16[256,512]{1,0:T(8,128)(2,1)} %get-tuple-element.180.part0, bf16[256,512]{1,0:T(8,128)(2,1)} %collective-permute-done.53.part1, ...), custom_call_target="tpu_custom_call" | custom-call | flops 24999999488 | bytes 8000000 | tf_op jit(solution)/shard_map/attend_back/pallas_call | solution.py:434
  461.6 16.4 %hyper_back.2 = (bf16[2,2,4,128,512]{4,3,2,1,0:T(8,128)(2,1)}, bf16[2,2,4,128,512]{4,3,2,1,0:T(8,128)(2,1)}, bf16[2,2,4,128,512]{4,3,2,1,0:T(8,128)(2,1)}, bf16[...) custom-call(s32[4]{0:T(128)} %pad_add_fusion.5.refs_0_, ...), custom_call_target="tpu_custom_call" | custom-call | flops 8000000000 | bytes 25000000 | tf_op jit(solution)/shard_map/hyper_back/pallas_call | solution.py:1123
  494.6 14.3 %hyper_back.3 = (bf16[2,2,4,112,512]{4,3,2,1,0:T(8,128)(2,1)}, bf16[2,2,4,112,512]{4,3,2,1,0:T(8,128)(2,1)}, bf16[2,2,4,112,512]{4,3,2,1,0:T(8,128)(2,1)}, bf16[...) custom-call(s32[4]{0:T(128)} %pad_add_fusion.5.refs_0_, ...), custom_call_target="tpu_custom_call" | custom-call | flops 8000000000 | bytes 25000000 | tf_op jit(solution)/shard_map/hyper_back/pallas_call | solution.py:1123
  559.6 15.2 %collective-permute-done.75 = bf16[256,512]{1,0:T(8,128)(2,1)S(1)} collective-permute-done((bf16[256,512]{1,0:T(8,128)(2,1)}, bf16[256,512]{1,0:T(8,128)(2,1)S(1)}, u32[]{:S(2)}, u32[]{:S(2)}) %collective-permute-start.75) | collective-permute-done | bytes 262176 | tf_op jit(solution)/shard_map/ppermute | solution.py:1384
  582.0 7.6 %collect.2.base_ref._after_one = f32[4096,128]{1,0:T(8,128)S(1)} custom-call(s32[2,2048]{1,0:T(2,128)S(1)} %slice.98.refs_0_, s32[2048,1]{1,0:T(8,128)S(1)} %copy-done.6, s32[2048,1]{1,0:T(8,128)S(1)} %copy-done.7, bf16[2048,128]{1,0:T(8,128)(2,1)S(1)} %bitcast.121, bf16[2048,128]{1,0:T(8,128)(2,1)} %bitcast.46.refs_4_), custom_call_target="tpu_custom_call" | custom-call | flops 8589934592 | bytes 2097152 | tf_op jit(solution)/shard_map/collect/pallas_call | solution.py:131
  596.1 9.1 %collective-permute-done.81 = bf16[224,512]{1,0:T(8,128)(2,1)S(1)} collective-permute-done((bf16[224,512]{1,0:T(8,128)(2,1)}, bf16[224,512]{1,0:T(8,128)(2,1)S(1)}, u32[]{:S(2)}, u32[]{:S(2)}) %collective-permute-start.81) | collective-permute-done | bytes 229408 | tf_op jit(solution)/shard_map/ppermute | solution.py:1384
  607.4 13.8 %collective-permute-done.82 = bf16[224,512]{1,0:T(8,128)(2,1)} collective-permute-done((bf16[224,512]{1,0:T(8,128)(2,1)S(1)}, bf16[224,512]{1,0:T(8,128)(2,1)}, u32[]{:S(2)}, u32[]{:S(2)}) %collective-permute-start.82) | collective-permute-done | bytes 229408 | tf_op jit(solution)/shard_map/ppermute | solution.py:1384
  624.1 9.0 %collect.3 = f32[4096,128]{1,0:T(8,128)} custom-call(s32[2,2048]{1,0:T(2,128)S(1)} %slice.91.ids_ref, s32[2048,1]{1,0:T(8,128)S(1)} %copy-done.4, s32[2048,1]{1,0:T(8,128)S(1)} %copy-done.5, bf16[2048,128]{1,0:T(8,128)(2,1)S(1)} %bitcast.122, bf16[2048,128]{1,0:T(8,128)(2,1)} %bitcast.44.right_ref, f32[4096,128]{1,0:T(8,128)S(1)} %copy-done.10), custom_call_target="tpu_custom_call" | custom-call | flops 8589934592 | bytes 2097152 | tf_op jit(solution)/shard_map/collect/pallas_call | solution.py:131
  (479 shorter events, 259.6 us)
Async XLA Ops:
  7.3 145.1 %all-gather.3.cloned.1.call-start = ((), (), s32[]{:S(2)}) async-start(), calls=%async_computation | async-start | bytes 16220160 | tf_op jit(solution)/shard_map/all_gather | solution.py:1482
  9.4 136.8 %collective-permute-start = (bf16[512,2048]{1,0:T(8,128)(2,1)}, bf16[512,2048]{1,0:T(8,128)(2,1)}, u32[]{:S(2)}, u32[]{:S(2)}) collective-permute-start(bf16[512,2048]{1,0:T(8,128)(2,1)} %w0.7), channel_id=1, source_target_pairs={{0,2},{1,3},{2,0},{3,1},{4,6},{5,7},{6,4},{7,5},{8,10},{9,11},{10,... | collective-permute-start | bytes 6291464 | tf_op jit(solution)/shard_map/ppermute | solution.py:64
  12.4 213.1 %collective-permute-start.18 = (bf16[512,2048]{1,0:T(8,128)(2,1)}, bf16[512,2048]{1,0:T(8,128)(2,1)}, u32[]{:S(2)}, u32[]{:S(2)}) collective-permute-start(bf16[512,2048]{1,0:T(8,128)(2,1)} %w0.7), channel_id=1, source_target_pairs={{0,1},{1,0},{2,3},{3,2},{4,5},{5,4},{6,7},{7,6},{8,9},{9,8},{10,11... | collective-permute-start | bytes 6291464 | tf_op jit(solution)/shard_map/ppermute | solution.py:64
  44.3 38.6 %collective-permute-start.6 = (bf16[4,4,256,128]{3,2,1,0:T(8,128)(2,1)}, bf16[4,4,256,128]{3,2,1,0:T(8,128)(2,1)}, u32[]{:S(2)}, u32[]{:S(2)}) collective-permute-start(bf16[4,4,256,128]{3,2,1,0:T(8,128)(2,1)} %bitcast.3._after), channel_id=1, source_target_pairs={{0,4},{4,0},{8,12},{12,8},{16,20},{20,16},{24,28},{28,24},{1,5},{5... | collective-permute-start | bytes 3145736 | tf_op jit(solution)/shard_map/ppermute | solution.py:64
  59.1 51.7 %collective-permute-start.4 = (bf16[256,2048]{1,0:T(8,128)(2,1)}, bf16[256,2048]{1,0:T(8,128)(2,1)}, u32[]{:S(2)}, u32[]{:S(2)}) collective-permute-start(bf16[256,2048]{1,0:T(8,128)(2,1)} %cast_after.2._values), channel_id=1, source_target_pairs={{0,1},{1,0},{2,3},{3,2},{4,5},{5,4},{6,7},{7,6},{8,9},{9,8},{10,11... | collective-permute-start | bytes 3145736 | tf_op jit(solution)/shard_map/ppermute | solution.py:64
  92.2 48.2 %collective-permute-start.5 = (bf16[256,2048]{1,0:T(8,128)(2,1)S(1)}, bf16[256,2048]{1,0:T(8,128)(2,1)}, u32[]{:S(2)}, u32[]{:S(2)}) collective-permute-start(bf16[256,2048]{1,0:T(8,128)(2,1)S(1)} %copy-done.19), channel_id=1, source_target_pairs={{0,1},{1,0},{2,3},{3,2},{4,5},{5,4},{6,7},{7,6},{8,9},{9,8},{10,11... | collective-permute-start | bytes 3145736 | tf_op jit(solution)/shard_map/ppermute | solution.py:64
  110.7 28.9 %collective-permute-start.8 = (bf16[1,4,256,128]{3,2,1,0:T(8,128)(2,1)S(1)}, bf16[1,4,256,128]{3,2,1,0:T(8,128)(2,1)S(1)}, u32[]{:S(2)}, u32[]{:S(2)}) collective-permute-start(bf16[1,4,256,128]{3,2,1,0:T(8,128)(2,1)S(1)} %slice.114), channel_id=1, source_target_pairs={{0,16},{4,20},{8,24},{12,28},{16,0},{20,4},{24,8},{28,12},{1,17},{... | collective-permute-start | bytes 786440 | tf_op jit(solution)/shard_map/ppermute | solution.py:64
  170.8 54.8 %collective-permute-start.19 = (bf16[512,2048]{1,0:T(8,128)(2,1)}, bf16[512,2048]{1,0:T(8,128)(2,1)S(1)}, u32[]{:S(2)}, u32[]{:S(2)}) collective-permute-start(bf16[512,2048]{1,0:T(8,128)(2,1)} %collective-permute-done.refs_1_.w2), channel_id=1, source_target_pairs={{0,1},{1,0},{2,3},{3,2},{4,5},{5,4},{6,7},{7,6},{8,9},{9,8},{10,11... | collective-permute-start | bytes 6291464 | tf_op jit(solution)/shard_map/ppermute | solution.py:64
  192.1 33.5 %collective-permute-start.15 = (bf16[2,256,512]{2,1,0:T(8,128)(2,1)}, bf16[2,256,512]{2,1,0:T(8,128)(2,1)S(1)}, u32[]{:S(2)}, u32[]{:S(2)}) collective-permute-start(bf16[2,256,512]{2,1,0:T(8,128)(2,1)} %get-tuple-element.136), channel_id=1, source_target_pairs={{0,1},{1,0},{2,3},{3,2},{4,5},{5,4},{6,7},{7,6},{8,9},{9,8},{10,11... | collective-permute-start | bytes 1572872 | tf_op jit(solution)/shard_map/ppermute | solution.py:64
  192.4 33.2 %collective-permute-start.17 = (bf16[2,256,512]{2,1,0:T(8,128)(2,1)}, bf16[2,256,512]{2,1,0:T(8,128)(2,1)S(1)}, u32[]{:S(2)}, u32[]{:S(2)}) collective-permute-start(bf16[2,256,512]{2,1,0:T(8,128)(2,1)} %get-tuple-element.136), channel_id=1, source_target_pairs={{0,3},{1,2},{2,1},{3,0},{4,7},{5,6},{6,5},{7,4},{8,11},{9,10},{10,... | collective-permute-start | bytes 1572872 | tf_op jit(solution)/shard_map/ppermute | solution.py:64
  264.7 33.7 %collective-permute-start.31 = (bf16[256,2048]{1,0:T(8,128)(2,1)}, bf16[256,2048]{1,0:T(8,128)(2,1)S(1)}, u32[]{:S(2)}, u32[]{:S(2)}) collective-permute-start(bf16[256,2048]{1,0:T(8,128)(2,1)} %tie.12), channel_id=1, source_target_pairs={{0,2},{1,3},{2,0},{3,1},{4,6},{5,7},{6,4},{7,5},{8,10},{9,11},{10,... | collective-permute-start | bytes 3145736 | tf_op jit(solution)/shard_map/ppermute | solution.py:64
  312.2 32.4 %collective-permute-start.33 = (bf16[128,2048]{1,0:T(8,128)(2,1)S(1)}, bf16[128,2048]{1,0:T(8,128)(2,1)}, u32[]{:S(2)}, u32[]{:S(2)}) collective-permute-start(bf16[128,2048]{1,0:T(8,128)(2,1)S(1)} %copy-done.80), channel_id=1, source_target_pairs={{0,1},{1,0},{2,3},{3,2},{4,5},{5,4},{6,7},{7,6},{8,9},{9,8},{10,11... | collective-permute-start | bytes 1572872 | tf_op jit(solution)/shard_map/ppermute | solution.py:64
  312.3 32.6 %collective-permute-start.34 = (bf16[128,2048]{1,0:T(8,128)(2,1)S(1)}, bf16[128,2048]{1,0:T(8,128)(2,1)S(1)}, u32[]{:S(2)}, u32[]{:S(2)}) collective-permute-start(bf16[128,2048]{1,0:T(8,128)(2,1)S(1)} %copy-done.79), channel_id=1, source_target_pairs={{0,1},{1,0},{2,3},{3,2},{4,5},{5,4},{6,7},{7,6},{8,9},{9,8},{10,11... | collective-permute-start | bytes 1572872 | tf_op jit(solution)/shard_map/ppermute | solution.py:64
  312.7 33.2 %collective-permute-start.35 = (bf16[256,2048]{1,0:T(8,128)(2,1)S(1)}, bf16[256,2048]{1,0:T(8,128)(2,1)S(1)}, u32[]{:S(2)}, u32[]{:S(2)}) collective-permute-start(bf16[256,2048]{1,0:T(8,128)(2,1)S(1)} %copy-done.30), channel_id=1, source_target_pairs={{0,2},{1,3},{2,0},{3,1},{4,6},{5,7},{6,4},{7,5},{8,10},{9,11},{10,... | collective-permute-start | bytes 3145736 | tf_op jit(solution)/shard_map/ppermute | solution.py:64
  314.5 44.9 %collective-permute-start.32 = (bf16[256,2048]{1,0:T(8,128)(2,1)}, bf16[256,2048]{1,0:T(8,128)(2,1)}, u32[]{:S(2)}, u32[]{:S(2)}) collective-permute-start(bf16[256,2048]{1,0:T(8,128)(2,1)} %get-tuple-element.151.refs_0_), channel_id=1, source_target_pairs={{0,1},{1,0},{2,3},{3,2},{4,5},{5,4},{6,7},{7,6},{8,9},{9,8},{10,11... | collective-permute-start | bytes 3145736 | tf_op jit(solution)/shard_map/ppermute | solution.py:64
  345.7 52.1 %collective-permute-start.22 = (bf16[256,2048]{1,0:T(8,128)(2,1)}, bf16[256,2048]{1,0:T(8,128)(2,1)S(1)}, u32[]{:S(2)}, u32[]{:S(2)}) collective-permute-start(bf16[256,2048]{1,0:T(8,128)(2,1)} %get-tuple-element.141), channel_id=1, source_target_pairs={{0,1},{1,0},{2,3},{3,2},{4,5},{5,4},{6,7},{7,6},{8,9},{9,8},{10,11... | collective-permute-start | bytes 3145736 | tf_op jit(solution)/shard_map/ppermute | solution.py:64
  345.9 35.7 %collective-permute-start.27 = (bf16[256,2048]{1,0:T(8,128)(2,1)}, bf16[256,2048]{1,0:T(8,128)(2,1)S(1)}, u32[]{:S(2)}, u32[]{:S(2)}) collective-permute-start(bf16[256,2048]{1,0:T(8,128)(2,1)} %get-tuple-element.146), channel_id=1, source_target_pairs={{0,1},{1,0},{2,3},{3,2},{4,5},{5,4},{6,7},{7,6},{8,9},{9,8},{10,11... | collective-permute-start | bytes 3145736 | tf_op jit(solution)/shard_map/ppermute | solution.py:64
  358.4 29.6 %collective-permute-start.48 = (bf16[256,2048]{1,0:T(8,128)(2,1)}, bf16[256,2048]{1,0:T(8,128)(2,1)}, u32[]{:S(2)}, u32[]{:S(2)}) collective-permute-start(bf16[256,2048]{1,0:T(8,128)(2,1)} %add_convert_fusion.1.refs_8_), channel_id=1, source_target_pairs={{0,2},{1,3},{2,0},{3,1},{4,6},{5,7},{6,4},{7,5},{8,10},{9,11},{10,... | collective-permute-start | bytes 3145736 | tf_op jit(solution)/shard_map/ppermute | solution.py:64
  388.0 33.2 %collective-permute-start.40 = (bf16[256,2048]{1,0:T(8,128)(2,1)S(1)}, bf16[256,2048]{1,0:T(8,128)(2,1)S(1)}, u32[]{:S(2)}, u32[]{:S(2)}) collective-permute-start(bf16[256,2048]{1,0:T(8,128)(2,1)S(1)} %copy-done.15), channel_id=1, source_target_pairs={{0,2},{1,3},{2,0},{3,1},{4,6},{5,7},{6,4},{7,5},{8,10},{9,11},{10,... | collective-permute-start | bytes 3145736 | tf_op jit(solution)/shard_map/ppermute | solution.py:64
  399.4 31.7 %collective-permute-start.55 = (bf16[256,512]{1,0:T(8,128)(2,1)}, bf16[256,512]{1,0:T(8,128)(2,1)S(1)}, u32[]{:S(2)}, u32[]{:S(2)}) collective-permute-start(bf16[256,512]{1,0:T(8,128)(2,1)} %get-tuple-element.183), channel_id=1, source_target_pairs={{0,3},{1,2},{2,1},{3,0},{4,7},{5,6},{6,5},{7,4},{8,11},{9,10},{10,... | collective-permute-start | bytes 786440 | tf_op jit(solution)/shard_map/ppermute | solution.py:64
  421.3 39.2 %collective-permute-start.49 = (bf16[256,2048]{1,0:T(8,128)(2,1)}, bf16[256,2048]{1,0:T(8,128)(2,1)S(1)}, u32[]{:S(2)}, u32[]{:S(2)}) collective-permute-start(bf16[256,2048]{1,0:T(8,128)(2,1)} %tie.14), channel_id=1, source_target_pairs={{0,2},{1,3},{2,0},{3,1},{4,6},{5,7},{6,4},{7,5},{8,10},{9,11},{10,... | collective-permute-start | bytes 3145736 | tf_op jit(solution)/shard_map/ppermute | solution.py:64
  422.3 31.6 %collective-permute-start.50 = (bf16[16,2048]{1,0:T(8,128)(2,1)S(1)}, bf16[16,2048]{1,0:T(8,128)(2,1)S(1)}, u32[]{:S(2)}, u32[]{:S(2)}) collective-permute-start(bf16[16,2048]{1,0:T(8,128)(2,1)S(1)} %copy-done.94), channel_id=1, source_target_pairs={{0,1},{1,0},{2,3},{3,2},{4,5},{5,4},{6,7},{7,6},{8,9},{9,8},{10,11... | collective-permute-start | bytes 196616 | tf_op jit(solution)/shard_map/ppermute | solution.py:64
  422.3 34.1 %collective-permute-start.51 = (bf16[16,2048]{1,0:T(8,128)(2,1)S(1)}, bf16[16,2048]{1,0:T(8,128)(2,1)S(1)}, u32[]{:S(2)}, u32[]{:S(2)}) collective-permute-start(bf16[16,2048]{1,0:T(8,128)(2,1)S(1)} %copy-done.93), channel_id=1, source_target_pairs={{0,2},{1,3},{2,0},{3,1},{4,6},{5,7},{6,4},{7,5},{8,10},{9,11},{10,... | collective-permute-start | bytes 196616 | tf_op jit(solution)/shard_map/ppermute | solution.py:64
  427.0 30.0 %collective-permute-start.52 = (bf16[16,2048]{1,0:T(8,128)(2,1)S(1)}, bf16[16,2048]{1,0:T(8,128)(2,1)S(1)}, u32[]{:S(2)}, u32[]{:S(2)}) collective-permute-start(bf16[16,2048]{1,0:T(8,128)(2,1)S(1)} %copy-done.92), channel_id=1, source_target_pairs={{0,3},{1,2},{2,1},{3,0},{4,7},{5,6},{6,5},{7,4},{8,11},{9,10},{10,... | collective-permute-start | bytes 196616 | tf_op jit(solution)/shard_map/ppermute | solution.py:64
  (159 other events, 1483.8 us)
Sparse Core Ops, SparseCore 0:
  11.0 141.3 all-gather.2

commit v5 on v4

--- a/solution.py
+++ b/solution.py
@@ -1544,7 +1544,7 @@
         )
         kept_attn.append(kept)
         contexts.append([near, *exchange_relative(far, near, far)])
-        after = (near, cots_peer[0][0])
+        after = (near, near)
 
     def after_attention(micro, after):
         own, peer, rows = hidden_rows_of(
@@ -1573,7 +1573,7 @@
         total = (peer[0].astype(F32) + pair_swap(peer[1], 1).astype(F32)).astype(BF16)
         return pair_swap(tie(total, after), 2)
 
-    near_in, peer_in, rows_a = after_attention(0, (contexts[1][0], contexts[1][0]))
+    near_in, peer_in, rows_a = after_attention(0, (contexts[1][0], cots_peer[0][0]))
     near_a = feed_forward(near_in, grads_near[0], rows_a)
     cots_peer.append(peer_cot(1, near_a[2]))
     peer_a = feed_forward(peer_in, cots_peer[0], near_a[2], contexts[1][2], contexts[1][3])

time: 653 us -> 665 us (1.018)
  waiting for transfers between devices: 149 us -> 164 us
    ppermute x75, waiting for transfers between devices: 100 us -> 114 us  [swap(): return lax.ppermute(values, axis, [(i, i ^ bit) for i in range(size)])]
    unnamed x199 -> x195, local copies, waits for them, and re-layouts: 29.2 us -> 27.3 us
  transfers between devices with their start and end apart: 85 -> 85, of which waited for: 30 -> 34; matrix products, arithmetic and copies ran while one was open for 11% -> 11% of each run, Pallas kernels for 43% -> 42%
where the time goes in v5:
time: 665 us; the launch traced here: 657 us
  Pallas kernels  328 us (49%)
  waiting for transfers between devices  164 us (25%)
  local copies, waits for them, and re-layouts  53.8 us (8%)
  starting transfers between devices  52.5 us (8%)
  other arithmetic  21.1 us (3%)
  matrix products  20.9 us (3%)
  between operations  15.8 us (2%)
    ppermute x75, waiting for transfers between devices, swap(): return lax.ppermute(values, axis, [(i, i ^ bit) for i in range(size)])  114 us
    pallas_call x4, Pallas kernels, mlp(): pl.pallas_call(lambda *refs: mlp_kernel(ready, *refs), in_specs=[vmem] *...  94.1 us
    ppermute x75, starting transfers between devices, swap(): return lax.ppermute(values, axis, [(i, i ^ bit) for i in range(size)])  50.7 us
    ppermute x9, waiting for transfers between devices, next_on_line(): lax.ppermute(values, 'dp', [(i, (i + 2) % size) for i in range(size)])  43.5 us
    pallas_call x2, Pallas kernels, attend_back(): pl.pallas_call(attend_back_kernel, grid=(pairs,), in_specs=[pl.BlockSpec(...  41.3 us
    pallas_call x2, Pallas kernels, attend(): pl.pallas_call(attend_kernel, grid=(pairs,), in_specs=[pl.BlockSpec(memor...  33.8 us
    pallas_call x2, Pallas kernels, hyper_backward(): pl.pallas_call(lambda *refs: hyper_back_kernel(slots, layer, layers, last...  30.6 us
    unnamed x195, local copies, waits for them, and re-layouts  27.3 us
  transfers between devices with their start and end apart: 85, of which 34 were waited for; matrix products, arithmetic and copies ran while one was open for 11% of the time, Pallas kernels for 42%

profile of v5, /device:TPU:0, one launch (start us, length us, event | category | flops | bytes accessed | tf_op | source)
XLA Modules:
  0.0 656.6 jit_solution(14718023982545450535)
XLA Ops:
  37.5 6.8 %lookup.2 = bf16[4096,128]{1,0:T(8,128)(2,1)} custom-call(s32[4096,1]{1,0:T(8,128)S(1)} %copy-done.8, bf16[4096,128]{1,0:T(8,128)(2,1)S(1)} %copy-done.11, s32[2,4096]{1,0:T(2,128)S(1)} %reshape.292._after), custom_call_target="tpu_custom_call" | custom-call | flops 8589934592 | bytes 2097152 | tf_op jit(solution)/shard_map/lookup/pallas_call | solution.py:84
  64.8 18.1 %collective-permute-done.6 = bf16[4,4,256,128]{3,2,1,0:T(8,128)(2,1)} collective-permute-done((bf16[4,4,256,128]{3,2,1,0:T(8,128)(2,1)}, bf16[4,4,256,128]{3,2,1,0:T(8,128)(2,1)}, u32[]{:S(2)}, u32[]{:S(2)}) %collective-permute-start.6) | collective-permute-done | bytes 1048608 | tf_op jit(solution)/shard_map/ppermute | solution.py:64
  116.7 22.9 %collective-permute-done.8 = bf16[1,4,256,128]{3,2,1,0:T(8,128)(2,1)S(1)} collective-permute-done((bf16[1,4,256,128]{3,2,1,0:T(8,128)(2,1)S(1)}, bf16[1,4,256,128]{3,2,1,0:T(8,128)(2,1)S(1)}, u32[]{:S(2)}, u32[]{:S(2)}) %collective-permute-start.8) | collective-permute-done | bytes 262176 | tf_op jit(solution)/shard_map/ppermute | solution.py:64
  152.5 15.3 %hyper.1 = (f32[18,512]{1,0:T(8,128)}, f32[2,2048]{1,0:T(2,128)}, f32[2,256,512]{2,1,0:T(8,128)}, bf16[2,256,1536]{2,1,0:T(8,128)(2,1)}, bf16[2,256,512]{2,1,0:T...) custom-call(s32[1]{0:T(128)} %bitcast.refs_0_.place, ...), custom_call_target="tpu_custom_call" | custom-call | flops 8000000000 | bytes 25000000 | tf_op jit(solution)/shard_map/hyper/pallas_call | solution.py:876
  176.7 12.6 %attend.2 = (bf16[2,256,512]{2,1,0:T(8,128)(2,1)}, bf16[2,256,512]{2,1,0:T(8,128)(2,1)}, bf16[512,1024]{1,0:T(8,128)(2,1)}, f32[4,2,1024]{2,1,0:T(2,128)}, bf16[...) custom-call(s32[1]{0:T(128)} %bitcast.refs_0_.place, ...), custom_call_target="tpu_custom_call" | custom-call | flops 12000000000 | bytes 8000000 | tf_op jit(solution)/shard_map/attend/pallas_call | solution.py:252
  193.1 21.2 %attend.3 = (bf16[2,256,512]{2,1,0:T(8,128)(2,1)}, bf16[2,256,512]{2,1,0:T(8,128)(2,1)}, bf16[512,1024]{1,0:T(8,128)(2,1)}, f32[4,2,1024]{2,1,0:T(2,128)}, bf16[...) custom-call(s32[1]{0:T(128)} %bitcast.refs_0_.place, ...), custom_call_target="tpu_custom_call" | custom-call | flops 12000000000 | bytes 8000000 | tf_op jit(solution)/shard_map/attend/pallas_call | solution.py:252
  215.9 22.1 %collective-permute-done.20._after_two.refs_2_ = bf16[256,2048]{1,0:T(8,128)(2,1)S(1)} collective-permute-done((bf16[256,2048]{1,0:T(8,128)(2,1)}, bf16[256,2048]{1,0:T(8,128)(2,1)S(1)}, u32[]{:S(2)}, u32[]{:S(2)}) %collective-permute-start.20) | collective-permute-done | bytes 1048608 | tf_op jit(solution)/shard_map/ppermute | solution.py:64
  239.0 11.6 %hidden.2 = (bf16[256,2048]{1,0:T(8,128)(2,1)}, bf16[256,2048]{1,0:T(8,128)(2,1)}, f32[256,2048]{1,0:T(8,128)}) custom-call(bf16[64,2048]{1,0:T(8,128)(2,1)} %get-tuple-element.134.embeds, s32[1,256]{1,0:T(1,128)} %copy-done.66, s32[1,256]{1,0:T(1,128)} %copy-done.68, bf16[1,2048]{1,0:T(2,128)(2,1)} %broadcast_in_dim.58.gain, ...), custom_call_target="tpu_custom_call" | custom-call | flops 6000000000 | bytes 18000000 | tf_op jit(solution)/shard_map/hidden/pallas_call | solution.py:523
  254.6 21.7 %mlp.4 = (bf16[256,2048]{1,0:T(8,128)(2,1)}, bf16[256,2048]{1,0:T(8,128)(2,1)}, bf16[256,2048]{1,0:T(8,128)(2,1)}, bf16[128,2048]{1,0:T(8,128)(2,1)}, bf16[128,2048]{1,0:T(8,128)(2,1)}) custom-call(bf16[256,2048]{1,0:T(8,128)(2,1)} %get-tuple-element.139.refs_0_, bf16[256,2048]{1,0:T(8,128)(2,1)} %copy-done.77, ...), custom_call_target="tpu_custom_call" | custom-call | flops 17716740096 | bytes 26000000 | tf_op jit(solution)/shard_map/mlp/pallas_call | solution.py:649
  280.1 25.2 %mlp.5 = (bf16[256,2048]{1,0:T(8,128)(2,1)}, bf16[256,2048]{1,0:T(8,128)(2,1)}, bf16[256,2048]{1,0:T(8,128)(2,1)}, bf16[128,2048]{1,0:T(8,128)(2,1)}, bf16[128,2048]{1,0:T(8,128)(2,1)}) custom-call(bf16[256,2048]{1,0:T(8,128)(2,1)} %get-tuple-element.142.refs_0_, bf16[256,2048]{1,0:T(8,128)(2,1)} %copy-done.73, bf16[256,2048]{1,0:T(8,128)(2,1)} %copy-done.72, ...), custom_call_target="tpu_custom_call" | custom-call | flops 17716740096 | bytes 26000000 | tf_op jit(solution)/shard_map/mlp/pallas_call | solution.py:649
  312.0 11.9 %hidden.3 = (bf16[256,2048]{1,0:T(8,128)(2,1)}, bf16[256,2048]{1,0:T(8,128)(2,1)}, f32[256,2048]{1,0:T(8,128)}) custom-call(bf16[64,2048]{1,0:T(8,128)(2,1)} %get-tuple-element.147.embeds, s32[1,256]{1,0:T(1,128)} %copy-done.65, s32[1,256]{1,0:T(1,128)} %copy-done.67, bf16[1,2048]{1,0:T(2,128)(2,1)} %broadcast_in_dim.58.gain, ...), custom_call_target="tpu_custom_call" | custom-call | flops 6000000000 | bytes 18000000 | tf_op jit(solution)/shard_map/hidden/pallas_call | solution.py:523
  331.6 25.1 %mlp.6 = (bf16[256,2048]{1,0:T(8,128)(2,1)}, bf16[256,2048]{1,0:T(8,128)(2,1)}, bf16[256,2048]{1,0:T(8,128)(2,1)}, bf16[128,2048]{1,0:T(8,128)(2,1)}, bf16[128,2048]{1,0:T(8,128)(2,1)}) custom-call(bf16[256,2048]{1,0:T(8,128)(2,1)} %get-tuple-element.155.refs_0_, bf16[256,2048]{1,0:T(8,128)(2,1)} %copy-done.75, bf16[256,2048]{1,0:T(8,128)(2,1)} %copy-done.71, ...), custom_call_target="tpu_custom_call" | custom-call | flops 17716740096 | bytes 26000000 | tf_op jit(solution)/shard_map/mlp/pallas_call | solution.py:649
  359.2 8.5 %hidden_back.2 = (bf16[256,2048]{1,0:T(8,128)(2,1)}, bf16[256,512]{1,0:T(8,128)(2,1)}, bf16[256,512]{1,0:T(8,128)(2,1)}, bf16[256,512]{1,0:T(8,128)(2,1)}, bf16[256,512]{1,0:T(8,128)(2,1)}) custom-call(f32[2,256,2048]{2,1,0:T(8,128)} %cotangent.3, f32[256,2048]{1,0:T(8,128)} %get-tuple-element.138.refs_7_.refs_8_.refs_9_.hidden.refs_0_, ...), custom_call_target="tpu_custom_call" | custom-call | flops 2000000000 | bytes 16000000 | tf_op jit(solution)/shard_map/hidden_back/pallas_call | solution.py:565
  371.4 22.1 %mlp.7 = (bf16[256,2048]{1,0:T(8,128)(2,1)}, bf16[256,2048]{1,0:T(8,128)(2,1)}, bf16[256,2048]{1,0:T(8,128)(2,1)}, bf16[128,2048]{1,0:T(8,128)(2,1)}, bf16[128,2048]{1,0:T(8,128)(2,1)}) custom-call(bf16[256,2048]{1,0:T(8,128)(2,1)} %get-tuple-element.151.refs_0_, bf16[256,2048]{1,0:T(8,128)(2,1)} %collective-permute-done.32.refs_1_, ...), custom_call_target="tpu_custom_call" | custom-call | flops 17716740096 | bytes 26000000 | tf_op jit(solution)/shard_map/mlp/pallas_call | solution.py:649
  401.4 8.7 %hidden_back.3 = (bf16[256,2048]{1,0:T(8,128)(2,1)}, bf16[256,512]{1,0:T(8,128)(2,1)}, bf16[256,512]{1,0:T(8,128)(2,1)}, bf16[256,512]{1,0:T(8,128)(2,1)}, bf16[256,512]{1,0:T(8,128)(2,1)}) custom-call(f32[2,256,2048]{2,1,0:T(8,128)} %cotangent.3, f32[256,2048]{1,0:T(8,128)} %get-tuple-element.156.refs_7_.refs_8_.refs_9_.hidden.refs_4_, ...), custom_call_target="tpu_custom_call" | custom-call | flops 2000000000 | bytes 16000000 | tf_op jit(solution)/shard_map/hidden_back/pallas_call | solution.py:565
  412.4 20.5 %attend_back.2 = (bf16[16,2048]{1,0:T(8,128)(2,1)}, bf16[16,2048]{1,0:T(8,128)(2,1)}, bf16[16,2048]{1,0:T(8,128)(2,1)}, bf16[16,2048]{1,0:T(8,128)(2,1)}) custom-call(s32[1]{0:T(128)} %bitcast.refs_0_.place, bf16[256,512]{1,0:T(8,128)(2,1)} %get-tuple-element.165.part0, bf16[256,512]{1,0:T(8,128)(2,1)} %copy-done.84, bf16[256,512]{1,0:T(8,128)(2,1)} %copy-done.85, ...), custom_call_target="tpu_custom_call" | custom-call | flops 24999999488 | bytes 8000000 | tf_op jit(solution)/shard_map/attend_back/pallas_call | solution.py:434
  444.2 20.7 %attend_back.3 = (bf16[16,2048]{1,0:T(8,128)(2,1)}, bf16[16,2048]{1,0:T(8,128)(2,1)}, bf16[16,2048]{1,0:T(8,128)(2,1)}, bf16[16,2048]{1,0:T(8,128)(2,1)}) custom-call(s32[1]{0:T(128)} %bitcast.refs_0_.place, bf16[256,512]{1,0:T(8,128)(2,1)} %get-tuple-element.180.part0, bf16[256,512]{1,0:T(8,128)(2,1)} %collective-permute-done.53.part1, ...), custom_call_target="tpu_custom_call" | custom-call | flops 24999999488 | bytes 8000000 | tf_op jit(solution)/shard_map/attend_back/pallas_call | solution.py:434
  473.9 16.4 %hyper_back.2 = (bf16[2,2,4,128,512]{4,3,2,1,0:T(8,128)(2,1)}, bf16[2,2,4,128,512]{4,3,2,1,0:T(8,128)(2,1)}, bf16[2,2,4,128,512]{4,3,2,1,0:T(8,128)(2,1)}, bf16[...) custom-call(s32[4]{0:T(128)} %pad_add_fusion.5.refs_0_, ...), custom_call_target="tpu_custom_call" | custom-call | flops 8000000000 | bytes 25000000 | tf_op jit(solution)/shard_map/hyper_back/pallas_call | solution.py:1123
  506.7 14.3 %hyper_back.3 = (bf16[2,2,4,112,512]{4,3,2,1,0:T(8,128)(2,1)}, bf16[2,2,4,112,512]{4,3,2,1,0:T(8,128)(2,1)}, bf16[2,2,4,112,512]{4,3,2,1,0:T(8,128)(2,1)}, bf16[...) custom-call(s32[4]{0:T(128)} %pad_add_fusion.5.refs_0_, ...), custom_call_target="tpu_custom_call" | custom-call | flops 8000000000 | bytes 25000000 | tf_op jit(solution)/shard_map/hyper_back/pallas_call | solution.py:1123
  571.9 15.0 %collective-permute-done.75 = bf16[256,512]{1,0:T(8,128)(2,1)S(1)} collective-permute-done((bf16[256,512]{1,0:T(8,128)(2,1)}, bf16[256,512]{1,0:T(8,128)(2,1)S(1)}, u32[]{:S(2)}, u32[]{:S(2)}) %collective-permute-start.75) | collective-permute-done | bytes 262176 | tf_op jit(solution)/shard_map/ppermute | solution.py:1384
  594.1 7.6 %collect.2.base_ref._after_one = f32[4096,128]{1,0:T(8,128)S(1)} custom-call(s32[2,2048]{1,0:T(2,128)S(1)} %slice.98.refs_0_, s32[2048,1]{1,0:T(8,128)S(1)} %copy-done.6, s32[2048,1]{1,0:T(8,128)S(1)} %copy-done.7, bf16[2048,128]{1,0:T(8,128)(2,1)S(1)} %bitcast.121, bf16[2048,128]{1,0:T(8,128)(2,1)} %bitcast.46.refs_4_), custom_call_target="tpu_custom_call" | custom-call | flops 8589934592 | bytes 2097152 | tf_op jit(solution)/shard_map/collect/pallas_call | solution.py:131
  608.1 9.5 %collective-permute-done.81 = bf16[224,512]{1,0:T(8,128)(2,1)S(1)} collective-permute-done((bf16[224,512]{1,0:T(8,128)(2,1)}, bf16[224,512]{1,0:T(8,128)(2,1)S(1)}, u32[]{:S(2)}, u32[]{:S(2)}) %collective-permute-start.81) | collective-permute-done | bytes 229408 | tf_op jit(solution)/shard_map/ppermute | solution.py:1384
  619.5 14.1 %collective-permute-done.82 = bf16[224,512]{1,0:T(8,128)(2,1)} collective-permute-done((bf16[224,512]{1,0:T(8,128)(2,1)S(1)}, bf16[224,512]{1,0:T(8,128)(2,1)}, u32[]{:S(2)}, u32[]{:S(2)}) %collective-permute-start.82) | collective-permute-done | bytes 229408 | tf_op jit(solution)/shard_map/ppermute | solution.py:1384
  636.4 9.0 %collect.3 = f32[4096,128]{1,0:T(8,128)} custom-call(s32[2,2048]{1,0:T(2,128)S(1)} %slice.91.ids_ref, s32[2048,1]{1,0:T(8,128)S(1)} %copy-done.4, s32[2048,1]{1,0:T(8,128)S(1)} %copy-done.5, bf16[2048,128]{1,0:T(8,128)(2,1)S(1)} %bitcast.122, bf16[2048,128]{1,0:T(8,128)(2,1)} %bitcast.44.right_ref, f32[4096,128]{1,0:T(8,128)S(1)} %copy-done.10), custom_call_target="tpu_custom_call" | custom-call | flops 8589934592 | bytes 2097152 | tf_op jit(solution)/shard_map/collect/pallas_call | solution.py:131
  (475 shorter events, 259.7 us)
Async XLA Ops:
  7.3 145.2 %all-gather.3.cloned.1.call-start = ((), (), s32[]{:S(2)}) async-start(), calls=%async_computation | async-start | bytes 16220160 | tf_op jit(solution)/shard_map/all_gather | solution.py:1482
  9.4 136.8 %collective-permute-start = (bf16[512,2048]{1,0:T(8,128)(2,1)}, bf16[512,2048]{1,0:T(8,128)(2,1)}, u32[]{:S(2)}, u32[]{:S(2)}) collective-permute-start(bf16[512,2048]{1,0:T(8,128)(2,1)} %w0.7), channel_id=1, source_target_pairs={{0,2},{1,3},{2,0},{3,1},{4,6},{5,7},{6,4},{7,5},{8,10},{9,11},{10,... | collective-permute-start | bytes 6291464 | tf_op jit(solution)/shard_map/ppermute | solution.py:64
  12.4 179.2 %collective-permute-start.18 = (bf16[512,2048]{1,0:T(8,128)(2,1)}, bf16[512,2048]{1,0:T(8,128)(2,1)}, u32[]{:S(2)}, u32[]{:S(2)}) collective-permute-start(bf16[512,2048]{1,0:T(8,128)(2,1)} %w0.7), channel_id=1, source_target_pairs={{0,1},{1,0},{2,3},{3,2},{4,5},{5,4},{6,7},{7,6},{8,9},{9,8},{10,11... | collective-permute-start | bytes 6291464 | tf_op jit(solution)/shard_map/ppermute | solution.py:64
  44.3 38.6 %collective-permute-start.6 = (bf16[4,4,256,128]{3,2,1,0:T(8,128)(2,1)}, bf16[4,4,256,128]{3,2,1,0:T(8,128)(2,1)}, u32[]{:S(2)}, u32[]{:S(2)}) collective-permute-start(bf16[4,4,256,128]{3,2,1,0:T(8,128)(2,1)} %bitcast.3._after), channel_id=1, source_target_pairs={{0,4},{4,0},{8,12},{12,8},{16,20},{20,16},{24,28},{28,24},{1,5},{5... | collective-permute-start | bytes 3145736 | tf_op jit(solution)/shard_map/ppermute | solution.py:64
  59.0 51.7 %collective-permute-start.4 = (bf16[256,2048]{1,0:T(8,128)(2,1)}, bf16[256,2048]{1,0:T(8,128)(2,1)}, u32[]{:S(2)}, u32[]{:S(2)}) collective-permute-start(bf16[256,2048]{1,0:T(8,128)(2,1)} %cast_after.2._values), channel_id=1, source_target_pairs={{0,1},{1,0},{2,3},{3,2},{4,5},{5,4},{6,7},{7,6},{8,9},{9,8},{10,11... | collective-permute-start | bytes 3145736 | tf_op jit(solution)/shard_map/ppermute | solution.py:64
  92.2 48.2 %collective-permute-start.5 = (bf16[256,2048]{1,0:T(8,128)(2,1)S(1)}, bf16[256,2048]{1,0:T(8,128)(2,1)}, u32[]{:S(2)}, u32[]{:S(2)}) collective-permute-start(bf16[256,2048]{1,0:T(8,128)(2,1)S(1)} %copy-done.19), channel_id=1, source_target_pairs={{0,1},{1,0},{2,3},{3,2},{4,5},{5,4},{6,7},{7,6},{8,9},{9,8},{10,11... | collective-permute-start | bytes 3145736 | tf_op jit(solution)/shard_map/ppermute | solution.py:64
  110.7 28.9 %collective-permute-start.8 = (bf16[1,4,256,128]{3,2,1,0:T(8,128)(2,1)S(1)}, bf16[1,4,256,128]{3,2,1,0:T(8,128)(2,1)S(1)}, u32[]{:S(2)}, u32[]{:S(2)}) collective-permute-start(bf16[1,4,256,128]{3,2,1,0:T(8,128)(2,1)S(1)} %slice.114), channel_id=1, source_target_pairs={{0,16},{4,20},{8,24},{12,28},{16,0},{20,4},{24,8},{28,12},{1,17},{... | collective-permute-start | bytes 786440 | tf_op jit(solution)/shard_map/ppermute | solution.py:64
  170.8 43.5 %collective-permute-start.19 = (bf16[512,2048]{1,0:T(8,128)(2,1)}, bf16[512,2048]{1,0:T(8,128)(2,1)S(1)}, u32[]{:S(2)}, u32[]{:S(2)}) collective-permute-start(bf16[512,2048]{1,0:T(8,128)(2,1)} %collective-permute-done.refs_1_.w2), channel_id=1, source_target_pairs={{0,1},{1,0},{2,3},{3,2},{4,5},{5,4},{6,7},{7,6},{8,9},{9,8},{10,11... | collective-permute-start | bytes 6291464 | tf_op jit(solution)/shard_map/ppermute | solution.py:64
  191.6 46.4 %collective-permute-start.20 = (bf16[256,2048]{1,0:T(8,128)(2,1)}, bf16[256,2048]{1,0:T(8,128)(2,1)S(1)}, u32[]{:S(2)}, u32[]{:S(2)}) collective-permute-start(bf16[256,2048]{1,0:T(8,128)(2,1)} %tie.11), channel_id=1, source_target_pairs={{0,2},{1,3},{2,0},{3,1},{4,6},{5,7},{6,4},{7,5},{8,10},{9,11},{10,... | collective-permute-start | bytes 3145736 | tf_op jit(solution)/shard_map/ppermute | solution.py:64
  276.3 34.5 %collective-permute-start.31 = (bf16[256,2048]{1,0:T(8,128)(2,1)}, bf16[256,2048]{1,0:T(8,128)(2,1)S(1)}, u32[]{:S(2)}, u32[]{:S(2)}) collective-permute-start(bf16[256,2048]{1,0:T(8,128)(2,1)} %tie.12), channel_id=1, source_target_pairs={{0,2},{1,3},{2,0},{3,1},{4,6},{5,7},{6,4},{7,5},{8,10},{9,11},{10,... | collective-permute-start | bytes 3145736 | tf_op jit(solution)/shard_map/ppermute | solution.py:64
  324.5 32.4 %collective-permute-start.33 = (bf16[128,2048]{1,0:T(8,128)(2,1)S(1)}, bf16[128,2048]{1,0:T(8,128)(2,1)}, u32[]{:S(2)}, u32[]{:S(2)}) collective-permute-start(bf16[128,2048]{1,0:T(8,128)(2,1)S(1)} %copy-done.79), channel_id=1, source_target_pairs={{0,1},{1,0},{2,3},{3,2},{4,5},{5,4},{6,7},{7,6},{8,9},{9,8},{10,11... | collective-permute-start | bytes 1572872 | tf_op jit(solution)/shard_map/ppermute | solution.py:64
  324.6 32.6 %collective-permute-start.34 = (bf16[128,2048]{1,0:T(8,128)(2,1)S(1)}, bf16[128,2048]{1,0:T(8,128)(2,1)S(1)}, u32[]{:S(2)}, u32[]{:S(2)}) collective-permute-start(bf16[128,2048]{1,0:T(8,128)(2,1)S(1)} %copy-done.78), channel_id=1, source_target_pairs={{0,1},{1,0},{2,3},{3,2},{4,5},{5,4},{6,7},{7,6},{8,9},{9,8},{10,11... | collective-permute-start | bytes 1572872 | tf_op jit(solution)/shard_map/ppermute | solution.py:64
  325.0 33.2 %collective-permute-start.35 = (bf16[256,2048]{1,0:T(8,128)(2,1)S(1)}, bf16[256,2048]{1,0:T(8,128)(2,1)S(1)}, u32[]{:S(2)}, u32[]{:S(2)}) collective-permute-start(bf16[256,2048]{1,0:T(8,128)(2,1)S(1)} %copy-done.30), channel_id=1, source_target_pairs={{0,2},{1,3},{2,0},{3,1},{4,6},{5,7},{6,4},{7,5},{8,10},{9,11},{10,... | collective-permute-start | bytes 3145736 | tf_op jit(solution)/shard_map/ppermute | solution.py:64
  326.9 44.5 %collective-permute-start.32 = (bf16[256,2048]{1,0:T(8,128)(2,1)}, bf16[256,2048]{1,0:T(8,128)(2,1)}, u32[]{:S(2)}, u32[]{:S(2)}) collective-permute-start(bf16[256,2048]{1,0:T(8,128)(2,1)} %get-tuple-element.151.refs_0_), channel_id=1, source_target_pairs={{0,1},{1,0},{2,3},{3,2},{4,5},{5,4},{6,7},{7,6},{8,9},{9,8},{10,11... | collective-permute-start | bytes 3145736 | tf_op jit(solution)/shard_map/ppermute | solution.py:64
  358.1 52.1 %collective-permute-start.22 = (bf16[256,2048]{1,0:T(8,128)(2,1)}, bf16[256,2048]{1,0:T(8,128)(2,1)S(1)}, u32[]{:S(2)}, u32[]{:S(2)}) collective-permute-start(bf16[256,2048]{1,0:T(8,128)(2,1)} %get-tuple-element.141), channel_id=1, source_target_pairs={{0,1},{1,0},{2,3},{3,2},{4,5},{5,4},{6,7},{7,6},{8,9},{9,8},{10,11... | collective-permute-start | bytes 3145736 | tf_op jit(solution)/shard_map/ppermute | solution.py:64
  358.2 35.3 %collective-permute-start.27 = (bf16[256,2048]{1,0:T(8,128)(2,1)}, bf16[256,2048]{1,0:T(8,128)(2,1)S(1)}, u32[]{:S(2)}, u32[]{:S(2)}) collective-permute-start(bf16[256,2048]{1,0:T(8,128)(2,1)} %get-tuple-element.146), channel_id=1, source_target_pairs={{0,1},{1,0},{2,3},{3,2},{4,5},{5,4},{6,7},{7,6},{8,9},{9,8},{10,11... | collective-permute-start | bytes 3145736 | tf_op jit(solution)/shard_map/ppermute | solution.py:64
  370.8 29.6 %collective-permute-start.48 = (bf16[256,2048]{1,0:T(8,128)(2,1)}, bf16[256,2048]{1,0:T(8,128)(2,1)}, u32[]{:S(2)}, u32[]{:S(2)}) collective-permute-start(bf16[256,2048]{1,0:T(8,128)(2,1)} %add_convert_fusion.1.refs_8_), channel_id=1, source_target_pairs={{0,2},{1,3},{2,0},{3,1},{4,6},{5,7},{6,4},{7,5},{8,10},{9,11},{10,... | collective-permute-start | bytes 3145736 | tf_op jit(solution)/shard_map/ppermute | solution.py:64
  400.3 32.9 %collective-permute-start.40 = (bf16[256,2048]{1,0:T(8,128)(2,1)S(1)}, bf16[256,2048]{1,0:T(8,128)(2,1)S(1)}, u32[]{:S(2)}, u32[]{:S(2)}) collective-permute-start(bf16[256,2048]{1,0:T(8,128)(2,1)S(1)} %copy-done.15), channel_id=1, source_target_pairs={{0,2},{1,3},{2,0},{3,1},{4,6},{5,7},{6,4},{7,5},{8,10},{9,11},{10,... | collective-permute-start | bytes 3145736 | tf_op jit(solution)/shard_map/ppermute | solution.py:64
  410.8 28.2 %collective-permute-start.54 = (bf16[256,512]{1,0:T(8,128)(2,1)}, bf16[256,512]{1,0:T(8,128)(2,1)}, u32[]{:S(2)}, u32[]{:S(2)}) collective-permute-start(bf16[256,512]{1,0:T(8,128)(2,1)} %get-tuple-element.182), channel_id=1, source_target_pairs={{0,2},{1,3},{2,0},{3,1},{4,6},{5,7},{6,4},{7,5},{8,10},{9,11},{10,... | collective-permute-start | bytes 786440 | tf_op jit(solution)/shard_map/ppermute | solution.py:64
  411.7 31.8 %collective-permute-start.55 = (bf16[256,512]{1,0:T(8,128)(2,1)}, bf16[256,512]{1,0:T(8,128)(2,1)S(1)}, u32[]{:S(2)}, u32[]{:S(2)}) collective-permute-start(bf16[256,512]{1,0:T(8,128)(2,1)} %get-tuple-element.183), channel_id=1, source_target_pairs={{0,3},{1,2},{2,1},{3,0},{4,7},{5,6},{6,5},{7,4},{8,11},{9,10},{10,... | collective-permute-start | bytes 786440 | tf_op jit(solution)/shard_map/ppermute | solution.py:64
  433.2 39.7 %collective-permute-start.49 = (bf16[256,2048]{1,0:T(8,128)(2,1)}, bf16[256,2048]{1,0:T(8,128)(2,1)S(1)}, u32[]{:S(2)}, u32[]{:S(2)}) collective-permute-start(bf16[256,2048]{1,0:T(8,128)(2,1)} %tie.14), channel_id=1, source_target_pairs={{0,2},{1,3},{2,0},{3,1},{4,6},{5,7},{6,4},{7,5},{8,10},{9,11},{10,... | collective-permute-start | bytes 3145736 | tf_op jit(solution)/shard_map/ppermute | solution.py:64
  434.7 31.1 %collective-permute-start.50 = (bf16[16,2048]{1,0:T(8,128)(2,1)S(1)}, bf16[16,2048]{1,0:T(8,128)(2,1)S(1)}, u32[]{:S(2)}, u32[]{:S(2)}) collective-permute-start(bf16[16,2048]{1,0:T(8,128)(2,1)S(1)} %copy-done.92), channel_id=1, source_target_pairs={{0,1},{1,0},{2,3},{3,2},{4,5},{5,4},{6,7},{7,6},{8,9},{9,8},{10,11... | collective-permute-start | bytes 196616 | tf_op jit(solution)/shard_map/ppermute | solution.py:64
  434.7 33.6 %collective-permute-start.51 = (bf16[16,2048]{1,0:T(8,128)(2,1)S(1)}, bf16[16,2048]{1,0:T(8,128)(2,1)S(1)}, u32[]{:S(2)}, u32[]{:S(2)}) collective-permute-start(bf16[16,2048]{1,0:T(8,128)(2,1)S(1)} %copy-done.91), channel_id=1, source_target_pairs={{0,2},{1,3},{2,0},{3,1},{4,6},{5,7},{6,4},{7,5},{8,10},{9,11},{10,... | collective-permute-start | bytes 196616 | tf_op jit(solution)/shard_map/ppermute | solution.py:64
  438.9 30.0 %collective-permute-start.52 = (bf16[16,2048]{1,0:T(8,128)(2,1)S(1)}, bf16[16,2048]{1,0:T(8,128)(2,1)S(1)}, u32[]{:S(2)}, u32[]{:S(2)}) collective-permute-start(bf16[16,2048]{1,0:T(8,128)(2,1)S(1)} %copy-done.90), channel_id=1, source_target_pairs={{0,3},{1,2},{2,1},{3,0},{4,7},{5,6},{6,5},{7,4},{8,11},{9,10},{10,... | collective-permute-start | bytes 196616 | tf_op jit(solution)/shard_map/ppermute | solution.py:64
  (157 other events, 1488.5 us)
Sparse Core Ops, SparseCore 0:
  11.0 141.3 all-gather.2
